TPU v7x, 32 devices: a whole 2x2x4 slice. The times are simulated.
32 devices in a mesh: copies: 2 (over y), shard: 4 (over z), dom: 4 (over x, core).
Axes of the slice: x: 2, y: 2, z: 4, core: 2. Of those that a mesh axis runs over, the one named last changes fastest.
Arguments:
- features: float32 [16384, 256], P(('copies', 'shard', 'dom')), parts along dimension 0, may hold values from -6 to 6
- weight: float32 [256, 256], replicated, may hold values from -0.375 to 0.375
- cotangent: float32 [16384, 256], P(('copies', 'shard', 'dom')), parts along dimension 0, may hold values from -6 to 6
- block_values: bfloat16 [128, 16, 128, 128], P(('copies', 'shard', 'dom')), parts along dimension 0
- block_list: int32 [128, 16], P(('copies', 'shard', 'dom')), parts along dimension 0, may hold values from 0 to 19, as said below
- send_inner: int32 [32, 4, 2], P(('copies', 'shard', 'dom')), parts along dimension 0, may hold values from -1 to 3, as said below
- send_outer: int32 [32, 4, 2], P(('copies', 'shard', 'dom')), parts along dimension 0, may hold values from -1 to 3, as said below
Outputs:
- activations: float32 [16384, 256], P(('copies', 'shard', 'dom')), parts along dimension 0
- grad_features: float32 [16384, 256], P(('copies', 'shard', 'dom')), parts along dimension 0
- grad_weight: float32 [512, 256], P('copies'), parts along dimension 0
There are 2 independent parts, one for each index of `copies`. A program takes and returns all parts, laid end to end along the dimension named above; an argument that names none is the same for every part. Nothing has to cross between parts.
Inputs may be any that keep to these rules, and one draw needn't show every extreme that they name: `block_list`: every nonempty slot of send_inner and send_outer is named exactly once on the receiving device, and no empty slot is named. Values below 4 name local row blocks. `send_inner`: -1 marks an empty slot; nonempty slots come first; a device sends nothing to itself; in every partition one device receives 2 row blocks from each other device of it. `send_outer`: -1 marks an empty slot; nonempty slots come first; nothing goes to the own partition; for every shard index one partition receives 2 row blocks from each other partition.
All inputs are finite; a program needn't handle non-finite values.
Results may differ from a plain program's by a relative error of at most 0.0033.
Values may be sent and summed in bfloat16 or wider, within the bound.
No kernel may reach another device: no remote copies, remote signals or barrier semaphores. Data moves between devices by JAX's collectives and lax.ppermute only.
A program may use at most 128 MiB of HBM per device.

v0:
```python
import jax
import jax.numpy as jnp
from jax import lax
from jax.sharding import PartitionSpec as P


def pack_rows(blocks, targets):
    picked = blocks[jnp.maximum(targets, 0)]
    return jnp.where((targets >= 0)[:, :, None, None], picked, jnp.zeros_like(picked))


def on_device(features, weight, cotangent, block_values, block_list, send_inner, send_outer):
    highest = lax.Precision.HIGHEST
    node_count, feat_width = features.shape
    row_blocks, fanout, block_side, _ = block_values.shape
    shard_count = lax.axis_size("shard")
    dom_count = lax.axis_size("dom")
    inner_cap = send_inner.shape[2]
    outer_cap = send_outer.shape[2]
    inner_slots = shard_count * inner_cap
    outer_slots = dom_count * outer_cap
    remote_slots = inner_slots + outer_slots
    inner_targets = send_inner[0]
    outer_targets = send_outer[0]
    projected = jnp.dot(features, weight, precision=highest, preferred_element_type=jnp.float32)
    half_blocks = projected.astype(jnp.bfloat16).reshape(row_blocks, block_side, feat_width)
    inner_blocks = lax.all_to_all(
        pack_rows(half_blocks, inner_targets), "shard", split_axis=0, concat_axis=0, tiled=True
    )
    outer_blocks = lax.all_to_all(
        pack_rows(half_blocks, outer_targets), "dom", split_axis=0, concat_axis=0, tiled=True
    )
    sources = jnp.concatenate(
        [
            half_blocks,
            inner_blocks.reshape(inner_slots, block_side, feat_width),
            outer_blocks.reshape(outer_slots, block_side, feat_width),
        ],
        axis=0,
    )
    picked = sources[block_list]
    summed = jnp.einsum("rkab,rkbf->raf", block_values, picked, preferred_element_type=jnp.float32)
    squares = jnp.sum(jnp.square(block_values.astype(jnp.float32)), axis=(1, 3))
    row_scale = jnp.sqrt(1.0 + squares).reshape(node_count, 1)
    mixed_rows = (projected + summed.reshape(node_count, feat_width)) / row_scale
    logistic = jax.nn.sigmoid(mixed_rows)
    activations = mixed_rows * logistic
    grad_mixed = cotangent * logistic * (1.0 + mixed_rows * (1.0 - logistic))
    scaled = grad_mixed / row_scale
    scaled_half = scaled.astype(jnp.bfloat16).reshape(row_blocks, block_side, feat_width)
    contributions = jnp.einsum(
        "rkab,raf->rkbf", block_values, scaled_half, preferred_element_type=jnp.float32
    )
    flat_list = block_list.reshape(-1)
    flat_terms = contributions.reshape(row_blocks * fanout, block_side, feat_width)
    targets = jnp.concatenate([inner_targets.reshape(-1), outer_targets.reshape(-1)])
    owner_index = jnp.where(targets >= 0, targets, row_blocks)
    per_source = (
        jnp.zeros((row_blocks + remote_slots, block_side, feat_width), jnp.float32)
        .at[flat_list]
        .add(flat_terms)
    )
    local_grad = per_source[:row_blocks]
    remote_terms = per_source[row_blocks:]
    inner_back = lax.all_to_all(
        remote_terms[:inner_slots]
        .reshape(shard_count, inner_cap, block_side, feat_width)
        .astype(jnp.bfloat16),
        "shard",
        split_axis=0,
        concat_axis=0,
        tiled=True,
    ).astype(jnp.float32)
    outer_back = lax.all_to_all(
        remote_terms[inner_slots:]
        .reshape(dom_count, outer_cap, block_side, feat_width)
        .astype(jnp.bfloat16),
        "dom",
        split_axis=0,
        concat_axis=0,
        tiled=True,
    ).astype(jnp.float32)
    returned = jnp.concatenate(
        [
            inner_back.reshape(inner_slots, block_side, feat_width),
            outer_back.reshape(outer_slots, block_side, feat_width),
        ],
        axis=0,
    )
    added = (
        jnp.zeros((row_blocks, block_side, feat_width), jnp.float32)
        .at[owner_index]
        .add(returned, mode="drop")
    )
    grad_projected = scaled + (local_grad + added).reshape(node_count, feat_width)
    weight_term = lax.dot_general(
        features,
        grad_projected,
        (((0,), (0,)), ((), ())),
        precision=highest,
        preferred_element_type=jnp.float32,
    )
    grad_weight = lax.psum(weight_term, ("shard", "dom"))
    grad_features = lax.dot_general(
        grad_projected,
        weight,
        (((1,), (1,)), ((), ())),
        precision=highest,
        preferred_element_type=jnp.float32,
    )
    return (activations, grad_features, grad_weight)


def solution(mesh):
    return jax.shard_map(
        on_device,
        mesh=mesh,
        in_specs=(
            P(("copies", "shard", "dom"), None),
            P(),
            P(("copies", "shard", "dom"), None),
            P(("copies", "shard", "dom"), None, None, None),
            P(("copies", "shard", "dom"), None),
            P(("copies", "shard", "dom"), None, None),
            P(("copies", "shard", "dom"), None, None),
        ),
        out_specs=(
            P(("copies", "shard", "dom"), None),
            P(("copies", "shard", "dom"), None),
            P("copies", None),
        ),
        check_vma=False,
    )
```

profile of v0, /device:TPU:0, one launch (start us, length us, event | category | flops | bytes accessed | tf_op | source)
XLA Modules:
  0.0 216.9 jit_solution(593038491711419575)
XLA Ops:
  8.9 1.5 fusion.6
  12.0 4.3 %all-to-all-start.1 = ((bf16[4,2,128,256]{3,2,1,0:T(8,128)(2,1)}), bf16[4,2,128,256]{3,2,1,0:T(8,128)(2,1)}, u32[]{:S(2)}, u32[]{:S(2)}) async-start(bf16[4,2,128,256]{3,2,1,0:T(8,128)(2,1)} %broadcast_select_fusion), calls=%async_computation.1 | async-start | bytes 1048576 | tf_op jit(solution)/shard_map/all_to_all | solution.py:30
  16.5 1.4 gather_fusion
  18.2 1.9 broadcast_select_fusion.1
  20.1 5.6 %all-to-all-done.1 = bf16[4,2,128,256]{3,2,1,0:T(8,128)(2,1)} async-done(((bf16[4,2,128,256]{3,2,1,0:T(8,128)(2,1)}), bf16[4,2,128,256]{3,2,1,0:T(8,128)(2,1)}, u32[]{:S(2)}, u32[]{:S(2)}) %all-to-all-start.1) | async-done | bytes 524320 | tf_op jit(solution)/shard_map/all_to_all | solution.py:30
  25.8 5.7 %all-to-all-start = ((bf16[4,2,128,256]{3,2,1,0:T(8,128)(2,1)}), bf16[4,2,128,256]{3,2,1,0:T(8,128)(2,1)}, u32[]{:S(2)}, u32[]{:S(2)}) async-start(bf16[4,2,128,256]{3,2,1,0:T(8,128)(2,1)} %broadcast_select_fusion.1), calls=%async_computation | async-start | bytes 1048576 | tf_op jit(solution)/shard_map/all_to_all | solution.py:27
  32.0 13.9 %all-to-all-done = bf16[4,2,128,256]{3,2,1,0:T(8,128)(2,1)} async-done(((bf16[4,2,128,256]{3,2,1,0:T(8,128)(2,1)}), bf16[4,2,128,256]{3,2,1,0:T(8,128)(2,1)}, u32[]{:S(2)}, u32[]{:S(2)}) %all-to-all-start) | async-done | bytes 524320 | tf_op jit(solution)/shard_map/all_to_all | solution.py:27
  45.9 2.4 %pad_maximum_fusion = bf16[20,128,256]{2,1,0:T(8,128)(2,1)} fusion(bf16[8,128,256]{2,1,0:T(8,128)(2,1)} %bitcast.6, bf16[8,128,256]{2,1,0:T(8,128)(2,1)} %bitcast.3, bf16[4,128,256]{2,1,0:T(8,128)(2,1)S(1)} %bitcast.58), kind=kLoop, calls=%fused_computation.6 | loop fusion | flops 1310720 | bytes 2621440 | tf_op jit(solution)/shard_map/concatenate | solution.py:33
  48.3 4.1 %gather_fusion.2 = bf16[64,128,256]{2,1,0:T(8,128)(2,1)} fusion(bf16[20,128,256]{2,1,0:T(8,128)(2,1)} %pad_maximum_fusion, s32[1024]{0:T(1024)S(1)} %pad_clamp_fusion), kind=kCustom, calls=%fused_computation.2 | custom fusion | bytes 8388864 | tf_op jit(solution)/shard_map/gather | solution.py:41
  52.4 3.0 %fusion.9 = f32[4,256,128,1]{1,2,3,0:T(8,128)S(1)} fusion(bf16[4,16,128,128]{3,2,1,0:T(8,128)(2,1)S(1)} %copy-done.1, bf16[4,16,128,256]{3,2,1,0:T(8,128)(2,1)} %bitcast.55), kind=kOutput, calls=%fused_computation.36 | convolution fusion | flops 536870912 | bytes 6815744 | tf_op jit(solution)/shard_map/rkab,rkbf->raf/dot_general | solution.py:42
  55.4 1.3 fusion.4
  56.7 4.5 %fusion.7 = f32[4,256,16,128]{3,1,2,0:T(8,128)} fusion(bf16[4,128,256,1]{2,1,3,0:T(8,128)(2,1)S(1)} %bitcast.64, bf16[4,16,128,128]{3,2,1,0:T(8,128)(2,1)S(1)} %copy-done.1), kind=kOutput, calls=%fused_computation.34 | convolution fusion | flops 536870912 | bytes 10747904 | tf_op jit(solution)/shard_map/rkab,raf->rkbf/dot_general | solution.py:51
  61.2 9.0 %copy.24 = f32[64,128,256]{2,1,0:T(8,128)} copy(f32[64,128,256]{1,2,0:T(8,128)} %bitcast.54) | data formatting | bytes 16777216 | tf_op jit(solution)/shard_map/reshape | solution.py:55
  70.4 12.3 %scatter_fusion = f32[20,128,256]{2,1,0:T(8,128)S(1)} fusion(f32[20,128,256]{2,1,0:T(8,128)S(1)} %broadcast_in_dim.33, s32[64]{0:T(128)S(1)} %fusion.2, f32[64,128,256]{2,1,0:T(8,128)} %copy.24), kind=kCustom, calls=%fused_computation.3 | custom fusion | flops 2097152 | bytes 25166080 | tf_op jit(solution)/shard_map/scatter-add | solution.py:61
  83.9 11.9 %all_to_all.20 = bf16[4,2,128,256]{3,2,1,0:T(8,128)(2,1)} all-to-all(bf16[4,2,128,256]{3,2,1,0:T(8,128)(2,1)S(1)} %bitcast.63), channel_id=1, replica_groups=mesh['copies'=2,'shard'=4,'dom'=4] {'dom'}, dimensions={0} | all-to-all | bytes 1048576 | tf_op jit(solution)/shard_map/all_to_all | solution.py:74
  95.8 4.1 %all-to-all-start.2 = ((bf16[4,2,128,256]{3,2,1,0:T(8,128)(2,1)}), bf16[4,2,128,256]{3,2,1,0:T(8,128)(2,1)}, u32[]{:S(2)}, u32[]{:S(2)}) async-start(bf16[4,2,128,256]{3,2,1,0:T(8,128)(2,1)} %bitcast.62), calls=%async_computation.2 | async-start | bytes 1048576 | tf_op jit(solution)/shard_map/all_to_all | solution.py:65
  101.3 13.1 %all-to-all-done.2 = bf16[4,2,128,256]{3,2,1,0:T(8,128)(2,1)} async-done(((bf16[4,2,128,256]{3,2,1,0:T(8,128)(2,1)}), bf16[4,2,128,256]{3,2,1,0:T(8,128)(2,1)}, u32[]{:S(2)}, u32[]{:S(2)}) %all-to-all-start.2) | async-done | bytes 524320 | tf_op jit(solution)/shard_map/all_to_all | solution.py:65
  114.4 1.3 maximum_convert_fusion
  115.8 2.2 %scatter_fusion.1 = f32[4,128,256]{2,1,0:T(8,128)S(1)} fusion(f32[4,128,256]{2,1,0:T(8,128)S(1)} %copy-done.2, s32[16]{0:T(128)S(1)} %fusion.3, f32[16,128,256]{2,1,0:T(8,128)S(1)} %maximum_convert_fusion), kind=kCustom, calls=%fused_computation.4 | custom fusion | flops 524288 | bytes 6291520 | tf_op jit(solution)/shard_map/scatter-add | solution.py:93
  118.0 1.1 bitcast_add_fusion.1
  119.1 1.7 convolution_bitcast_fusion
  120.8 1.4 fusion.8
  122.2 86.0 %all-reduce.2.cloned.1.call-done = f32[256,256]{0,1:T(8,128)} async-done(((f32[256,256]{0,1:T(8,128)}), f32[256,256]{0,1:T(8,128)}) %all-reduce.2.cloned.1.call-update) | async-done | bytes 262160 | tf_op jit(solution)/shard_map/psum | solution.py:103
  208.2 1.8 copy.27
  (48 shorter events, 6.9 us)
Async XLA Ops:
  7.2 1.7 copy-start
  8.9 7.4 %copy-start.6 = (s32[1,4,2]{1,2,0:T(2,128)S(1)}, s32[1,4,2]{1,2,0:T(2,128)}, u32[]{:S(2)}) copy-start(s32[1,4,2]{1,2,0:T(2,128)} %param.12) | copy-start | bytes 100
  10.5 7.5 %copy-start.5 = (s32[4,16]{1,0:T(4,128)S(1)}, s32[4,16]{1,0:T(4,128)}, u32[]{:S(2)}) copy-start(s32[4,16]{1,0:T(4,128)} %param.11) | copy-start | bytes 772
  12.0 19.5 %copy-start.1 = (bf16[4,16,128,128]{3,2,1,0:T(8,128)(2,1)S(1)}, bf16[4,16,128,128]{3,2,1,0:T(8,128)(2,1)}, u32[]{:S(2)}) copy-start(bf16[4,16,128,128]{3,2,1,0:T(8,128)(2,1)} %param.10) | copy-start | bytes 6291460
  12.0 13.8 %all-to-all-start.1 = ((bf16[4,2,128,256]{3,2,1,0:T(8,128)(2,1)}), bf16[4,2,128,256]{3,2,1,0:T(8,128)(2,1)}, u32[]{:S(2)}, u32[]{:S(2)}) async-start(bf16[4,2,128,256]{3,2,1,0:T(8,128)(2,1)} %broadcast_select_fusion), calls=%async_computation.1 | async-start | bytes 1048576 | tf_op jit(solution)/shard_map/all_to_all | solution.py:30
  25.8 20.1 %all-to-all-start = ((bf16[4,2,128,256]{3,2,1,0:T(8,128)(2,1)}), bf16[4,2,128,256]{3,2,1,0:T(8,128)(2,1)}, u32[]{:S(2)}, u32[]{:S(2)}) async-start(bf16[4,2,128,256]{3,2,1,0:T(8,128)(2,1)} %broadcast_select_fusion.1), calls=%async_computation | async-start | bytes 1048576 | tf_op jit(solution)/shard_map/all_to_all | solution.py:27
  52.4 3.0 %copy-start.4 = (f32[512,256]{1,0:T(8,128)S(1)}, f32[512,256]{1,0:T(8,128)}, u32[]{:S(2)}) copy-start(f32[512,256]{1,0:T(8,128)} %param.9) | copy-start | bytes 1572868
  83.0 17.1 %copy-start.7 = (s32[1,4,2]{1,2,0:T(2,128)S(1)}, s32[1,4,2]{1,2,0:T(2,128)}, u32[]{:S(2)}) copy-start(s32[1,4,2]{1,2,0:T(2,128)} %param.13) | copy-start | bytes 100
  95.8 18.6 %all-to-all-start.2 = ((bf16[4,2,128,256]{3,2,1,0:T(8,128)(2,1)}), bf16[4,2,128,256]{3,2,1,0:T(8,128)(2,1)}, u32[]{:S(2)}, u32[]{:S(2)}) async-start(bf16[4,2,128,256]{3,2,1,0:T(8,128)(2,1)} %bitcast.62), calls=%async_computation.2 | async-start | bytes 1048576 | tf_op jit(solution)/shard_map/all_to_all | solution.py:65
  99.9 108.3 %all-reduce.2.cloned.1.call-start = ((), (), s32[]{:S(2)}) async-start(), calls=%async_computation.4 | async-start | bytes 524288 | tf_op jit(solution)/shard_map/psum | solution.py:103
  101.3 14.5 %copy-start.2 = (f32[4,128,256]{2,1,0:T(8,128)S(1)}, f32[4,128,256]{2,1,0:T(8,128)}, u32[]{:S(2)}) copy-start(f32[4,128,256]{2,1,0:T(8,128)} %slice.23) | copy-start | bytes 1572868
  117.9 2.9 %copy-start.3 = (f32[256,256]{1,0:T(8,128)S(1)}, f32[256,256]{1,0:T(8,128)}, u32[]{:S(2)}) copy-start(f32[256,256]{1,0:T(8,128)} %param.8) | copy-start | bytes 786436
Sparse Core Ops, SparseCore 0:
  120.9 87.2 all-reduce.1
where the time goes:
time: 218 us; the launch traced here: 217 us
  waiting for transfers between devices  119 us (55%)
  other arithmetic  25.8 us (12%)
  local copies, waits for them, and re-layouts  19.9 us (9%)
  starting transfers between devices  14.2 us (7%)
  between operations  14.2 us (7%)
  matrix products  12.2 us (6%)
  blocking collectives  11.9 us (5%)
    psum x1, waiting for transfers between devices, on_device(): grad_weight = lax.psum(weight_term, ('shard', 'dom'))  86 us
    all_to_all x1, waiting for transfers between devices, on_device(): lax.all_to_all(pack_rows(half_blocks, inner_targets), 'shard', split_axis...  13.9 us
    all_to_all x1, waiting for transfers between devices, on_device(): lax.all_to_all(remote_terms[:inner_slots].reshape(shard_count, inner_cap,...  13.1 us
    scatter-add x1, other arithmetic, on_device(): per_source = jnp.zeros((row_blocks + remote_slots, block_side, feat_width...  12.3 us
    all_to_all x1, blocking collectives, on_device(): lax.all_to_all(remote_terms[inner_slots:].reshape(dom_count, outer_cap, b...  11.9 us
    reshape x1, local copies, waits for them, and re-layouts, on_device(): contributions.reshape(row_blocks * fanout, block_side, feat_width)  8.97 us
    all_to_all x1, starting transfers between devices, on_device(): lax.all_to_all(pack_rows(half_blocks, inner_targets), 'shard', split_axis...  5.71 us
    all_to_all x1, waiting for transfers between devices, on_device(): lax.all_to_all(pack_rows(half_blocks, outer_targets), 'dom', split_axis=0...  5.65 us
  transfers between devices with their start and end apart: 4, of which 4 were waited for; matrix products, arithmetic and copies ran while one was open for 3% of the time, Pallas kernels for 0%

commit v1 on v0

v1 whole, which is shorter than its diff:
```python
import functools
import jax
import jax.numpy as jnp
from jax import lax
from jax.experimental import pallas as pl
from jax.experimental.pallas import tpu as pltpu
from jax.sharding import PartitionSpec as P

F32 = jnp.float32
BF16 = jnp.bfloat16
VMEM = pl.BlockSpec(memory_space=pltpu.VMEM)
SMEM = pl.BlockSpec(memory_space=pltpu.SMEM)
PARAMS = pltpu.CompilerParams(vmem_limit_bytes=48 * 1024 * 1024)


def partner(i, k, n):
    if n & (n - 1) == 0:
        return i ^ k
    return (i + k) % n


def back_partner(i, k, n):
    if n & (n - 1) == 0:
        return i ^ k
    return (i + n - k) % n


def exchange_order(n):
    return sorted(range(1, n), key=lambda k: -k)


def send(x, axis, k, n):
    return lax.ppermute(x, axis, [(i, partner(i, k, n)) for i in range(n)])


def send_back(x, axis, k, n):
    return lax.ppermute(x, axis, [(i, back_partner(i, k, n)) for i in range(n)])


def split(x):
    hi = x.astype(BF16)
    return hi, (x - hi.astype(F32)).astype(BF16)


def mm(a, b, dims=((1,), (0,))):
    return lax.dot_general(a, b, (dims, ((), ())), preferred_element_type=F32)


def mm3(a, b, dims=((1,), (0,))):
    ah, al = a
    bh, bl = b
    return mm(ah, bh, dims) + (mm(ah, bl, dims) + mm(al, bh, dims))


def call(kernel, out_shape, flops, nbytes, in_specs, out_specs, scratch=()):
    return pl.pallas_call(
        kernel,
        out_shape=out_shape,
        in_specs=in_specs,
        out_specs=out_specs,
        scratch_shapes=list(scratch),
        compiler_params=PARAMS,
        cost_estimate=pl.CostEstimate(flops=flops, bytes_accessed=nbytes, transcendentals=0),
    )


def pack_kernel(axis, n, side, targets_ref, features_ref, *out_refs):
    me = lax.axis_index(axis)
    cap = targets_ref.shape[2]
    for out_ref, k in zip(out_refs, exchange_order(n)):
        peer = partner(me, k, n)
        for j in range(cap):
            target = targets_ref[0, peer, j]
            row = pl.multiple_of(jnp.maximum(target, 0) * side, side)
            rows = features_ref[pl.ds(row, side), :]
            out_ref[j * side : (j + 1) * side, :] = jnp.where(target >= 0, rows, 0.0).astype(BF16)


def slot_codes(row_blocks, ns, nd, inner_cap, outer_cap):
    s = lax.axis_index("shard")
    p = lax.axis_index("dom")
    codes = []
    for k in exchange_order(ns):
        for j in range(inner_cap):
            codes.append(row_blocks + back_partner(s, k, ns) * inner_cap + j)
    for k in exchange_order(nd):
        for j in range(outer_cap):
            codes.append(row_blocks + ns * inner_cap + back_partner(p, k, nd) * outer_cap + j)
    return codes


def local_kernel(
    dims, list_ref, features_ref, weight_ref, values_ref,
    base_ref, local_ref, scale_ref, picked_ref, turned_ref, place_ref,
    sources_ref, inverse_ref,
):
    row_blocks, fanout, side, width, ns, nd, inner_cap, outer_cap = dims
    codes = row_blocks + ns * inner_cap + nd * outer_cap
    for c in range(codes):
        inverse_ref[c] = 0
    for n in range(row_blocks * fanout):
        inverse_ref[list_ref[n // fanout, n % fanout]] = n
    for i, code in enumerate(slot_codes(row_blocks, ns, nd, inner_cap, outer_cap)):
        n = inverse_ref[code]
        r = n // fanout
        place_ref[i] = r
        block = values_ref[r, n % fanout]
        picked_ref[i] = block
        turned_ref[i] = block.T
    fh, fl = split(features_ref[...])
    projected = mm3((fh, fl), split(weight_ref[...]))
    sources_ref[: row_blocks * side, :width] = projected.astype(BF16)
    sources_ref[: row_blocks * side, width : 2 * width] = fh
    sources_ref[: row_blocks * side, 2 * width :] = fl
    sources_ref[row_blocks * side :, :] = jnp.zeros((side, 3 * width), BF16)
    for r in range(row_blocks):
        rows = slice(r * side, (r + 1) * side)
        squares = jnp.zeros((side, side), F32)
        for k in range(fanout):
            block = values_ref[r, k].astype(F32)
            squares = squares + block * block
        scale = lax.rsqrt(1.0 + jnp.sum(squares, axis=1, keepdims=True))
        scale_ref[rows, :] = jnp.broadcast_to(scale, (side, width))
        total = jnp.zeros((side, 3 * width), F32)
        for k in range(0, fanout, 2):
            blocks = jnp.concatenate([values_ref[r, k], values_ref[r, k + 1]], axis=1)
            picks = []
            for kk in (k, k + 1):
                at = pl.multiple_of(jnp.minimum(list_ref[r, kk], row_blocks) * side, side)
                picks.append(sources_ref[pl.ds(at, side), :])
            total = total + mm(blocks, jnp.concatenate(picks, axis=0))
        base_ref[rows, :] = projected[rows, :] + total[:, :width]
        local_ref[rows, :] = total[:, width : 2 * width] + total[:, 2 * width :]


def middle_kernel(dims, place_ref, *refs):
    row_blocks, fanout, side, width, ns, nd, inner_cap, outer_cap = dims
    n_in = (ns - 1) + (nd - 1)
    arrived = refs[:n_in]
    base_ref, scale_ref, picked_ref, turned_ref, weight_ref, cotangent_ref = refs[n_in : n_in + 6]
    act_ref, scaled_ref, half_ref, total_ref = refs[n_in + 6 : n_in + 10]
    leaving = refs[n_in + 10 :]
    total_ref[...] = jnp.zeros_like(total_ref)
    i = 0
    for ref in arrived:
        for j in range(ref.shape[0] // side):
            term = mm(picked_ref[i], ref[j * side : (j + 1) * side, :])
            rows = pl.ds(pl.multiple_of(place_ref[i] * side, side), side)
            total_ref[rows, :] += term
            i += 1
    weight = split(weight_ref[...])
    for r in range(row_blocks):
        rows = slice(r * side, (r + 1) * side)
        scale = scale_ref[rows, :]
        mixed = (base_ref[rows, :] + mm3(split(total_ref[rows, :]), weight)) * scale
        gate = jax.nn.sigmoid(mixed)
        act_ref[rows, :] = mixed * gate
        scaled = cotangent_ref[rows, :] * gate * (1.0 + mixed * (1.0 - gate)) * scale
        scaled_ref[rows, :] = scaled
        half_ref[rows, :] = scaled.astype(BF16)
    i = 0
    for ref in leaving:
        for j in range(ref.shape[0] // side):
            rows = pl.ds(pl.multiple_of(place_ref[i] * side, side), side)
            ref[j * side : (j + 1) * side, :] = mm(turned_ref[i], half_ref[rows, :]).astype(BF16)
            i += 1


def weight_kernel(nd, features_ref, local_ref, total_ref, scaled_ref, half_ref, *out_refs):
    p = lax.axis_index("dom")
    down = ((0,), (0,))
    ah, al = split(local_ref[...] + total_ref[...])
    half = half_ref[...]
    term = mm3(split(features_ref[...]), split(scaled_ref[...]), down)
    term = term + (mm(ah, half, down) + mm(al, half, down))
    scratch_ref = out_refs[-1]
    scratch_ref[...] = term
    piece = term.shape[0] // nd
    for out_ref, k in zip(out_refs[:-1], [0] + exchange_order(nd)):
        at = pl.multiple_of(partner(p, k, nd) * piece, 8)
        out_ref[...] = scratch_ref[pl.ds(at, piece), :]


def spread_kernel(dims, list_ref, values_ref, scaled_ref, half_ref, weight_ref, out_ref, sums_ref):
    row_blocks, fanout, side, width = dims
    sums_ref[...] = jnp.zeros_like(sums_ref)
    for r in range(row_blocks):
        half = half_ref[r * side : (r + 1) * side, :]
        for k in range(fanout):
            at = pl.multiple_of(jnp.minimum(list_ref[r, k], row_blocks) * side, side)
            sums_ref[pl.ds(at, side), :] += mm(values_ref[r, k], half, ((0,), (0,)))
    grad = scaled_ref[...] + sums_ref[: row_blocks * side, :]
    out_ref[...] = mm3(split(grad), split(weight_ref[...]), ((1,), (1,)))


def finish_kernel(ns, nd, side, inner_ref, outer_ref, weight_ref, part_ref, *refs):
    arrived, out_ref, sums_ref = refs[:-2], refs[-2], refs[-1]
    sums_ref[...] = jnp.zeros_like(sums_ref)
    slots = []
    for axis, n, targets_ref in (("shard", ns, inner_ref), ("dom", nd, outer_ref)):
        me = lax.axis_index(axis)
        for k in exchange_order(n):
            slots.append((targets_ref, partner(me, k, n)))
    for ref, (targets_ref, peer) in zip(arrived, slots):
        for j in range(ref.shape[0] // side):
            target = targets_ref[0, peer, j]
            rows = pl.ds(pl.multiple_of(jnp.maximum(target, 0) * side, side), side)
            term = ref[j * side : (j + 1) * side, :].astype(F32)
            sums_ref[rows, :] += jnp.where(target >= 0, term, 0.0)
    out_ref[...] = part_ref[...] + mm3(split(sums_ref[...]), split(weight_ref[...]), ((1,), (1,)))


def add_kernel(*refs):
    total = refs[0][...]
    for ref in refs[1:-1]:
        total = total + ref[...]
    refs[-1][...] = total


def place_kernel(nd, *refs):
    p = lax.axis_index("dom")
    out_ref = refs[-1]
    piece = refs[0].shape[0]
    for ref, k in zip(refs[:-1], [0] + exchange_order(nd)):
        at = pl.multiple_of(back_partner(p, k, nd) * piece, 8)
        out_ref[pl.ds(at, piece), :] = ref[...]


def on_device(features, weight, cotangent, block_values, block_list, send_inner, send_outer):
    node_count, width = features.shape
    row_blocks, fanout, side, _ = block_values.shape
    ns = lax.axis_size("shard")
    nd = lax.axis_size("dom")
    inner_cap = send_inner.shape[2]
    outer_cap = send_outer.shape[2]
    slots = (ns - 1) * inner_cap + (nd - 1) * outer_cap
    dims = (row_blocks, fanout, side, width, ns, nd, inner_cap, outer_cap)
    shape = jax.ShapeDtypeStruct
    rows_f32 = shape((node_count, width), F32)
    rows_f16 = shape((node_count, width), BF16)
    packed_inner = [shape((inner_cap * side, width), BF16)] * (ns - 1)
    packed_outer = [shape((outer_cap * side, width), BF16)] * (nd - 1)
    nbytes = node_count * width * 4

    def pack(axis, n, targets, shapes):
        return call(
            functools.partial(pack_kernel, axis, n, side), shapes, 0, 3 * nbytes,
            [SMEM, VMEM], [VMEM] * len(shapes),
        )(targets, features)

    inner_out = pack("shard", ns, send_inner, packed_inner)
    inner_in = [send(x, "shard", k, ns) for x, k in zip(inner_out, exchange_order(ns))]
    outer_out = pack("dom", nd, send_outer, packed_outer)
    outer_in = [send(x, "dom", k, nd) for x, k in zip(outer_out, exchange_order(nd))]

    base, local, scale, picked, turned, place = call(
        functools.partial(local_kernel, dims),
        [
            rows_f32, rows_f32, rows_f32,
            shape((slots, side, side), BF16), shape((slots, side, side), BF16), shape((slots,), jnp.int32),
        ],
        4 * row_blocks * fanout * side * side * width * 3, 12 * nbytes,
        [SMEM, VMEM, VMEM, VMEM], [VMEM] * 5 + [SMEM],
        [
            pltpu.VMEM(((row_blocks + 1) * side, 3 * width), BF16),
            pltpu.SMEM((row_blocks + ns * inner_cap + nd * outer_cap,), jnp.int32),
        ],
    )(block_list, features, weight, block_values)

    n_in = ns - 1 + nd - 1
    outs = call(
        functools.partial(middle_kernel, dims),
        [rows_f32, rows_f32, rows_f16, rows_f32] + packed_inner + packed_outer,
        2 * slots * side * side * width * 2, 8 * nbytes,
        [SMEM] + [VMEM] * (n_in + 6), [VMEM] * (4 + n_in),
    )(place, *inner_in, *outer_in, base, scale, picked, turned, weight, cotangent)
    activations, scaled, half, total = outs[:4]
    inner_terms, outer_terms = outs[4 : 4 + ns - 1], outs[4 + ns - 1 :]

    inner_back = [send_back(x, "shard", k, ns) for x, k in zip(inner_terms, exchange_order(ns))]
    piece = shape((width // nd, width), F32)
    pieces = call(
        functools.partial(weight_kernel, nd),
        [piece] * nd, 10 * node_count * width * width, 5 * nbytes,
        [VMEM] * 5, [VMEM] * nd, [pltpu.VMEM((width, width), F32)],
    )(features, local, total, scaled, half)
    outer_back = [send_back(x, "dom", k, nd) for x, k in zip(outer_terms, exchange_order(nd))]

    add = lambda xs: call(
        add_kernel, piece, 0, len(xs) * nbytes // 8, [VMEM] * len(xs), VMEM
    )(*xs)
    weight_sum = add([pieces[0]] + [send(x, "dom", k, nd) for x, k in zip(pieces[1:], exchange_order(nd))])
    weight_sum = add([weight_sum] + [send(weight_sum, "shard", k, ns) for k in exchange_order(ns)])
    gathered = [weight_sum] + [send(weight_sum, "dom", k, nd) for k in exchange_order(nd)]
    grad_weight = call(
        functools.partial(place_kernel, nd), shape((width, width), F32), 0, nbytes,
        [VMEM] * nd, VMEM,
    )(*gathered)

    part = call(
        functools.partial(spread_kernel, dims[:4]), rows_f32,
        2 * row_blocks * fanout * side * side * width, 8 * nbytes,
        [SMEM] + [VMEM] * 4, VMEM, [pltpu.VMEM(((row_blocks + 1) * side, width), F32)],
    )(block_list, block_values, scaled, half, weight)
    grad_features = call(
        functools.partial(finish_kernel, ns, nd, side), rows_f32,
        6 * node_count * width * width, 4 * nbytes,
        [SMEM, SMEM] + [VMEM] * (2 + n_in), VMEM, [pltpu.VMEM((node_count, width), F32)],
    )(send_inner, send_outer, weight, part, *inner_back, *outer_back)
    return (activations, grad_features, grad_weight)


def solution(mesh):
    rows = ("copies", "shard", "dom")
    return jax.shard_map(
        on_device,
        mesh=mesh,
        in_specs=(
            P(rows, None),
            P(),
            P(rows, None),
            P(rows, None, None, None),
            P(rows, None),
            P(rows, None, None),
            P(rows, None, None),
        ),
        out_specs=(P(rows, None), P(rows, None), P("copies", None)),
        check_vma=False,
    )
```

time: 218 us -> 55.3 us (0.25)
  waiting for transfers between devices: 119 us -> 11.4 us
  other arithmetic: 25.8 us -> 0 us
  between operations: 14.2 us -> 0.77 us
  Pallas kernels: 0 us -> 12.9 us
  matrix products: 12.2 us -> 0 us
  local copies, waits for them, and re-layouts: 19.9 us -> 7.9 us
  blocking collectives: 11.9 us -> 0 us
  starting transfers between devices: 14.2 us -> 22 us
    psum x1 -> x0, waiting for transfers between devices: 86 us -> none  [on_device(): grad_weight = lax.psum(weight_term, ('shard', 'dom'))]
    all_to_all x3 -> x0, waiting for transfers between devices: 32.6 us -> none  [the longest x1 13.9 us: on_device(): lax.all_to_all(pack_rows(half_blocks, inner_targets), 'shard', split_axis...]
    ppermute x0 -> x21, starting transfers between devices: none -> 22 us  [the longest x15 15.9 us: send(): return lax.ppermute(x, axis, [(i, partner(i, k, n)) for i in range(n)])]
    scatter-add x2 -> x0, other arithmetic: 14.5 us -> none  [the longest x1 12.3 us: on_device(): per_source = jnp.zeros((row_blocks + remote_slots, block_side, feat_width...]
    all_to_all x3 -> x0, starting transfers between devices: 14.2 us -> none  [the longest x1 5.71 us: on_device(): lax.all_to_all(pack_rows(half_blocks, inner_targets), 'shard', split_axis...]
    pallas_call x0 -> x10, Pallas kernels: none -> 12.9 us  [the longest x1 3.66 us: on_device(): call(functools.partial(local_kernel, dims), [rows_f32, rows_f32, rows_f32...]
    dot_general x5 -> x0, matrix products: 12.2 us -> none  [the longest x1 4.52 us: on_device(): jnp.einsum('rkab,raf->rkbf', block_values, scaled_half, preferred_element...]
    all_to_all x1 -> x0, blocking collectives: 11.9 us -> none  [on_device(): lax.all_to_all(remote_terms[inner_slots:].reshape(dom_count, outer_cap, b...]
  transfers between devices with their start and end apart: 4 -> 21, of which waited for: 4 -> 6; matrix products, arithmetic and copies ran while one was open for 3% -> 1% of each run, Pallas kernels for 0% -> 16%
where the time goes in v1:
time: 55.3 us; the launch traced here: 55 us
  starting transfers between devices  22 us (40%)
  Pallas kernels  12.9 us (23%)
  waiting for transfers between devices  11.4 us (21%)
  local copies, waits for them, and re-layouts  7.9 us (14%)
  between operations  0.77 us (1%)
    ppermute x15, starting transfers between devices, send(): return lax.ppermute(x, axis, [(i, partner(i, k, n)) for i in range(n)])  15.9 us
    ppermute x15, waiting for transfers between devices, send(): return lax.ppermute(x, axis, [(i, partner(i, k, n)) for i in range(n)])  8.18 us
    unnamed x24, local copies, waits for them, and re-layouts  7.9 us
    ppermute x6, starting transfers between devices, send_back(): return lax.ppermute(x, axis, [(i, back_partner(i, k, n)) for i in range(n)])  6.06 us
    pallas_call x1, Pallas kernels, on_device(): call(functools.partial(local_kernel, dims), [rows_f32, rows_f32, rows_f32...  3.66 us
    ppermute x6, waiting for transfers between devices, send_back(): return lax.ppermute(x, axis, [(i, back_partner(i, k, n)) for i in range(n)])  3.2 us
    pallas_call x1, Pallas kernels, on_device(): call(functools.partial(middle_kernel, dims), [rows_f32, rows_f32, rows_f1...  2.34 us
    pallas_call x1, Pallas kernels, on_device(): call(functools.partial(spread_kernel, dims[:4]), rows_f32, 2 * row_blocks...  2.27 us
  transfers between devices with their start and end apart: 21, of which 6 were waited for; matrix products, arithmetic and copies ran while one was open for 1% of the time, Pallas kernels for 16%

profile of v1, /device:TPU:0, one launch (start us, length us, event | category | flops | bytes accessed | tf_op | source)
XLA Modules:
  0.0 55.0 jit_solution(11974297852075511596)
XLA Ops:
  1.4 1.0 %copy-done = f32[512,256]{1,0:T(8,128)S(1)} copy-done((f32[512,256]{1,0:T(8,128)S(1)}, f32[512,256]{1,0:T(8,128)}, u32[]{:S(2)}) %copy-start) | copy-done | bytes 524312
  3.1 2.4 %collective-permute-start.3 = (bf16[256,256]{1,0:T(8,128)(2,1)S(1)}, bf16[256,256]{1,0:T(8,128)(2,1)S(1)}, u32[]{:S(2)}, u32[]{:S(2)}) collective-permute-start(bf16[256,256]{1,0:T(8,128)(2,1)S(1)} %get-tuple-element.33), channel_id=1, source_target_pairs={{0,3},{1,2},{2,1},{3,0},{4,7},{5,6},{6,5},{7,4},{8,11},{9,10},{10,... | collective-permute-start | bytes 393224 | tf_op jit(solution)/shard_map/ppermute | solution.py:33
  7.0 1.0 %copy-done.1 = f32[512,256]{1,0:T(8,128)S(1)} copy-done((f32[512,256]{1,0:T(8,128)S(1)}, f32[512,256]{1,0:T(8,128)}, u32[]{:S(2)}) %copy-start.1) | copy-done | bytes 524312
  8.7 3.9 %collective-permute-start = (bf16[256,256]{1,0:T(8,128)(2,1)S(1)}, bf16[256,256]{1,0:T(8,128)(2,1)S(1)}, u32[]{:S(2)}, u32[]{:S(2)}) collective-permute-start(bf16[256,256]{1,0:T(8,128)(2,1)S(1)} %get-tuple-element.30), channel_id=1, source_target_pairs={{0,12},{4,8},{8,4},{12,0},{1,13},{5,9},{9,5},{13,1},{2,14},{6,10},... | collective-permute-start | bytes 393224 | tf_op jit(solution)/shard_map/ppermute | solution.py:33
  13.3 1.0 %copy-done.2 = f32[512,256]{1,0:T(8,128)S(1)} copy-done((f32[512,256]{1,0:T(8,128)S(1)}, f32[512,256]{1,0:T(8,128)}, u32[]{:S(2)}) %copy-start.2) | copy-done | bytes 524312
  14.3 0.9 %copy-done.4 = f32[256,256]{1,0:T(8,128)S(1)} copy-done((f32[256,256]{1,0:T(8,128)S(1)}, f32[256,256]{1,0:T(8,128)}, u32[]{:S(2)}) %copy-start.4) | copy-done | bytes 262168
  15.3 1.6 %copy-done.6 = bf16[4,16,128,128]{3,2,1,0:T(8,128)(2,1)S(1)} copy-done((bf16[4,16,128,128]{3,2,1,0:T(8,128)(2,1)S(1)}, bf16[4,16,128,128]{3,2,1,0:T(8,128)(2,1)}, u32[]{:S(2)}) %copy-start.6) | copy-done | bytes 2097176
  17.5 3.7 %shard_map.94 = (f32[512,256]{1,0:T(8,128)S(1)}, f32[512,256]{1,0:T(8,128)S(1)}, f32[512,256]{1,0:T(8,128)S(1)}, bf16[12,128,128]{2,1,0:T(8,128)(2,1)S(1)}, bf16...) custom-call(s32[4,16]{1,0:T(4,128)S(1)} %copy-done.9, f32[512,256]{1,0:T(8,128)S(1)} %copy-done.2, f32[256,256]{1,0:T(8,128)S(1)} %copy-done.4, ...), custom_call_target="tpu_custom_call" | custom-call | flops 3221225472 | bytes 6291456 | tf_op jit(solution)/shard_map/pallas_call | solution.py:256
  21.2 2.8 %collective-permute-done.1.refs_1_ = bf16[256,256]{1,0:T(8,128)(2,1)S(1)} collective-permute-done((bf16[256,256]{1,0:T(8,128)(2,1)S(1)}, bf16[256,256]{1,0:T(8,128)(2,1)S(1)}, u32[]{:S(2)}, u32[]{:S(2)}) %collective-permute-start.1) | collective-permute-done | bytes 131104 | tf_op jit(solution)/shard_map/ppermute | solution.py:33
  24.1 2.3 %shard_map.97 = (f32[512,256]{1,0:T(8,128)}, f32[512,256]{1,0:T(8,128)S(1)}, bf16[512,256]{1,0:T(8,128)(2,1)S(1)}, f32[512,256]{1,0:T(8,128)S(1)}, bf16[256,256]...) custom-call(s32[12]{0:T(128)S(1)} %get-tuple-element.29.place_ref, ...), custom_call_target="tpu_custom_call" | custom-call | flops 201326592 | bytes 4194304 | tf_op jit(solution)/shard_map/pallas_call | solution.py:271
  27.4 1.2 %collective-permute-start.13 = (f32[64,256]{1,0:T(8,128)S(1)}, f32[64,256]{1,0:T(8,128)S(1)}, u32[]{:S(2)}, u32[]{:S(2)}) collective-permute-start(f32[64,256]{1,0:T(8,128)S(1)} %get-tuple-element.53), channel_id=1, source_target_pairs={{0,2},{1,3},{2,0},{3,1},{4,6},{5,7},{6,4},{7,5},{8,10},{9,11},{10,... | collective-permute-start | bytes 196616 | tf_op jit(solution)/shard_map/ppermute | solution.py:33
  29.0 2.5 %collective-permute-start.6 = (bf16[256,256]{1,0:T(8,128)(2,1)S(1)}, bf16[256,256]{1,0:T(8,128)(2,1)S(1)}, u32[]{:S(2)}, u32[]{:S(2)}) collective-permute-start(bf16[256,256]{1,0:T(8,128)(2,1)S(1)} %get-tuple-element.43), channel_id=1, source_target_pairs={{0,12},{4,8},{8,4},{12,0},{1,13},{5,9},{9,5},{13,1},{2,14},{6,10},... | collective-permute-start | bytes 393224 | tf_op jit(solution)/shard_map/ppermute | solution.py:37
  31.5 1.3 %collective-permute-done.13.refs_2_ = f32[64,256]{1,0:T(8,128)S(1)} collective-permute-done((f32[64,256]{1,0:T(8,128)S(1)}, f32[64,256]{1,0:T(8,128)S(1)}, u32[]{:S(2)}, u32[]{:S(2)}) %collective-permute-start.13) | collective-permute-done | bytes 65568 | tf_op jit(solution)/shard_map/ppermute | solution.py:33
  32.9 3.1 %collective-permute-start.16 = (f32[64,256]{1,0:T(8,128)S(1)}, f32[64,256]{1,0:T(8,128)S(1)}, u32[]{:S(2)}, u32[]{:S(2)}) collective-permute-start(f32[64,256]{1,0:T(8,128)S(1)} %shard_map.101.refs_0_), channel_id=1, source_target_pairs={{0,8},{4,12},{8,0},{12,4},{1,9},{5,13},{9,1},{13,5},{2,10},{6,14},... | collective-permute-start | bytes 196616 | tf_op jit(solution)/shard_map/ppermute | solution.py:33
  36.0 1.3 %collective-permute-start.15 = (f32[64,256]{1,0:T(8,128)S(1)}, f32[64,256]{1,0:T(8,128)S(1)}, u32[]{:S(2)}, u32[]{:S(2)}) collective-permute-start(f32[64,256]{1,0:T(8,128)S(1)} %shard_map.101.refs_0_), channel_id=1, source_target_pairs={{0,12},{4,8},{8,4},{12,0},{1,13},{5,9},{9,5},{13,1},{2,14},{6,10},... | collective-permute-start | bytes 196616 | tf_op jit(solution)/shard_map/ppermute | solution.py:33
  37.5 1.4 %collective-permute-done.17.refs_3_ = f32[64,256]{1,0:T(8,128)S(1)} collective-permute-done((f32[64,256]{1,0:T(8,128)S(1)}, f32[64,256]{1,0:T(8,128)S(1)}, u32[]{:S(2)}, u32[]{:S(2)}) %collective-permute-start.17) | collective-permute-done | bytes 65568 | tf_op jit(solution)/shard_map/ppermute | solution.py:33
  38.9 1.5 %collective-permute-start.8 = (bf16[256,256]{1,0:T(8,128)(2,1)S(1)}, bf16[256,256]{1,0:T(8,128)(2,1)S(1)}, u32[]{:S(2)}, u32[]{:S(2)}) collective-permute-start(bf16[256,256]{1,0:T(8,128)(2,1)S(1)} %get-tuple-element.45), channel_id=1, source_target_pairs={{0,4},{4,0},{8,12},{12,8},{1,5},{5,1},{9,13},{13,9},{2,6},{6,2},{1... | collective-permute-start | bytes 393224 | tf_op jit(solution)/shard_map/ppermute | solution.py:37
  40.4 2.6 %collective-permute-done.16.refs_2_ = f32[64,256]{1,0:T(8,128)S(1)} collective-permute-done((f32[64,256]{1,0:T(8,128)S(1)}, f32[64,256]{1,0:T(8,128)S(1)}, u32[]{:S(2)}, u32[]{:S(2)}) %collective-permute-start.16) | collective-permute-done | bytes 65568 | tf_op jit(solution)/shard_map/ppermute | solution.py:33
  43.0 1.2 %collective-permute-start.10 = (bf16[256,256]{1,0:T(8,128)(2,1)S(1)}, bf16[256,256]{1,0:T(8,128)(2,1)S(1)}, u32[]{:S(2)}, u32[]{:S(2)}) collective-permute-start(bf16[256,256]{1,0:T(8,128)(2,1)S(1)} %get-tuple-element.47), channel_id=1, source_target_pairs={{0,2},{1,3},{2,0},{3,1},{4,6},{5,7},{6,4},{7,5},{8,10},{9,11},{10,... | collective-permute-start | bytes 393224 | tf_op jit(solution)/shard_map/ppermute | solution.py:37
  44.9 3.2 %collective-permute-done.7.refs_1_ = bf16[256,256]{1,0:T(8,128)(2,1)S(1)} collective-permute-done((bf16[256,256]{1,0:T(8,128)(2,1)S(1)}, bf16[256,256]{1,0:T(8,128)(2,1)S(1)}, u32[]{:S(2)}, u32[]{:S(2)}) %collective-permute-start.7) | collective-permute-done | bytes 131104 | tf_op jit(solution)/shard_map/ppermute | solution.py:37
  48.1 1.0 %collective-permute-start.19 = (f32[64,256]{1,0:T(8,128)S(1)}, f32[64,256]{1,0:T(8,128)S(1)}, u32[]{:S(2)}, u32[]{:S(2)}) collective-permute-start(f32[64,256]{1,0:T(8,128)S(1)} %shard_map.102.refs_0_), channel_id=1, source_target_pairs={{0,2},{1,3},{2,0},{3,1},{4,6},{5,7},{6,4},{7,5},{8,10},{9,11},{10,... | collective-permute-start | bytes 196616 | tf_op jit(solution)/shard_map/ppermute | solution.py:33
  49.1 0.8 %collective-permute-start.18 = (f32[64,256]{1,0:T(8,128)S(1)}, f32[64,256]{1,0:T(8,128)S(1)}, u32[]{:S(2)}, u32[]{:S(2)}) collective-permute-start(f32[64,256]{1,0:T(8,128)S(1)} %shard_map.102.refs_0_), channel_id=1, source_target_pairs={{0,3},{1,2},{2,1},{3,0},{4,7},{5,6},{6,5},{7,4},{8,11},{9,10},{10,... | collective-permute-start | bytes 196616 | tf_op jit(solution)/shard_map/ppermute | solution.py:33
  50.0 2.3 %shard_map.98.part_ref = f32[512,256]{1,0:T(8,128)S(1)} custom-call(s32[4,16]{1,0:T(4,128)S(1)} %copy-done.10, bf16[4,16,128,128]{3,2,1,0:T(8,128)(2,1)S(1)} %copy-done.7, f32[512,256]{1,0:T(8,128)S(1)} %get-tuple-element.41.scaled_ref, bf16[512,256]{1,0:T(8,128)(2,1)S(1)} %get-tuple-element.42.half_ref, f32[256,256]{1,0:T(8,128)S(1)} %copy-done.5), custom_call_target="tpu_custom_call" | custom-call | flops 536870912 | bytes 4194304 | tf_op jit(solution)/shard_map/pallas_call | solution.py:300
  52.2 2.0 %shard_map.99 = f32[512,256]{1,0:T(8,128)} custom-call(s32[1,4,2]{2,1,0:T(4,128)S(1)} %copy.10.targets_ref.inner_ref, s32[1,4,2]{2,1,0:T(4,128)S(1)} %copy.11.targets_ref.outer_ref, f32[256,256]{1,0:T(8,128)S(1)} %copy-done.5, f32[512,256]{1,0:T(8,128)S(1)} %shard_map.98.part_ref, bf16[256,256]{1,0:T(8,128)(2,1)S(1)} %collective-permute-done.6.refs_0_, ...), custom_call_target="tpu_custom_call" | custom-call | flops 201326592 | bytes 2097152 | tf_op jit(solution)/shard_map/pallas_call | solution.py:305
  (52 shorter events, 8.1 us)
Async XLA Ops:
  3.1 9.5 %collective-permute-start.3 = (bf16[256,256]{1,0:T(8,128)(2,1)S(1)}, bf16[256,256]{1,0:T(8,128)(2,1)S(1)}, u32[]{:S(2)}, u32[]{:S(2)}) collective-permute-start(bf16[256,256]{1,0:T(8,128)(2,1)S(1)} %get-tuple-element.33), channel_id=1, source_target_pairs={{0,3},{1,2},{2,1},{3,0},{4,7},{5,6},{6,5},{7,4},{8,11},{9,10},{10,... | collective-permute-start | bytes 393224 | tf_op jit(solution)/shard_map/ppermute | solution.py:33
  5.5 15.7 %collective-permute-start.4 = (bf16[256,256]{1,0:T(8,128)(2,1)S(1)}, bf16[256,256]{1,0:T(8,128)(2,1)S(1)}, u32[]{:S(2)}, u32[]{:S(2)}) collective-permute-start(bf16[256,256]{1,0:T(8,128)(2,1)S(1)} %get-tuple-element.34), channel_id=1, source_target_pairs={{0,2},{1,3},{2,0},{3,1},{4,6},{5,7},{6,4},{7,5},{8,10},{9,11},{10,... | collective-permute-start | bytes 393224 | tf_op jit(solution)/shard_map/ppermute | solution.py:33
  6.2 15.0 %collective-permute-start.5 = (bf16[256,256]{1,0:T(8,128)(2,1)S(1)}, bf16[256,256]{1,0:T(8,128)(2,1)S(1)}, u32[]{:S(2)}, u32[]{:S(2)}) collective-permute-start(bf16[256,256]{1,0:T(8,128)(2,1)S(1)} %get-tuple-element.35), channel_id=1, source_target_pairs={{0,1},{1,0},{2,3},{3,2},{4,5},{5,4},{6,7},{7,6},{8,9},{9,8},{10,11... | collective-permute-start | bytes 393224 | tf_op jit(solution)/shard_map/ppermute | solution.py:33
  8.7 12.5 %collective-permute-start = (bf16[256,256]{1,0:T(8,128)(2,1)S(1)}, bf16[256,256]{1,0:T(8,128)(2,1)S(1)}, u32[]{:S(2)}, u32[]{:S(2)}) collective-permute-start(bf16[256,256]{1,0:T(8,128)(2,1)S(1)} %get-tuple-element.30), channel_id=1, source_target_pairs={{0,12},{4,8},{8,4},{12,0},{1,13},{5,9},{9,5},{13,1},{2,14},{6,10},... | collective-permute-start | bytes 393224 | tf_op jit(solution)/shard_map/ppermute | solution.py:33
  12.6 11.5 %collective-permute-start.1 = (bf16[256,256]{1,0:T(8,128)(2,1)S(1)}, bf16[256,256]{1,0:T(8,128)(2,1)S(1)}, u32[]{:S(2)}, u32[]{:S(2)}) collective-permute-start(bf16[256,256]{1,0:T(8,128)(2,1)S(1)} %get-tuple-element.31), channel_id=1, source_target_pairs={{0,8},{4,12},{8,0},{12,4},{1,9},{5,13},{9,1},{13,5},{2,10},{6,14},... | collective-permute-start | bytes 393224 | tf_op jit(solution)/shard_map/ppermute | solution.py:33
  12.6 11.5 %collective-permute-start.2 = (bf16[256,256]{1,0:T(8,128)(2,1)S(1)}, bf16[256,256]{1,0:T(8,128)(2,1)S(1)}, u32[]{:S(2)}, u32[]{:S(2)}) collective-permute-start(bf16[256,256]{1,0:T(8,128)(2,1)S(1)} %get-tuple-element.32), channel_id=1, source_target_pairs={{0,4},{4,0},{8,12},{12,8},{1,5},{5,1},{9,13},{13,9},{2,6},{6,2},{1... | collective-permute-start | bytes 393224 | tf_op jit(solution)/shard_map/ppermute | solution.py:33
  17.5 6.6 %copy-start.8 = (f32[512,256]{1,0:T(8,128)S(1)}, f32[512,256]{1,0:T(8,128)}, u32[]{:S(2)}) copy-start(f32[512,256]{1,0:T(8,128)} %refs_11_.1) | copy-start | bytes 1572868
  26.4 23.5 %copy-start.7 = (bf16[4,16,128,128]{3,2,1,0:T(8,128)(2,1)S(1)}, bf16[4,16,128,128]{3,2,1,0:T(8,128)(2,1)}, u32[]{:S(2)}) copy-start(bf16[4,16,128,128]{3,2,1,0:T(8,128)(2,1)} %values_ref.3) | copy-start | bytes 6291460
  26.4 23.5 %copy-start.10 = (s32[4,16]{1,0:T(4,128)S(1)}, s32[4,16]{1,0:T(4,128)}, u32[]{:S(2)}) copy-start(s32[4,16]{1,0:T(4,128)} %list_ref.3) | copy-start | bytes 772
  27.1 4.5 %collective-permute-start.12 = (f32[64,256]{1,0:T(8,128)S(1)}, f32[64,256]{1,0:T(8,128)S(1)}, u32[]{:S(2)}, u32[]{:S(2)}) collective-permute-start(f32[64,256]{1,0:T(8,128)S(1)} %get-tuple-element.52), channel_id=1, source_target_pairs={{0,3},{1,2},{2,1},{3,0},{4,7},{5,6},{6,5},{7,4},{8,11},{9,10},{10,... | collective-permute-start | bytes 196616 | tf_op jit(solution)/shard_map/ppermute | solution.py:33
  27.4 5.4 %collective-permute-start.13 = (f32[64,256]{1,0:T(8,128)S(1)}, f32[64,256]{1,0:T(8,128)S(1)}, u32[]{:S(2)}, u32[]{:S(2)}) collective-permute-start(f32[64,256]{1,0:T(8,128)S(1)} %get-tuple-element.53), channel_id=1, source_target_pairs={{0,2},{1,3},{2,0},{3,1},{4,6},{5,7},{6,4},{7,5},{8,10},{9,11},{10,... | collective-permute-start | bytes 196616 | tf_op jit(solution)/shard_map/ppermute | solution.py:33
  28.6 4.2 %collective-permute-start.14 = (f32[64,256]{1,0:T(8,128)S(1)}, f32[64,256]{1,0:T(8,128)S(1)}, u32[]{:S(2)}, u32[]{:S(2)}) collective-permute-start(f32[64,256]{1,0:T(8,128)S(1)} %get-tuple-element.54), channel_id=1, source_target_pairs={{0,1},{1,0},{2,3},{3,2},{4,5},{5,4},{6,7},{7,6},{8,9},{9,8},{10,11... | collective-permute-start | bytes 196616 | tf_op jit(solution)/shard_map/ppermute | solution.py:33
  29.0 15.2 %collective-permute-start.6 = (bf16[256,256]{1,0:T(8,128)(2,1)S(1)}, bf16[256,256]{1,0:T(8,128)(2,1)S(1)}, u32[]{:S(2)}, u32[]{:S(2)}) collective-permute-start(bf16[256,256]{1,0:T(8,128)(2,1)S(1)} %get-tuple-element.43), channel_id=1, source_target_pairs={{0,12},{4,8},{8,4},{12,0},{1,13},{5,9},{9,5},{13,1},{2,14},{6,10},... | collective-permute-start | bytes 393224 | tf_op jit(solution)/shard_map/ppermute | solution.py:37
  32.8 6.1 %collective-permute-start.17 = (f32[64,256]{1,0:T(8,128)S(1)}, f32[64,256]{1,0:T(8,128)S(1)}, u32[]{:S(2)}, u32[]{:S(2)}) collective-permute-start(f32[64,256]{1,0:T(8,128)S(1)} %shard_map.101.refs_0_), channel_id=1, source_target_pairs={{0,4},{4,0},{8,12},{12,8},{1,5},{5,1},{9,13},{13,9},{2,6},{6,2},{1... | collective-permute-start | bytes 196616 | tf_op jit(solution)/shard_map/ppermute | solution.py:33
  32.9 10.1 %collective-permute-start.16 = (f32[64,256]{1,0:T(8,128)S(1)}, f32[64,256]{1,0:T(8,128)S(1)}, u32[]{:S(2)}, u32[]{:S(2)}) collective-permute-start(f32[64,256]{1,0:T(8,128)S(1)} %shard_map.101.refs_0_), channel_id=1, source_target_pairs={{0,8},{4,12},{8,0},{12,4},{1,9},{5,13},{9,1},{13,5},{2,10},{6,14},... | collective-permute-start | bytes 196616 | tf_op jit(solution)/shard_map/ppermute | solution.py:33
  36.0 7.0 %collective-permute-start.15 = (f32[64,256]{1,0:T(8,128)S(1)}, f32[64,256]{1,0:T(8,128)S(1)}, u32[]{:S(2)}, u32[]{:S(2)}) collective-permute-start(f32[64,256]{1,0:T(8,128)S(1)} %shard_map.101.refs_0_), channel_id=1, source_target_pairs={{0,12},{4,8},{8,4},{12,0},{1,13},{5,9},{9,5},{13,1},{2,14},{6,10},... | collective-permute-start | bytes 196616 | tf_op jit(solution)/shard_map/ppermute | solution.py:33
  37.3 10.8 %collective-permute-start.7 = (bf16[256,256]{1,0:T(8,128)(2,1)S(1)}, bf16[256,256]{1,0:T(8,128)(2,1)S(1)}, u32[]{:S(2)}, u32[]{:S(2)}) collective-permute-start(bf16[256,256]{1,0:T(8,128)(2,1)S(1)} %get-tuple-element.44), channel_id=1, source_target_pairs={{0,8},{4,12},{8,0},{12,4},{1,9},{5,13},{9,1},{13,5},{2,10},{6,14},... | collective-permute-start | bytes 393224 | tf_op jit(solution)/shard_map/ppermute | solution.py:37
  38.9 9.1 %collective-permute-start.8 = (bf16[256,256]{1,0:T(8,128)(2,1)S(1)}, bf16[256,256]{1,0:T(8,128)(2,1)S(1)}, u32[]{:S(2)}, u32[]{:S(2)}) collective-permute-start(bf16[256,256]{1,0:T(8,128)(2,1)S(1)} %get-tuple-element.45), channel_id=1, source_target_pairs={{0,4},{4,0},{8,12},{12,8},{1,5},{5,1},{9,13},{13,9},{2,6},{6,2},{1... | collective-permute-start | bytes 393224 | tf_op jit(solution)/shard_map/ppermute | solution.py:37
  43.0 6.1 %collective-permute-start.9 = (bf16[256,256]{1,0:T(8,128)(2,1)S(1)}, bf16[256,256]{1,0:T(8,128)(2,1)S(1)}, u32[]{:S(2)}, u32[]{:S(2)}) collective-permute-start(bf16[256,256]{1,0:T(8,128)(2,1)S(1)} %get-tuple-element.46), channel_id=1, source_target_pairs={{0,3},{1,2},{2,1},{3,0},{4,7},{5,6},{6,5},{7,4},{8,11},{9,10},{10,... | collective-permute-start | bytes 393224 | tf_op jit(solution)/shard_map/ppermute | solution.py:37
  43.0 9.2 %collective-permute-start.10 = (bf16[256,256]{1,0:T(8,128)(2,1)S(1)}, bf16[256,256]{1,0:T(8,128)(2,1)S(1)}, u32[]{:S(2)}, u32[]{:S(2)}) collective-permute-start(bf16[256,256]{1,0:T(8,128)(2,1)S(1)} %get-tuple-element.47), channel_id=1, source_target_pairs={{0,2},{1,3},{2,0},{3,1},{4,6},{5,7},{6,4},{7,5},{8,10},{9,11},{10,... | collective-permute-start | bytes 393224 | tf_op jit(solution)/shard_map/ppermute | solution.py:37
  44.2 8.0 %collective-permute-start.11 = (bf16[256,256]{1,0:T(8,128)(2,1)S(1)}, bf16[256,256]{1,0:T(8,128)(2,1)S(1)}, u32[]{:S(2)}, u32[]{:S(2)}) collective-permute-start(bf16[256,256]{1,0:T(8,128)(2,1)S(1)} %get-tuple-element.48), channel_id=1, source_target_pairs={{0,1},{1,0},{2,3},{3,2},{4,5},{5,4},{6,7},{7,6},{8,9},{9,8},{10,11... | collective-permute-start | bytes 393224 | tf_op jit(solution)/shard_map/ppermute | solution.py:37
  48.1 6.2 %collective-permute-start.20 = (f32[64,256]{1,0:T(8,128)S(1)}, f32[64,256]{1,0:T(8,128)S(1)}, u32[]{:S(2)}, u32[]{:S(2)}) collective-permute-start(f32[64,256]{1,0:T(8,128)S(1)} %shard_map.102.refs_0_), channel_id=1, source_target_pairs={{0,1},{1,0},{2,3},{3,2},{4,5},{5,4},{6,7},{7,6},{8,9},{9,8},{10,11... | collective-permute-start | bytes 196616 | tf_op jit(solution)/shard_map/ppermute | solution.py:33
  48.1 6.1 %collective-permute-start.19 = (f32[64,256]{1,0:T(8,128)S(1)}, f32[64,256]{1,0:T(8,128)S(1)}, u32[]{:S(2)}, u32[]{:S(2)}) collective-permute-start(f32[64,256]{1,0:T(8,128)S(1)} %shard_map.102.refs_0_), channel_id=1, source_target_pairs={{0,2},{1,3},{2,0},{3,1},{4,6},{5,7},{6,4},{7,5},{8,10},{9,11},{10,... | collective-permute-start | bytes 196616 | tf_op jit(solution)/shard_map/ppermute | solution.py:33
  49.1 5.1 %collective-permute-start.18 = (f32[64,256]{1,0:T(8,128)S(1)}, f32[64,256]{1,0:T(8,128)S(1)}, u32[]{:S(2)}, u32[]{:S(2)}) collective-permute-start(f32[64,256]{1,0:T(8,128)S(1)} %shard_map.102.refs_0_), channel_id=1, source_target_pairs={{0,3},{1,2},{2,1},{3,0},{4,7},{5,6},{6,5},{7,4},{8,11},{9,10},{10,... | collective-permute-start | bytes 196616 | tf_op jit(solution)/shard_map/ppermute | solution.py:33
  (8 other events, 18.1 us)

commit v2 on v1

v2 whole, which is shorter than its diff:
```python
import functools
import jax
import jax.numpy as jnp
from jax import lax
from jax.experimental import pallas as pl
from jax.experimental.pallas import tpu as pltpu
from jax.sharding import PartitionSpec as P

F32 = jnp.float32
BF16 = jnp.bfloat16
VMEM = pl.BlockSpec(memory_space=pltpu.VMEM)
SMEM = pl.BlockSpec(memory_space=pltpu.SMEM)
HBM = pl.BlockSpec(memory_space=pltpu.HBM)
PARAMS = pltpu.CompilerParams(vmem_limit_bytes=48 * 1024 * 1024)


def partner(i, k, n):
    if n & (n - 1) == 0:
        return i ^ k
    return (i + k) % n


def back_partner(i, k, n):
    if n & (n - 1) == 0:
        return i ^ k
    return (i + n - k) % n


def exchange_order(n):
    return sorted(range(1, n), key=lambda k: -k)


def send(x, axis, k, n):
    return lax.ppermute(x, axis, [(i, partner(i, k, n)) for i in range(n)])


def send_back(x, axis, k, n):
    return lax.ppermute(x, axis, [(i, back_partner(i, k, n)) for i in range(n)])


def split(x):
    hi = x.astype(BF16)
    return hi, (x - hi.astype(F32)).astype(BF16)


def mm(a, b, dims=((1,), (0,))):
    return lax.dot_general(a, b, (dims, ((), ())), preferred_element_type=F32)


def mm3(a, b, dims=((1,), (0,))):
    ah, al = a
    bh, bl = b
    return mm(ah, bh, dims) + (mm(ah, bl, dims) + mm(al, bh, dims))


def call(kernel, out_shape, flops, nbytes, in_specs, out_specs, scratch=()):
    return pl.pallas_call(
        kernel,
        out_shape=out_shape,
        in_specs=in_specs,
        out_specs=out_specs,
        scratch_shapes=list(scratch),
        compiler_params=PARAMS,
        cost_estimate=pl.CostEstimate(flops=flops, bytes_accessed=nbytes, transcendentals=0),
    )


def fetch(pairs, sems):
    copies = [pltpu.make_async_copy(src, dst, sems.at[i]) for i, (src, dst) in enumerate(pairs)]
    for copy in copies:
        copy.start()
    return copies


def pack_rows(out_ref, targets_ref, peer, rows_ref, side):
    for j in range(targets_ref.shape[1]):
        target = targets_ref[0, j, peer]
        rows = rows_ref[pl.ds(pl.multiple_of(jnp.maximum(target, 0) * side, side), side), :]
        out_ref[j * side : (j + 1) * side, :] = jnp.where(target >= 0, rows, 0.0).astype(BF16)


def pack_kernel(ns, nd, side, inner_hbm, outer_hbm, features_hbm, *refs):
    out_refs, (inner_ref, outer_ref, rows_ref, sems) = refs[:-4], refs[-4:]
    half = rows_ref.shape[0] // 2
    copies = fetch(
        [
            (inner_hbm, inner_ref),
            (outer_hbm, outer_ref),
            (features_hbm.at[:half], rows_ref.at[:half]),
            (features_hbm.at[half:], rows_ref.at[half:]),
        ],
        sems,
    )
    for copy in copies:
        copy.wait()
    s = lax.axis_index("shard")
    p = lax.axis_index("dom")
    plan = [(inner_ref, partner(s, k, ns)) for k in exchange_order(ns)]
    plan += [(outer_ref, partner(p, k, nd)) for k in exchange_order(nd)[:-1]]
    for out_ref, (targets_ref, peer) in zip(out_refs, plan):
        pack_rows(out_ref, targets_ref, peer, rows_ref, side)


def slot_codes(row_blocks, ns, nd, inner_cap, outer_cap):
    s = lax.axis_index("shard")
    p = lax.axis_index("dom")
    codes = []
    for k in exchange_order(ns):
        for j in range(inner_cap):
            codes.append(row_blocks + back_partner(s, k, ns) * inner_cap + j)
    for k in exchange_order(nd):
        for j in range(outer_cap):
            codes.append(row_blocks + ns * inner_cap + back_partner(p, k, nd) * outer_cap + j)
    return codes


def local_kernel(
    dims, list_hbm, outer_hbm, features_hbm, weight_hbm, values_hbm,
    near_ref, base_ref, local_ref, scale_ref, picked_ref, turned_ref, place_ref,
    list_ref, outer_ref, features_ref, weight_ref, values_ref, sources_ref, inverse_ref, sems,
):
    row_blocks, fanout, side, width, ns, nd, inner_cap, outer_cap = dims
    pairs = [
        (list_hbm, list_ref), (outer_hbm, outer_ref), (features_hbm, features_ref), (weight_hbm, weight_ref)
    ]
    pairs += [(values_hbm.at[r], values_ref.at[r]) for r in range(row_blocks)]
    copies = fetch(pairs, sems)
    for copy in copies[:4]:
        copy.wait()
    pack_rows(near_ref, outer_ref, partner(lax.axis_index("dom"), exchange_order(nd)[-1], nd), features_ref, side)
    codes = row_blocks + ns * inner_cap + nd * outer_cap
    for c in range(codes):
        inverse_ref[c] = 0
    for n in range(row_blocks * fanout):
        inverse_ref[list_ref[n // fanout, n % fanout]] = n
    fh, fl = split(features_ref[...])
    projected = mm3((fh, fl), split(weight_ref[...]))
    sources_ref[: row_blocks * side, :width] = projected.astype(BF16)
    sources_ref[: row_blocks * side, width : 2 * width] = fh
    sources_ref[: row_blocks * side, 2 * width :] = fl
    sources_ref[row_blocks * side :, :] = jnp.zeros((side, 3 * width), BF16)
    for copy in copies[4:]:
        copy.wait()
    for r in range(row_blocks):
        rows = slice(r * side, (r + 1) * side)
        squares = jnp.zeros((side, side), F32)
        for k in range(fanout):
            block = values_ref[r, k].astype(F32)
            squares = squares + block * block
        scale = lax.rsqrt(1.0 + jnp.sum(squares, axis=1, keepdims=True))
        scale_ref[rows, :] = jnp.broadcast_to(scale, (side, width))
        total = jnp.zeros((side, 3 * width), F32)
        for k in range(0, fanout, 2):
            blocks = jnp.concatenate([values_ref[r, k], values_ref[r, k + 1]], axis=1)
            picks = []
            for kk in (k, k + 1):
                at = pl.multiple_of(jnp.minimum(list_ref[r, kk], row_blocks) * side, side)
                picks.append(sources_ref[pl.ds(at, side), :])
            total = total + mm(blocks, jnp.concatenate(picks, axis=0))
        base_ref[rows, :] = projected[rows, :] + total[:, :width]
        local_ref[rows, :] = total[:, width : 2 * width] + total[:, 2 * width :]
    for i, code in enumerate(slot_codes(row_blocks, ns, nd, inner_cap, outer_cap)):
        n = inverse_ref[code]
        r = n // fanout
        place_ref[i] = r
        block = values_ref[r, n % fanout]
        picked_ref[i] = block
        turned_ref[i] = block.T


def middle_kernel(dims, place_ref, *refs):
    row_blocks, fanout, side, width, ns, nd, inner_cap, outer_cap = dims
    n_in = (ns - 1) + (nd - 1)
    arrived = refs[:n_in]
    base_ref, scale_ref, picked_ref, turned_ref, weight_ref, cotangent_ref = refs[n_in : n_in + 6]
    act_ref, scaled_ref, half_ref, total_ref = refs[n_in + 6 : n_in + 10]
    leaving = refs[n_in + 10 :]
    total_ref[...] = jnp.zeros_like(total_ref)
    i = 0
    for ref in arrived:
        for j in range(ref.shape[0] // side):
            term = mm(picked_ref[i], ref[j * side : (j + 1) * side, :])
            rows = pl.ds(pl.multiple_of(place_ref[i] * side, side), side)
            total_ref[rows, :] += term
            i += 1
    weight = split(weight_ref[...])
    for r in range(row_blocks):
        rows = slice(r * side, (r + 1) * side)
        scale = scale_ref[rows, :]
        mixed = (base_ref[rows, :] + mm3(split(total_ref[rows, :]), weight)) * scale
        gate = jax.nn.sigmoid(mixed)
        act_ref[rows, :] = mixed * gate
        scaled = cotangent_ref[rows, :] * gate * (1.0 + mixed * (1.0 - gate)) * scale
        scaled_ref[rows, :] = scaled
        half_ref[rows, :] = scaled.astype(BF16)
    i = 0
    for ref in leaving:
        for j in range(inner_cap):
            rows = pl.ds(pl.multiple_of(place_ref[i] * side, side), side)
            ref[j * side : (j + 1) * side, :] = mm(turned_ref[i], half_ref[rows, :]).astype(BF16)
            i += 1


def weight_kernel(
    dims, first, place_ref, features_ref, local_ref, total_ref, scaled_ref, half_ref, turned_ref, own_ref, *refs
):
    row_blocks, fanout, side, width, ns, nd, inner_cap, outer_cap = dims
    leaving, term_ref = refs[:-1], refs[-1]
    p = lax.axis_index("dom")
    down = ((0,), (0,))
    ah, al = split(local_ref[...] + total_ref[...])
    half = half_ref[...]
    term = mm3(split(features_ref[...]), split(scaled_ref[...]), down)
    term_ref[...] = term + (mm(ah, half, down) + mm(al, half, down))
    piece = own_ref.shape[0]
    own_ref[...] = term_ref[pl.ds(pl.multiple_of(p * piece, 8), piece), :]
    i = first
    for ref, k in zip(leaving, exchange_order(nd)):
        for j in range(outer_cap):
            rows = pl.ds(pl.multiple_of(place_ref[i] * side, side), side)
            ref[j * side : (j + 1) * side, :] = mm(turned_ref[i], half_ref[rows, :]).astype(BF16)
            i += 1
        at = pl.multiple_of(back_partner(p, k, nd) * piece, 8)
        hi, lo = split(term_ref[pl.ds(at, piece), :])
        ref[outer_cap * side : outer_cap * side + piece, :] = hi
        ref[outer_cap * side + piece :, :] = lo


def spread_kernel(dims, list_hbm, values_hbm, scaled_ref, half_ref, out_ref, list_ref, values_ref, sums_ref, sems):
    row_blocks, fanout, side, width = dims
    copies = fetch(
        [(list_hbm, list_ref)] + [(values_hbm.at[r], values_ref.at[r]) for r in range(row_blocks)], sems
    )
    sums_ref[: row_blocks * side, :] = scaled_ref[...]
    copies[0].wait()
    for r in range(row_blocks):
        copies[r + 1].wait()
        half = half_ref[r * side : (r + 1) * side, :]
        for k in range(fanout):
            at = pl.multiple_of(jnp.minimum(list_ref[r, k], row_blocks) * side, side)
            sums_ref[pl.ds(at, side), :] += mm(values_ref[r, k], half, ((0,), (0,)))
    out_ref[...] = sums_ref[: row_blocks * side, :]


def tree_sum(terms):
    while len(terms) > 1:
        terms = [sum(terms[i : i + 2][1:], terms[i]) for i in range(0, len(terms), 2)]
    return terms[0]


def add_rows(sums_ref, ref, targets_ref, peer, side):
    for j in range(targets_ref.shape[1]):
        target = targets_ref[0, j, peer]
        rows = pl.ds(pl.multiple_of(jnp.maximum(target, 0) * side, side), side)
        term = ref[j * side : (j + 1) * side, :].astype(F32)
        sums_ref[rows, :] += jnp.where(target >= 0, term, 0.0)


def dom_sum_kernel(nd, side, targets_ref, part_ref, own_ref, *refs):
    arrived, (sums_ref, piece_ref) = refs[:-2], refs[-2:]
    piece = own_ref.shape[0]
    start = targets_ref.shape[1] * side
    terms = [own_ref[...]]
    for ref in reversed(arrived):
        hi = ref[start : start + piece, :].astype(F32)
        terms.append(hi + ref[start + piece :, :].astype(F32))
    piece_ref[...] = tree_sum(terms).astype(BF16)
    sums_ref[...] = part_ref[...]
    p = lax.axis_index("dom")
    for ref, k in zip(arrived, exchange_order(nd)):
        add_rows(sums_ref, ref, targets_ref, partner(p, k, nd), side)


def shard_sum_kernel(ns, side, targets_ref, part_ref, own_ref, *refs):
    arrived, pieces, (sums_ref, out_ref) = refs[: ns - 2], refs[ns - 2 : -2], refs[-2:]
    out_ref[...] = tree_sum([ref[...].astype(F32) for ref in (own_ref, *reversed(pieces))])
    sums_ref[...] = part_ref[...]
    s = lax.axis_index("shard")
    for ref, k in zip(arrived, exchange_order(ns)):
        add_rows(sums_ref, ref, targets_ref, partner(s, k, ns), side)


def finish_kernel(ns, side, targets_ref, part_ref, weight_ref, near_ref, out_ref, sums_ref):
    sums_ref[...] = part_ref[...]
    peer = partner(lax.axis_index("shard"), exchange_order(ns)[-1], ns)
    add_rows(sums_ref, near_ref, targets_ref, peer, side)
    out_ref[...] = mm3(split(sums_ref[...]), split(weight_ref[...]), ((1,), (1,)))


def place_kernel(nd, *refs):
    p = lax.axis_index("dom")
    out_ref = refs[-1]
    piece = refs[0].shape[0]
    for ref, k in zip(refs[:-1], [0] + exchange_order(nd)):
        at = pl.multiple_of(back_partner(p, k, nd) * piece, 8)
        out_ref[pl.ds(at, piece), :] = ref[...]


def on_device(features, weight, cotangent, block_values, block_list, send_inner, send_outer):
    keep = lambda x: pltpu.with_memory_space_constraint(x, pltpu.HBM)
    node_count, width = features.shape
    row_blocks, fanout, side, _ = block_values.shape
    ns = lax.axis_size("shard")
    nd = lax.axis_size("dom")
    inner_cap = send_inner.shape[2]
    outer_cap = send_outer.shape[2]
    slots = (ns - 1) * inner_cap + (nd - 1) * outer_cap
    dims = (row_blocks, fanout, side, width, ns, nd, inner_cap, outer_cap)
    shape = jax.ShapeDtypeStruct
    rows_f32 = shape((node_count, width), F32)
    rows_f16 = shape((node_count, width), BF16)
    packed_inner = [shape((inner_cap * side, width), BF16)] * (ns - 1)
    packed_outer = [shape((outer_cap * side, width), BF16)] * (nd - 1)
    nbytes = node_count * width * 4

    inner_targets = jnp.swapaxes(send_inner, 1, 2)
    outer_targets = jnp.swapaxes(send_outer, 1, 2)
    inner_table = pltpu.SMEM(inner_targets.shape, jnp.int32)
    outer_table = pltpu.SMEM(outer_targets.shape, jnp.int32)
    list_table = pltpu.SMEM(block_list.shape, jnp.int32)
    inner_order, outer_order = exchange_order(ns), exchange_order(nd)

    packed = call(
        functools.partial(pack_kernel, ns, nd, side), packed_inner + packed_outer[:-1], 0, 3 * nbytes,
        [HBM] * 3, [VMEM] * (ns - 1 + nd - 2),
        [inner_table, outer_table, pltpu.VMEM(features.shape, F32), pltpu.SemaphoreType.DMA((4,))],
    )(keep(inner_targets), keep(outer_targets), keep(features))
    inner_in = [send(x, "shard", k, ns) for x, k in zip(packed, inner_order)]
    outer_in = [send(x, "dom", k, nd) for x, k in zip(packed[ns - 1 :], outer_order)]

    near, base, local, scale, picked, turned, place = call(
        functools.partial(local_kernel, dims),
        [
            packed_outer[-1], rows_f32, rows_f32, rows_f32,
            shape((slots, side, side), BF16), shape((slots, side, side), BF16), shape((slots,), jnp.int32),
        ],
        4 * row_blocks * fanout * side * side * width * 3, 12 * nbytes,
        [HBM] * 5, [VMEM] * 6 + [SMEM],
        [
            list_table, outer_table, pltpu.VMEM(features.shape, F32), pltpu.VMEM(weight.shape, F32),
            pltpu.VMEM(block_values.shape, BF16),
            pltpu.VMEM(((row_blocks + 1) * side, 3 * width), BF16),
            pltpu.SMEM((row_blocks + ns * inner_cap + nd * outer_cap,), jnp.int32),
            pltpu.SemaphoreType.DMA((4 + row_blocks,)),
        ],
    )(keep(block_list), keep(outer_targets), keep(features), keep(weight), keep(block_values))
    outer_in.append(send(near, "dom", outer_order[-1], nd))

    n_in = ns - 1 + nd - 1
    outs = call(
        functools.partial(middle_kernel, dims),
        [rows_f32, rows_f32, rows_f16, rows_f32] + packed_inner,
        2 * slots * side * side * width * 2, 8 * nbytes,
        [SMEM] + [VMEM] * (n_in + 6), [VMEM] * (4 + ns - 1),
    )(place, *inner_in, *outer_in, base, scale, picked, turned, weight, cotangent)
    activations, scaled, half, total = outs[:4]
    inner_back = [send_back(x, "shard", k, ns) for x, k in zip(outs[4:], inner_order)]

    piece_rows = width // nd
    start = outer_cap * side
    outs = call(
        functools.partial(weight_kernel, dims, (ns - 1) * inner_cap),
        [shape((piece_rows, width), F32)] + [shape((start + 2 * piece_rows, width), BF16)] * (nd - 1),
        10 * node_count * width * width, 5 * nbytes,
        [SMEM] + [VMEM] * 6, [VMEM] * nd, [pltpu.VMEM((width, width), F32)],
    )(place, features, local, total, scaled, half, turned)
    outer_back = [send_back(x, "dom", k, nd) for x, k in zip(outs[1:], outer_order)]

    part = call(
        functools.partial(spread_kernel, dims[:4]), rows_f32,
        2 * row_blocks * fanout * side * side * width, 8 * nbytes,
        [HBM, HBM, VMEM, VMEM], VMEM,
        [
            list_table, pltpu.VMEM(block_values.shape, BF16),
            pltpu.VMEM(((row_blocks + 1) * side, width), F32), pltpu.SemaphoreType.DMA((1 + row_blocks,)),
        ],
    )(keep(block_list), keep(block_values), scaled, half)
    part, piece = call(
        functools.partial(dom_sum_kernel, nd, side), [rows_f32, shape((piece_rows, width), BF16)],
        0, 4 * nbytes, [SMEM] + [VMEM] * (nd + 1), [VMEM] * 2,
    )(outer_targets, part, outs[0], *outer_back)
    pieces = [send(piece, "shard", k, ns) for k in inner_order]
    part, weight_sum = call(
        functools.partial(shard_sum_kernel, ns, side), [rows_f32, shape((piece_rows, width), F32)],
        0, 4 * nbytes, [SMEM] + [VMEM] * (2 * ns - 1), [VMEM] * 2,
    )(inner_targets, part, piece, *inner_back[:-1], *pieces)
    gathered = [weight_sum] + [send(weight_sum, "dom", k, nd) for k in outer_order]
    grad_weight = call(
        functools.partial(place_kernel, nd), shape((width, width), F32), 0, nbytes, [VMEM] * nd, VMEM
    )(*gathered)
    grad_features = call(
        functools.partial(finish_kernel, ns, side), rows_f32, 6 * node_count * width * width, 4 * nbytes,
        [SMEM] + [VMEM] * 3, VMEM, [pltpu.VMEM((node_count, width), F32)],
    )(inner_targets, part, weight, inner_back[-1])
    return (activations, grad_features, grad_weight)


def solution(mesh):
    rows = ("copies", "shard", "dom")
    return jax.shard_map(
        on_device,
        mesh=mesh,
        in_specs=(
            P(rows, None),
            P(),
            P(rows, None),
            P(rows, None, None, None),
            P(rows, None),
            P(rows, None, None),
            P(rows, None, None),
        ),
        out_specs=(P(rows, None), P(rows, None), P("copies", None)),
        check_vma=False,
    )
```

time: 55.3 us -> 49.7 us (0.90)
  local copies, waits for them, and re-layouts: 7.9 us -> 0.02 us
  starting transfers between devices: 22 us -> 18.5 us
  Pallas kernels: 12.9 us -> 15.8 us
  waiting for transfers between devices: 11.4 us -> 14.3 us
    unnamed x24 -> x10, local copies, waits for them, and re-layouts: 7.9 us -> 0.02 us
    pallas_call x7 -> x6, Pallas kernels: 7.6 us -> 9.87 us  [the longest x1 4.3 us: on_device(): call(functools.partial(local_kernel, dims), [packed_outer[-1], rows_f32,...]
    ppermute x15 -> x12, waiting for transfers between devices: 8.18 us -> 10.3 us  [send(): return lax.ppermute(x, axis, [(i, partner(i, k, n)) for i in range(n)])]
    ppermute x15 -> x12, starting transfers between devices: 15.9 us -> 14.1 us  [send(): return lax.ppermute(x, axis, [(i, partner(i, k, n)) for i in range(n)])]
    ppermute x6, starting transfers between devices: 6.06 us -> 4.41 us  [send_back(): return lax.ppermute(x, axis, [(i, back_partner(i, k, n)) for i in range(n)])]
    ppermute x6, waiting for transfers between devices: 3.2 us -> 4.05 us  [send_back(): return lax.ppermute(x, axis, [(i, back_partner(i, k, n)) for i in range(n)])]
    pallas_call x1, Pallas kernels: 2.27 us -> 3.02 us  [on_device(): call(functools.partial(spread_kernel, dims[:4]), rows_f32, 2 * row_blocks...]
  transfers between devices with their start and end apart: 21 -> 18, of which waited for: 6 -> 8; matrix products, arithmetic and copies ran while one was open for 1% -> 0% of each run, Pallas kernels for 16% -> 21%
where the time goes in v2:
time: 49.7 us; the launch traced here: 49.5 us
  starting transfers between devices  18.5 us (37%)
  Pallas kernels  15.8 us (32%)
  waiting for transfers between devices  14.3 us (29%)
  between operations  0.76 us (2%)
    ppermute x12, starting transfers between devices, send(): return lax.ppermute(x, axis, [(i, partner(i, k, n)) for i in range(n)])  14.1 us
    ppermute x12, waiting for transfers between devices, send(): return lax.ppermute(x, axis, [(i, partner(i, k, n)) for i in range(n)])  10.3 us
    ppermute x6, starting transfers between devices, send_back(): return lax.ppermute(x, axis, [(i, back_partner(i, k, n)) for i in range(n)])  4.41 us
    pallas_call x1, Pallas kernels, on_device(): call(functools.partial(local_kernel, dims), [packed_outer[-1], rows_f32,...  4.3 us
    ppermute x6, waiting for transfers between devices, send_back(): return lax.ppermute(x, axis, [(i, back_partner(i, k, n)) for i in range(n)])  4.05 us
    pallas_call x1, Pallas kernels, on_device(): call(functools.partial(spread_kernel, dims[:4]), rows_f32, 2 * row_blocks...  3.02 us
    pallas_call x1, Pallas kernels, on_device(): call(functools.partial(middle_kernel, dims), [rows_f32, rows_f32, rows_f1...  2.19 us
    pallas_call x1, Pallas kernels, on_device(): call(functools.partial(finish_kernel, ns, side), rows_f32, 6 * node_count...  1.78 us
  transfers between devices with their start and end apart: 18, of which 8 were waited for; matrix products, arithmetic and copies ran while one was open for 0% of the time, Pallas kernels for 21%

profile of v2, /device:TPU:0, one launch (start us, length us, event | category | flops | bytes accessed | tf_op | source)
XLA Modules:
  0.0 49.5 jit_solution(17893904429092783556)
XLA Ops:
  0.6 1.2 %shard_map.95 = (bf16[256,256]{1,0:T(8,128)(2,1)S(1)}, bf16[256,256]{1,0:T(8,128)(2,1)S(1)}, bf16[256,256]{1,0:T(8,128)(2,1)S(1)}, bf16[256,256]{1,0:T(8,128)(2,1)S(1)}, bf16[256,256]{1,0:T(8,128)(2,1)S(1)}) custom-call(s32[1,2,4]{2,1,0:T(2,128)} %bitcast.2, s32[1,2,4]{2,1,0:T(2,128)} %bitcast.5, f32[512,256]{1,0:T(8,128)} %features_ref.1), custom_call_target="tpu_custom_call" | custom-call | bytes 1572864 | tf_op jit(solution)/shard_map/pallas_call | solution.py:323
  1.8 5.1 %collective-permute-start = (bf16[256,256]{1,0:T(8,128)(2,1)S(1)}, bf16[256,256]{1,0:T(8,128)(2,1)S(1)}, u32[]{:S(2)}, u32[]{:S(2)}) collective-permute-start(bf16[256,256]{1,0:T(8,128)(2,1)S(1)} %get-tuple-element.31), channel_id=1, source_target_pairs={{0,12},{4,8},{8,4},{12,0},{1,13},{5,9},{9,5},{13,1},{2,14},{6,10},... | collective-permute-start | bytes 393224 | tf_op jit(solution)/shard_map/ppermute | solution.py:34
  7.0 0.6 %collective-permute-start.2 = (bf16[256,256]{1,0:T(8,128)(2,1)S(1)}, bf16[256,256]{1,0:T(8,128)(2,1)S(1)}, u32[]{:S(2)}, u32[]{:S(2)}) collective-permute-start(bf16[256,256]{1,0:T(8,128)(2,1)S(1)} %get-tuple-element.33), channel_id=1, source_target_pairs={{0,4},{4,0},{8,12},{12,8},{1,5},{5,1},{9,13},{13,9},{2,6},{6,2},{1... | collective-permute-start | bytes 393224 | tf_op jit(solution)/shard_map/ppermute | solution.py:34
  8.0 1.3 %collective-permute-start.4 = (bf16[256,256]{1,0:T(8,128)(2,1)S(1)}, bf16[256,256]{1,0:T(8,128)(2,1)S(1)}, u32[]{:S(2)}, u32[]{:S(2)}) collective-permute-start(bf16[256,256]{1,0:T(8,128)(2,1)S(1)} %get-tuple-element.35), channel_id=1, source_target_pairs={{0,2},{1,3},{2,0},{3,1},{4,6},{5,7},{6,4},{7,5},{8,10},{9,11},{10,... | collective-permute-start | bytes 393224 | tf_op jit(solution)/shard_map/ppermute | solution.py:34
  9.3 4.3 %shard_map.94 = (bf16[256,256]{1,0:T(8,128)(2,1)S(1)}, f32[512,256]{1,0:T(8,128)S(1)}, f32[512,256]{1,0:T(8,128)S(1)}, f32[512,256]{1,0:T(8,128)S(1)}, bf16[12,1...) custom-call(s32[4,16]{1,0:T(4,128)} %list_hbm.3, s32[1,2,4]{2,1,0:T(2,128)} %bitcast.6, ...), custom_call_target="tpu_custom_call" | custom-call | flops 3221225472 | bytes 6291456 | tf_op jit(solution)/shard_map/pallas_call | solution.py:331
  13.9 4.1 %collective-permute-done.1.refs_1_ = bf16[256,256]{1,0:T(8,128)(2,1)S(1)} collective-permute-done((bf16[256,256]{1,0:T(8,128)(2,1)S(1)}, bf16[256,256]{1,0:T(8,128)(2,1)S(1)}, u32[]{:S(2)}, u32[]{:S(2)}) %collective-permute-start.1) | collective-permute-done | bytes 131104 | tf_op jit(solution)/shard_map/ppermute | solution.py:34
  18.1 2.2 %shard_map.96 = (f32[512,256]{1,0:T(8,128)}, f32[512,256]{1,0:T(8,128)S(1)}, bf16[512,256]{1,0:T(8,128)(2,1)S(1)}, f32[512,256]{1,0:T(8,128)S(1)}, bf16[256,256]...) custom-call(s32[12]{0:T(128)S(1)} %get-tuple-element.30.place_ref, ...), custom_call_target="tpu_custom_call" | custom-call | flops 201326592 | bytes 4194304 | tf_op jit(solution)/shard_map/pallas_call | solution.py:350
  20.3 1.2 %shard_map.98 = (f32[64,256]{1,0:T(8,128)S(1)}, bf16[384,256]{1,0:T(8,128)(2,1)S(1)}, bf16[384,256]{1,0:T(8,128)(2,1)S(1)}, bf16[384,256]{1,0:T(8,128)(2,1)S(1)}) custom-call(s32[12]{0:T(128)S(1)} %get-tuple-element.30.place_ref, f32[512,256]{1,0:T(8,128)S(1)} %copy-done, f32[512,256]{1,0:T(8,128)S(1)} %get-tuple-element.44.local_ref, ...), custom_call_target="tpu_custom_call" | custom-call | flops 335544320 | bytes 2621440 | tf_op jit(solution)/shard_map/pallas_call | solution.py:361
  21.8 1.3 %collective-permute-start.7 = (bf16[384,256]{1,0:T(8,128)(2,1)S(1)}, bf16[384,256]{1,0:T(8,128)(2,1)S(1)}, u32[]{:S(2)}, u32[]{:S(2)}) collective-permute-start(bf16[384,256]{1,0:T(8,128)(2,1)S(1)} %get-tuple-element.48), channel_id=1, source_target_pairs={{0,2},{1,3},{2,0},{3,1},{4,6},{5,7},{6,4},{7,5},{8,10},{9,11},{10,... | collective-permute-start | bytes 589832 | tf_op jit(solution)/shard_map/ppermute | solution.py:38
  23.5 2.5 %collective-permute-start.9 = (bf16[256,256]{1,0:T(8,128)(2,1)S(1)}, bf16[256,256]{1,0:T(8,128)(2,1)S(1)}, u32[]{:S(2)}, u32[]{:S(2)}) collective-permute-start(bf16[256,256]{1,0:T(8,128)(2,1)S(1)} %get-tuple-element.52), channel_id=1, source_target_pairs={{0,12},{4,8},{8,4},{12,0},{1,13},{5,9},{9,5},{13,1},{2,14},{6,10},... | collective-permute-start | bytes 393224 | tf_op jit(solution)/shard_map/ppermute | solution.py:38
  25.9 2.8 %collective-permute-done.6.refs_0_ = bf16[384,256]{1,0:T(8,128)(2,1)S(1)} collective-permute-done((bf16[384,256]{1,0:T(8,128)(2,1)S(1)}, bf16[384,256]{1,0:T(8,128)(2,1)S(1)}, u32[]{:S(2)}, u32[]{:S(2)}) %collective-permute-start.6) | collective-permute-done | bytes 196640 | tf_op jit(solution)/shard_map/ppermute | solution.py:38
  28.8 3.0 %shard_map.97.part_ref = f32[512,256]{1,0:T(8,128)S(1)} custom-call(s32[4,16]{1,0:T(4,128)} %list_hbm.3, bf16[4,16,128,128]{3,2,1,0:T(8,128)(2,1)} %values_hbm.3, f32[512,256]{1,0:T(8,128)S(1)} %get-tuple-element.42.scaled_ref, bf16[512,256]{1,0:T(8,128)(2,1)S(1)} %get-tuple-element.43.half_ref), custom_call_target="tpu_custom_call" | custom-call | flops 536870912 | bytes 4194304 | tf_op jit(solution)/shard_map/pallas_call | solution.py:369
  31.8 1.2 %collective-permute-done.7.refs_1_ = bf16[384,256]{1,0:T(8,128)(2,1)S(1)} collective-permute-done((bf16[384,256]{1,0:T(8,128)(2,1)S(1)}, bf16[384,256]{1,0:T(8,128)(2,1)S(1)}, u32[]{:S(2)}, u32[]{:S(2)}) %collective-permute-start.7) | collective-permute-done | bytes 196640 | tf_op jit(solution)/shard_map/ppermute | solution.py:38
  33.0 0.7 %shard_map.99 = (f32[512,256]{1,0:T(8,128)S(1)}, bf16[64,256]{1,0:T(8,128)(2,1)S(1)}) custom-call(s32[1,2,4]{2,1,0:T(2,128)S(1)} %bitcast.7, f32[512,256]{1,0:T(8,128)S(1)} %shard_map.97.part_ref, f32[64,256]{1,0:T(8,128)S(1)} %get-tuple-element.46.own_ref, bf16[384,256]{1,0:T(8,128)(2,1)S(1)} %collective-permute-done.6.refs_0_, ...), custom_call_target="tpu_custom_call" | custom-call | bytes 2097152 | tf_op jit(solution)/shard_map/pallas_call | solution.py:378
  33.7 0.9 %collective-permute-start.13 = (bf16[64,256]{1,0:T(8,128)(2,1)S(1)}, bf16[64,256]{1,0:T(8,128)(2,1)S(1)}, u32[]{:S(2)}, u32[]{:S(2)}) collective-permute-start(bf16[64,256]{1,0:T(8,128)(2,1)S(1)} %get-tuple-element.51.own_ref), channel_id=1, source_target_pairs={{0,4},{4,0},{8,12},{12,8},{1,5},{5,1},{9,13},{13,9},{2,6},{6,2},{1... | collective-permute-start | bytes 98312 | tf_op jit(solution)/shard_map/ppermute | solution.py:34
  34.6 2.2 %collective-permute-start.12 = (bf16[64,256]{1,0:T(8,128)(2,1)S(1)}, bf16[64,256]{1,0:T(8,128)(2,1)S(1)}, u32[]{:S(2)}, u32[]{:S(2)}) collective-permute-start(bf16[64,256]{1,0:T(8,128)(2,1)S(1)} %get-tuple-element.51.own_ref), channel_id=1, source_target_pairs={{0,8},{4,12},{8,0},{12,4},{1,9},{5,13},{9,1},{13,5},{2,10},{6,14},... | collective-permute-start | bytes 98312 | tf_op jit(solution)/shard_map/ppermute | solution.py:34
  36.8 1.3 %collective-permute-start.11 = (bf16[64,256]{1,0:T(8,128)(2,1)S(1)}, bf16[64,256]{1,0:T(8,128)(2,1)S(1)}, u32[]{:S(2)}, u32[]{:S(2)}) collective-permute-start(bf16[64,256]{1,0:T(8,128)(2,1)S(1)} %get-tuple-element.51.own_ref), channel_id=1, source_target_pairs={{0,12},{4,8},{8,4},{12,0},{1,13},{5,9},{9,5},{13,1},{2,14},{6,10},... | collective-permute-start | bytes 98312 | tf_op jit(solution)/shard_map/ppermute | solution.py:34
  38.3 1.5 %collective-permute-done.12.refs_3_ = bf16[64,256]{1,0:T(8,128)(2,1)S(1)} collective-permute-done((bf16[64,256]{1,0:T(8,128)(2,1)S(1)}, bf16[64,256]{1,0:T(8,128)(2,1)S(1)}, u32[]{:S(2)}, u32[]{:S(2)}) %collective-permute-start.12) | collective-permute-done | bytes 32800 | tf_op jit(solution)/shard_map/ppermute | solution.py:34
  39.8 2.7 %collective-permute-done.11.refs_2_ = bf16[64,256]{1,0:T(8,128)(2,1)S(1)} collective-permute-done((bf16[64,256]{1,0:T(8,128)(2,1)S(1)}, bf16[64,256]{1,0:T(8,128)(2,1)S(1)}, u32[]{:S(2)}, u32[]{:S(2)}) %collective-permute-start.11) | collective-permute-done | bytes 32800 | tf_op jit(solution)/shard_map/ppermute | solution.py:34
  42.5 0.7 %shard_map.100 = (f32[512,256]{1,0:T(8,128)S(1)}, f32[64,256]{1,0:T(8,128)S(1)}) custom-call(s32[1,2,4]{2,1,0:T(2,128)S(1)} %bitcast.3, f32[512,256]{1,0:T(8,128)S(1)} %get-tuple-element.50.part_ref, bf16[64,256]{1,0:T(8,128)(2,1)S(1)} %get-tuple-element.51.own_ref, bf16[256,256]{1,0:T(8,128)(2,1)S(1)} %collective-permute-done.9.refs_0_, ...), custom_call_target="tpu_custom_call" | custom-call | bytes 2097152 | tf_op jit(solution)/shard_map/pallas_call | solution.py:383
  43.7 1.4 %collective-permute-start.15 = (f32[64,256]{1,0:T(8,128)S(1)}, f32[64,256]{1,0:T(8,128)S(1)}, u32[]{:S(2)}, u32[]{:S(2)}) collective-permute-start(f32[64,256]{1,0:T(8,128)S(1)} %get-tuple-element.56.refs_0_), channel_id=1, source_target_pairs={{0,3},{1,2},{2,1},{3,0},{4,7},{5,6},{6,5},{7,4},{8,11},{9,10},{10,... | collective-permute-start | bytes 196616 | tf_op jit(solution)/shard_map/ppermute | solution.py:34
  45.1 1.8 %shard_map.101 = f32[512,256]{1,0:T(8,128)} custom-call(s32[1,2,4]{2,1,0:T(2,128)S(1)} %bitcast.4, f32[512,256]{1,0:T(8,128)S(1)} %get-tuple-element.54.part_ref, f32[256,256]{1,0:T(8,128)S(1)} %copy-done.1, bf16[256,256]{1,0:T(8,128)(2,1)S(1)} %collective-permute-done.14.near_ref), custom_call_target="tpu_custom_call" | custom-call | flops 201326592 | bytes 2097152 | tf_op jit(solution)/shard_map/pallas_call | solution.py:391
  46.9 1.3 %collective-permute-done.16.refs_2_ = f32[64,256]{1,0:T(8,128)S(1)} collective-permute-done((f32[64,256]{1,0:T(8,128)S(1)}, f32[64,256]{1,0:T(8,128)S(1)}, u32[]{:S(2)}, u32[]{:S(2)}) %collective-permute-start.16) | collective-permute-done | bytes 65568 | tf_op jit(solution)/shard_map/ppermute | solution.py:34
  48.7 0.7 %shard_map.102 = f32[256,256]{1,0:T(8,128)} custom-call(f32[64,256]{1,0:T(8,128)S(1)} %get-tuple-element.56.refs_0_, f32[64,256]{1,0:T(8,128)S(1)} %collective-permute-done.15.refs_1_, f32[64,256]{1,0:T(8,128)S(1)} %collective-permute-done.16.refs_2_, f32[64,256]{1,0:T(8,128)S(1)} %collective-permute-done.17.refs_3_), custom_call_target="tpu_custom_call" | custom-call | bytes 524288 | tf_op jit(solution)/shard_map/pallas_call | solution.py:388
  (31 shorter events, 2.5 us)
Async XLA Ops:
  1.8 11.8 %collective-permute-start = (bf16[256,256]{1,0:T(8,128)(2,1)S(1)}, bf16[256,256]{1,0:T(8,128)(2,1)S(1)}, u32[]{:S(2)}, u32[]{:S(2)}) collective-permute-start(bf16[256,256]{1,0:T(8,128)(2,1)S(1)} %get-tuple-element.31), channel_id=1, source_target_pairs={{0,12},{4,8},{8,4},{12,0},{1,13},{5,9},{9,5},{13,1},{2,14},{6,10},... | collective-permute-start | bytes 393224 | tf_op jit(solution)/shard_map/ppermute | solution.py:34
  7.0 11.1 %collective-permute-start.1 = (bf16[256,256]{1,0:T(8,128)(2,1)S(1)}, bf16[256,256]{1,0:T(8,128)(2,1)S(1)}, u32[]{:S(2)}, u32[]{:S(2)}) collective-permute-start(bf16[256,256]{1,0:T(8,128)(2,1)S(1)} %get-tuple-element.32), channel_id=1, source_target_pairs={{0,8},{4,12},{8,0},{12,4},{1,9},{5,13},{9,1},{13,5},{2,10},{6,14},... | collective-permute-start | bytes 393224 | tf_op jit(solution)/shard_map/ppermute | solution.py:34
  7.0 11.1 %collective-permute-start.2 = (bf16[256,256]{1,0:T(8,128)(2,1)S(1)}, bf16[256,256]{1,0:T(8,128)(2,1)S(1)}, u32[]{:S(2)}, u32[]{:S(2)}) collective-permute-start(bf16[256,256]{1,0:T(8,128)(2,1)S(1)} %get-tuple-element.33), channel_id=1, source_target_pairs={{0,4},{4,0},{8,12},{12,8},{1,5},{5,1},{9,13},{13,9},{2,6},{6,2},{1... | collective-permute-start | bytes 393224 | tf_op jit(solution)/shard_map/ppermute | solution.py:34
  7.6 10.4 %collective-permute-start.3 = (bf16[256,256]{1,0:T(8,128)(2,1)S(1)}, bf16[256,256]{1,0:T(8,128)(2,1)S(1)}, u32[]{:S(2)}, u32[]{:S(2)}) collective-permute-start(bf16[256,256]{1,0:T(8,128)(2,1)S(1)} %get-tuple-element.34), channel_id=1, source_target_pairs={{0,3},{1,2},{2,1},{3,0},{4,7},{5,6},{6,5},{7,4},{8,11},{9,10},{10,... | collective-permute-start | bytes 393224 | tf_op jit(solution)/shard_map/ppermute | solution.py:34
  8.0 10.1 %copy-start.1 = (f32[256,256]{1,0:T(8,128)S(1)}, f32[256,256]{1,0:T(8,128)}, u32[]{:S(2)}) copy-start(f32[256,256]{1,0:T(8,128)} %weight_ref.1) | copy-start | bytes 786436
  8.0 10.1 %copy-start.2 = (f32[512,256]{1,0:T(8,128)S(1)}, f32[512,256]{1,0:T(8,128)}, u32[]{:S(2)}) copy-start(f32[512,256]{1,0:T(8,128)} %refs_11_.1) | copy-start | bytes 1572868
  8.0 10.1 %collective-permute-start.4 = (bf16[256,256]{1,0:T(8,128)(2,1)S(1)}, bf16[256,256]{1,0:T(8,128)(2,1)S(1)}, u32[]{:S(2)}, u32[]{:S(2)}) collective-permute-start(bf16[256,256]{1,0:T(8,128)(2,1)S(1)} %get-tuple-element.35), channel_id=1, source_target_pairs={{0,2},{1,3},{2,0},{3,1},{4,6},{5,7},{6,4},{7,5},{8,10},{9,11},{10,... | collective-permute-start | bytes 393224 | tf_op jit(solution)/shard_map/ppermute | solution.py:34
  13.6 6.7 %copy-start = (f32[512,256]{1,0:T(8,128)S(1)}, f32[512,256]{1,0:T(8,128)}, u32[]{:S(2)}) copy-start(f32[512,256]{1,0:T(8,128)} %features_ref.1) | copy-start | bytes 1572868
  13.6 4.4 %collective-permute-start.5 = (bf16[256,256]{1,0:T(8,128)(2,1)S(1)}, bf16[256,256]{1,0:T(8,128)(2,1)S(1)}, u32[]{:S(2)}, u32[]{:S(2)}) collective-permute-start(bf16[256,256]{1,0:T(8,128)(2,1)S(1)} %get-tuple-element.36), channel_id=1, source_target_pairs={{0,1},{1,0},{2,3},{3,2},{4,5},{5,4},{6,7},{7,6},{8,9},{9,8},{10,11... | collective-permute-start | bytes 393224 | tf_op jit(solution)/shard_map/ppermute | solution.py:34
  21.5 11.5 %copy-start.4 = (s32[1,4,2]{1,2,0:T(2,128)S(1)}, s32[1,4,2]{1,2,0:T(2,128)}, u32[]{:S(2)}) copy-start(s32[1,4,2]{1,2,0:T(2,128)} %param.13) | copy-start | bytes 100
  21.5 7.2 %collective-permute-start.6 = (bf16[384,256]{1,0:T(8,128)(2,1)S(1)}, bf16[384,256]{1,0:T(8,128)(2,1)S(1)}, u32[]{:S(2)}, u32[]{:S(2)}) collective-permute-start(bf16[384,256]{1,0:T(8,128)(2,1)S(1)} %get-tuple-element.47), channel_id=1, source_target_pairs={{0,3},{1,2},{2,1},{3,0},{4,7},{5,6},{6,5},{7,4},{8,11},{9,10},{10,... | collective-permute-start | bytes 589832 | tf_op jit(solution)/shard_map/ppermute | solution.py:38
  21.8 11.2 %collective-permute-start.7 = (bf16[384,256]{1,0:T(8,128)(2,1)S(1)}, bf16[384,256]{1,0:T(8,128)(2,1)S(1)}, u32[]{:S(2)}, u32[]{:S(2)}) collective-permute-start(bf16[384,256]{1,0:T(8,128)(2,1)S(1)} %get-tuple-element.48), channel_id=1, source_target_pairs={{0,2},{1,3},{2,0},{3,1},{4,6},{5,7},{6,4},{7,5},{8,10},{9,11},{10,... | collective-permute-start | bytes 589832 | tf_op jit(solution)/shard_map/ppermute | solution.py:38
  23.2 9.9 %collective-permute-start.8 = (bf16[384,256]{1,0:T(8,128)(2,1)S(1)}, bf16[384,256]{1,0:T(8,128)(2,1)S(1)}, u32[]{:S(2)}, u32[]{:S(2)}) collective-permute-start(bf16[384,256]{1,0:T(8,128)(2,1)S(1)} %get-tuple-element.49), channel_id=1, source_target_pairs={{0,1},{1,0},{2,3},{3,2},{4,5},{5,4},{6,7},{7,6},{8,9},{9,8},{10,11... | collective-permute-start | bytes 589832 | tf_op jit(solution)/shard_map/ppermute | solution.py:38
  23.5 13.4 %collective-permute-start.9 = (bf16[256,256]{1,0:T(8,128)(2,1)S(1)}, bf16[256,256]{1,0:T(8,128)(2,1)S(1)}, u32[]{:S(2)}, u32[]{:S(2)}) collective-permute-start(bf16[256,256]{1,0:T(8,128)(2,1)S(1)} %get-tuple-element.52), channel_id=1, source_target_pairs={{0,12},{4,8},{8,4},{12,0},{1,13},{5,9},{9,5},{13,1},{2,14},{6,10},... | collective-permute-start | bytes 393224 | tf_op jit(solution)/shard_map/ppermute | solution.py:38
  25.9 12.2 %collective-permute-start.10 = (bf16[256,256]{1,0:T(8,128)(2,1)S(1)}, bf16[256,256]{1,0:T(8,128)(2,1)S(1)}, u32[]{:S(2)}, u32[]{:S(2)}) collective-permute-start(bf16[256,256]{1,0:T(8,128)(2,1)S(1)} %get-tuple-element.53), channel_id=1, source_target_pairs={{0,8},{4,12},{8,0},{12,4},{1,9},{5,13},{9,1},{13,5},{2,10},{6,14},... | collective-permute-start | bytes 393224 | tf_op jit(solution)/shard_map/ppermute | solution.py:38
  28.8 13.8 %copy-start.3 = (s32[1,4,2]{1,2,0:T(2,128)S(1)}, s32[1,4,2]{1,2,0:T(2,128)}, u32[]{:S(2)}) copy-start(s32[1,4,2]{1,2,0:T(2,128)} %param.12) | copy-start | bytes 100
  28.8 16.4 %collective-permute-start.14 = (bf16[256,256]{1,0:T(8,128)(2,1)S(1)}, bf16[256,256]{1,0:T(8,128)(2,1)S(1)}, u32[]{:S(2)}, u32[]{:S(2)}) collective-permute-start(bf16[256,256]{1,0:T(8,128)(2,1)S(1)} %get-tuple-element.55), channel_id=1, source_target_pairs={{0,4},{4,0},{8,12},{12,8},{1,5},{5,1},{9,13},{13,9},{2,6},{6,2},{1... | collective-permute-start | bytes 393224 | tf_op jit(solution)/shard_map/ppermute | solution.py:38
  33.7 4.6 %collective-permute-start.13 = (bf16[64,256]{1,0:T(8,128)(2,1)S(1)}, bf16[64,256]{1,0:T(8,128)(2,1)S(1)}, u32[]{:S(2)}, u32[]{:S(2)}) collective-permute-start(bf16[64,256]{1,0:T(8,128)(2,1)S(1)} %get-tuple-element.51.own_ref), channel_id=1, source_target_pairs={{0,4},{4,0},{8,12},{12,8},{1,5},{5,1},{9,13},{13,9},{2,6},{6,2},{1... | collective-permute-start | bytes 98312 | tf_op jit(solution)/shard_map/ppermute | solution.py:34
  34.6 5.2 %collective-permute-start.12 = (bf16[64,256]{1,0:T(8,128)(2,1)S(1)}, bf16[64,256]{1,0:T(8,128)(2,1)S(1)}, u32[]{:S(2)}, u32[]{:S(2)}) collective-permute-start(bf16[64,256]{1,0:T(8,128)(2,1)S(1)} %get-tuple-element.51.own_ref), channel_id=1, source_target_pairs={{0,8},{4,12},{8,0},{12,4},{1,9},{5,13},{9,1},{13,5},{2,10},{6,14},... | collective-permute-start | bytes 98312 | tf_op jit(solution)/shard_map/ppermute | solution.py:34
  36.8 5.7 %collective-permute-start.11 = (bf16[64,256]{1,0:T(8,128)(2,1)S(1)}, bf16[64,256]{1,0:T(8,128)(2,1)S(1)}, u32[]{:S(2)}, u32[]{:S(2)}) collective-permute-start(bf16[64,256]{1,0:T(8,128)(2,1)S(1)} %get-tuple-element.51.own_ref), channel_id=1, source_target_pairs={{0,12},{4,8},{8,4},{12,0},{1,13},{5,9},{9,5},{13,1},{2,14},{6,10},... | collective-permute-start | bytes 98312 | tf_op jit(solution)/shard_map/ppermute | solution.py:34
  43.2 3.7 %collective-permute-start.17 = (f32[64,256]{1,0:T(8,128)S(1)}, f32[64,256]{1,0:T(8,128)S(1)}, u32[]{:S(2)}, u32[]{:S(2)}) collective-permute-start(f32[64,256]{1,0:T(8,128)S(1)} %get-tuple-element.56.refs_0_), channel_id=1, source_target_pairs={{0,1},{1,0},{2,3},{3,2},{4,5},{5,4},{6,7},{7,6},{8,9},{9,8},{10,11... | collective-permute-start | bytes 196616 | tf_op jit(solution)/shard_map/ppermute | solution.py:34
  43.3 5.0 %collective-permute-start.16 = (f32[64,256]{1,0:T(8,128)S(1)}, f32[64,256]{1,0:T(8,128)S(1)}, u32[]{:S(2)}, u32[]{:S(2)}) collective-permute-start(f32[64,256]{1,0:T(8,128)S(1)} %get-tuple-element.56.refs_0_), channel_id=1, source_target_pairs={{0,2},{1,3},{2,0},{3,1},{4,6},{5,7},{6,4},{7,5},{8,10},{9,11},{10,... | collective-permute-start | bytes 196616 | tf_op jit(solution)/shard_map/ppermute | solution.py:34
  43.7 5.0 %collective-permute-start.15 = (f32[64,256]{1,0:T(8,128)S(1)}, f32[64,256]{1,0:T(8,128)S(1)}, u32[]{:S(2)}, u32[]{:S(2)}) collective-permute-start(f32[64,256]{1,0:T(8,128)S(1)} %get-tuple-element.56.refs_0_), channel_id=1, source_target_pairs={{0,3},{1,2},{2,1},{3,0},{4,7},{5,6},{6,5},{7,4},{8,11},{9,10},{10,... | collective-permute-start | bytes 196616 | tf_op jit(solution)/shard_map/ppermute | solution.py:34

commit v3 on v2

--- a/solution.py
+++ b/solution.py
@@ -11,6 +11,7 @@
 VMEM = pl.BlockSpec(memory_space=pltpu.VMEM)
 SMEM = pl.BlockSpec(memory_space=pltpu.SMEM)
 HBM = pl.BlockSpec(memory_space=pltpu.HBM)
+ANY = pl.BlockSpec(memory_space=pl.ANY)
 PARAMS = pltpu.CompilerParams(vmem_limit_bytes=48 * 1024 * 1024)
 
 
@@ -27,7 +28,7 @@
 
 
 def exchange_order(n):
-    return sorted(range(1, n), key=lambda k: -k)
+    return sorted(range(1, n), key=lambda k: (k == 1, k))
 
 
 def send(x, axis, k, n):
@@ -53,13 +54,14 @@
     return mm(ah, bh, dims) + (mm(ah, bl, dims) + mm(al, bh, dims))
 
 
-def call(kernel, out_shape, flops, nbytes, in_specs, out_specs, scratch=()):
+def call(kernel, out_shape, flops, nbytes, in_specs, out_specs, scratch=(), aliases={}):
     return pl.pallas_call(
         kernel,
         out_shape=out_shape,
         in_specs=in_specs,
         out_specs=out_specs,
         scratch_shapes=list(scratch),
+        input_output_aliases=aliases,
         compiler_params=PARAMS,
         cost_estimate=pl.CostEstimate(flops=flops, bytes_accessed=nbytes, transcendentals=0),
     )
@@ -116,8 +118,8 @@
 
 def local_kernel(
     dims, list_hbm, outer_hbm, features_hbm, weight_hbm, values_hbm,
-    near_ref, base_ref, local_ref, scale_ref, picked_ref, turned_ref, place_ref,
-    list_ref, outer_ref, features_ref, weight_ref, values_ref, sources_ref, inverse_ref, sems,
+    near_ref, base_ref, local_ref, scale_ref, picked_ref, turned_ref, values_ref, place_ref,
+    list_ref, outer_ref, features_ref, weight_ref, sources_ref, inverse_ref, sems,
 ):
     row_blocks, fanout, side, width, ns, nd, inner_cap, outer_cap = dims
     pairs = [
@@ -168,28 +170,31 @@
         turned_ref[i] = block.T
 
 
-def middle_kernel(dims, place_ref, *refs):
+def middle_kernel(dims, place_any, *refs):
     row_blocks, fanout, side, width, ns, nd, inner_cap, outer_cap = dims
     n_in = (ns - 1) + (nd - 1)
     arrived = refs[:n_in]
     base_ref, scale_ref, picked_ref, turned_ref, weight_ref, cotangent_ref = refs[n_in : n_in + 6]
-    act_ref, scaled_ref, half_ref, total_ref = refs[n_in + 6 : n_in + 10]
-    leaving = refs[n_in + 10 :]
-    total_ref[...] = jnp.zeros_like(total_ref)
-    i = 0
+    mixed_ref, scaled_ref, half_ref, total_ref = refs[n_in + 6 : n_in + 10]
+    leaving, (place_ref, sem) = refs[n_in + 10 : -2], refs[-2:]
+    copy = pltpu.make_async_copy(place_any, place_ref, sem)
+    copy.start()
+    terms = []
     for ref in arrived:
         for j in range(ref.shape[0] // side):
-            term = mm(picked_ref[i], ref[j * side : (j + 1) * side, :])
-            rows = pl.ds(pl.multiple_of(place_ref[i] * side, side), side)
-            total_ref[rows, :] += term
-            i += 1
+            terms.append(mm(picked_ref[len(terms)], ref[j * side : (j + 1) * side, :]))
+    total_ref[...] = jnp.zeros_like(total_ref)
+    copy.wait()
+    for i, term in enumerate(terms):
+        rows = pl.ds(pl.multiple_of(place_ref[i] * side, side), side)
+        total_ref[rows, :] += term
     weight = split(weight_ref[...])
     for r in range(row_blocks):
         rows = slice(r * side, (r + 1) * side)
         scale = scale_ref[rows, :]
         mixed = (base_ref[rows, :] + mm3(split(total_ref[rows, :]), weight)) * scale
         gate = jax.nn.sigmoid(mixed)
-        act_ref[rows, :] = mixed * gate
+        mixed_ref[rows, :] = mixed
         scaled = cotangent_ref[rows, :] * gate * (1.0 + mixed * (1.0 - gate)) * scale
         scaled_ref[rows, :] = scaled
         half_ref[rows, :] = scaled.astype(BF16)
@@ -201,45 +206,92 @@
             i += 1
 
 
+def turn_rows(ref, place_ref, turned_ref, half_ref, first, count, side):
+    for j in range(count):
+        rows = pl.ds(pl.multiple_of(place_ref[first + j] * side, side), side)
+        ref[j * side : (j + 1) * side, :] = mm(turned_ref[first + j], half_ref[rows, :]).astype(BF16)
+
+
 def weight_kernel(
-    dims, first, place_ref, features_ref, local_ref, total_ref, scaled_ref, half_ref, turned_ref, own_ref, *refs
+    dims, first, place_any, features_ref, local_ref, total_ref, scaled_ref, half_ref, turned_ref, own_ref, *refs
 ):
     row_blocks, fanout, side, width, ns, nd, inner_cap, outer_cap = dims
-    leaving, term_ref = refs[:-1], refs[-1]
-    p = lax.axis_index("dom")
+    leaving, (term_ref, place_ref, sem) = refs[:-3], refs[-3:]
+    copy = pltpu.make_async_copy(place_any, place_ref, sem)
+    copy.start()
     down = ((0,), (0,))
     ah, al = split(local_ref[...] + total_ref[...])
     half = half_ref[...]
     term = mm3(split(features_ref[...]), split(scaled_ref[...]), down)
     term_ref[...] = term + (mm(ah, half, down) + mm(al, half, down))
-    piece = own_ref.shape[0]
-    own_ref[...] = term_ref[pl.ds(pl.multiple_of(p * piece, 8), piece), :]
-    i = first
-    for ref, k in zip(leaving, exchange_order(nd)):
-        for j in range(outer_cap):
-            rows = pl.ds(pl.multiple_of(place_ref[i] * side, side), side)
-            ref[j * side : (j + 1) * side, :] = mm(turned_ref[i], half_ref[rows, :]).astype(BF16)
-            i += 1
-        at = pl.multiple_of(back_partner(p, k, nd) * piece, 8)
-        hi, lo = split(term_ref[pl.ds(at, piece), :])
-        ref[outer_cap * side : outer_cap * side + piece, :] = hi
-        ref[outer_cap * side + piece :, :] = lo
-
-
-def spread_kernel(dims, list_hbm, values_hbm, scaled_ref, half_ref, out_ref, list_ref, values_ref, sums_ref, sems):
+    count = own_ref.shape[0]
+    mine = lax.axis_index("dom") & 1
+    own_ref[...] = term_ref[pl.ds(pl.multiple_of(mine * count, 8), count), :]
+    hi, lo = split(term_ref[pl.ds(pl.multiple_of((1 - mine) * count, 8), count), :])
+    copy.wait()
+    for i, ref in enumerate(leaving):
+        turn_rows(ref, place_ref, turned_ref, half_ref, first + i * outer_cap, outer_cap, side)
+    start = outer_cap * side
+    leaving[-1][start : start + count, :] = hi
+    leaving[-1][start + count :, :] = lo
+
+
+def halve(rows, bit, own_ref, give_ref, total_ref):
+    mine = (lax.axis_index("dom") >> bit) & 1
+    own_ref[...] = total_ref[pl.ds(pl.multiple_of(mine * rows, 8), rows), :]
+    give_ref[...] = total_ref[pl.ds(pl.multiple_of((1 - mine) * rows, 8), rows), :]
+
+
+def near_sum_kernel(start, own_ref, load_ref, next_ref, give_ref, total_ref):
+    count = own_ref.shape[0]
+    hi = load_ref[start : start + count, :].astype(F32)
+    total_ref[...] = own_ref[...] + (hi + load_ref[start + count :, :].astype(F32))
+    halve(next_ref.shape[0], 1, next_ref, give_ref, total_ref)
+
+
+def far_sum_kernel(bit, own_ref, load_ref, next_ref, give_ref, total_ref):
+    total_ref[...] = own_ref[...] + load_ref[...]
+    halve(next_ref.shape[0], bit, next_ref, give_ref, total_ref)
+
+
+def last_sum_kernel(own_ref, load_ref, *refs):
+    refs[-1][...] = (own_ref[...] + load_ref[...]).astype(BF16)
+
+
+def shard_sum_kernel(ns, own_ref, *refs):
+    terms = dict(zip([0] + exchange_order(ns), (own_ref, *refs)))
+    refs[-1][...] = tree_sum([terms[k][...].astype(F32) for k in range(ns)])
+
+
+def join_kernel(bit, own_ref, load_ref, *refs):
+    rows = own_ref.shape[0]
+    mine = (lax.axis_index("dom") >> bit) & 1
+    refs[-1][pl.ds(pl.multiple_of(mine * rows, 8), rows), :] = own_ref[...]
+    refs[-1][pl.ds(pl.multiple_of((1 - mine) * rows, 8), rows), :] = load_ref[...]
+
+
+def spread_kernel(
+    dims, list_any, values_ref, mixed_ref, scaled_ref, half_ref, act_hbm, out_ref, act_ref, list_ref, sums_ref, sems
+):
     row_blocks, fanout, side, width = dims
-    copies = fetch(
-        [(list_hbm, list_ref)] + [(values_hbm.at[r], values_ref.at[r]) for r in range(row_blocks)], sems
-    )
-    sums_ref[: row_blocks * side, :] = scaled_ref[...]
-    copies[0].wait()
+    (listed,) = fetch([(list_any, list_ref)], sems)
+    mixed = mixed_ref[...]
+    act_ref[...] = mixed * jax.nn.sigmoid(mixed)
+    store = pltpu.make_async_copy(act_ref, act_hbm, sems.at[1])
+    store.start()
+    sums_ref[...] = jnp.zeros_like(sums_ref)
+    listed.wait()
     for r in range(row_blocks):
-        copies[r + 1].wait()
-        half = half_ref[r * side : (r + 1) * side, :]
-        for k in range(fanout):
-            at = pl.multiple_of(jnp.minimum(list_ref[r, k], row_blocks) * side, side)
-            sums_ref[pl.ds(at, side), :] += mm(values_ref[r, k], half, ((0,), (0,)))
-    out_ref[...] = sums_ref[: row_blocks * side, :]
+        half = half_ref[r * side : (r + 1) * side, :].astype(F32).T.astype(BF16)
+        for k in range(0, fanout, 2):
+            blocks = jnp.concatenate([values_ref[r, k], values_ref[r, k + 1]], axis=1)
+            terms = mm(half, blocks)
+            for kk in (0, 1):
+                sums_ref[jnp.minimum(list_ref[r, k + kk], row_blocks)] += terms[:, kk * side : (kk + 1) * side]
+    for c in range(row_blocks):
+        rows = slice(c * side, (c + 1) * side)
+        out_ref[rows, :] = scaled_ref[rows, :] + sums_ref[c].T
+    store.wait()
 
 
 def tree_sum(terms):
@@ -256,44 +308,27 @@
         sums_ref[rows, :] += jnp.where(target >= 0, term, 0.0)
 
 
-def dom_sum_kernel(nd, side, targets_ref, part_ref, own_ref, *refs):
-    arrived, (sums_ref, piece_ref) = refs[:-2], refs[-2:]
-    piece = own_ref.shape[0]
-    start = targets_ref.shape[1] * side
-    terms = [own_ref[...]]
-    for ref in reversed(arrived):
-        hi = ref[start : start + piece, :].astype(F32)
-        terms.append(hi + ref[start + piece :, :].astype(F32))
-    piece_ref[...] = tree_sum(terms).astype(BF16)
+def finish_kernel(items, sizes, side, inner_any, outer_any, part_ref, weight_ref, *refs):
+    arrived, (out_hbm, out_ref, sums_ref, inner_ref, outer_ref, sems) = refs[:-6], refs[-6:]
+    tables = fetch([(inner_any, inner_ref), (outer_any, outer_ref)], sems)
     sums_ref[...] = part_ref[...]
-    p = lax.axis_index("dom")
-    for ref, k in zip(arrived, exchange_order(nd)):
-        add_rows(sums_ref, ref, targets_ref, partner(p, k, nd), side)
-
-
-def shard_sum_kernel(ns, side, targets_ref, part_ref, own_ref, *refs):
-    arrived, pieces, (sums_ref, out_ref) = refs[: ns - 2], refs[ns - 2 : -2], refs[-2:]
-    out_ref[...] = tree_sum([ref[...].astype(F32) for ref in (own_ref, *reversed(pieces))])
-    sums_ref[...] = part_ref[...]
-    s = lax.axis_index("shard")
-    for ref, k in zip(arrived, exchange_order(ns)):
-        add_rows(sums_ref, ref, targets_ref, partner(s, k, ns), side)
-
-
-def finish_kernel(ns, side, targets_ref, part_ref, weight_ref, near_ref, out_ref, sums_ref):
-    sums_ref[...] = part_ref[...]
-    peer = partner(lax.axis_index("shard"), exchange_order(ns)[-1], ns)
-    add_rows(sums_ref, near_ref, targets_ref, peer, side)
-    out_ref[...] = mm3(split(sums_ref[...]), split(weight_ref[...]), ((1,), (1,)))
-
-
-def place_kernel(nd, *refs):
-    p = lax.axis_index("dom")
-    out_ref = refs[-1]
-    piece = refs[0].shape[0]
-    for ref, k in zip(refs[:-1], [0] + exchange_order(nd)):
-        at = pl.multiple_of(back_partner(p, k, nd) * piece, 8)
-        out_ref[pl.ds(at, piece), :] = ref[...]
+    weight = split(weight_ref[...])
+    for copy in tables:
+        copy.wait()
+    for (axis, k), ref in zip(items, arrived):
+        targets_ref = inner_ref if axis == "shard" else outer_ref
+        add_rows(sums_ref, ref, targets_ref, partner(lax.axis_index(axis), k, sizes[axis]), side)
+    stores = []
+    for r in range(sums_ref.shape[0] // side):
+        rows = slice(r * side, (r + 1) * side)
+        out_ref[rows, :] = mm3(split(sums_ref[rows, :]), weight, ((1,), (1,)))
+        stores.append(pltpu.make_async_copy(out_ref.at[rows], out_hbm.at[rows], sems.at[2 + r]))
+        stores[-1].start()
+    for store in stores:
+        store.wait()
+
+
+GATES = {"last": [("dom", 2), ("dom", 3), ("dom", 1)], "shard": [("shard", 2)], "join": [("shard", 3), ("shard", 1)], "place": []}
 
 
 def on_device(features, weight, cotangent, block_values, block_list, send_inner, send_outer):
@@ -328,17 +363,17 @@
     inner_in = [send(x, "shard", k, ns) for x, k in zip(packed, inner_order)]
     outer_in = [send(x, "dom", k, nd) for x, k in zip(packed[ns - 1 :], outer_order)]
 
-    near, base, local, scale, picked, turned, place = call(
+    near, base, local, scale, picked, turned, values, place = call(
         functools.partial(local_kernel, dims),
         [
             packed_outer[-1], rows_f32, rows_f32, rows_f32,
-            shape((slots, side, side), BF16), shape((slots, side, side), BF16), shape((slots,), jnp.int32),
+            shape((slots, side, side), BF16), shape((slots, side, side), BF16),
+            shape(block_values.shape, BF16), shape((slots,), jnp.int32),
         ],
         4 * row_blocks * fanout * side * side * width * 3, 12 * nbytes,
-        [HBM] * 5, [VMEM] * 6 + [SMEM],
+        [HBM] * 5, [VMEM] * 7 + [SMEM],
         [
             list_table, outer_table, pltpu.VMEM(features.shape, F32), pltpu.VMEM(weight.shape, F32),
-            pltpu.VMEM(block_values.shape, BF16),
             pltpu.VMEM(((row_blocks + 1) * side, 3 * width), BF16),
             pltpu.SMEM((row_blocks + ns * inner_cap + nd * outer_cap,), jnp.int32),
             pltpu.SemaphoreType.DMA((4 + row_blocks,)),
@@ -351,47 +386,75 @@
         functools.partial(middle_kernel, dims),
         [rows_f32, rows_f32, rows_f16, rows_f32] + packed_inner,
         2 * slots * side * side * width * 2, 8 * nbytes,
-        [SMEM] + [VMEM] * (n_in + 6), [VMEM] * (4 + ns - 1),
+        [ANY] + [VMEM] * (n_in + 6), [VMEM] * (4 + ns - 1),
+        [pltpu.SMEM((slots,), jnp.int32), pltpu.SemaphoreType.DMA],
     )(place, *inner_in, *outer_in, base, scale, picked, turned, weight, cotangent)
-    activations, scaled, half, total = outs[:4]
+    mixed, scaled, half, total = outs[:4]
     inner_back = [send_back(x, "shard", k, ns) for x, k in zip(outs[4:], inner_order)]
 
-    piece_rows = width // nd
-    start = outer_cap * side
+    count = width // 2
     outs = call(
         functools.partial(weight_kernel, dims, (ns - 1) * inner_cap),
-        [shape((piece_rows, width), F32)] + [shape((start + 2 * piece_rows, width), BF16)] * (nd - 1),
+        [shape((count, width), F32)] + packed_outer[:-1] + [shape((outer_cap * side + 2 * count, width), BF16)],
         10 * node_count * width * width, 5 * nbytes,
-        [SMEM] + [VMEM] * 6, [VMEM] * nd, [pltpu.VMEM((width, width), F32)],
+        [ANY] + [VMEM] * 6, [VMEM] * nd,
+        [pltpu.VMEM((width, width), F32), pltpu.SMEM((slots,), jnp.int32), pltpu.SemaphoreType.DMA],
     )(place, features, local, total, scaled, half, turned)
-    outer_back = [send_back(x, "dom", k, nd) for x, k in zip(outs[1:], outer_order)]
-
-    part = call(
-        functools.partial(spread_kernel, dims[:4]), rows_f32,
+    own, outer_terms = outs[0], outs[1:]
+    near_back = send_back(outer_terms[-1], "dom", 1, nd)
+    outer_back = [send_back(x, "dom", k, nd) for x, k in zip(outer_terms[:-1], outer_order)] + [near_back]
+
+    activations, part = call(
+        functools.partial(spread_kernel, dims[:4]), [rows_f32, rows_f32],
         2 * row_blocks * fanout * side * side * width, 8 * nbytes,
-        [HBM, HBM, VMEM, VMEM], VMEM,
+        [ANY] + [VMEM] * 4, [HBM, VMEM],
         [
-            list_table, pltpu.VMEM(block_values.shape, BF16),
-            pltpu.VMEM(((row_blocks + 1) * side, width), F32), pltpu.SemaphoreType.DMA((1 + row_blocks,)),
+            pltpu.VMEM((node_count, width), F32), list_table, pltpu.VMEM((row_blocks + 1, width, side), F32),
+            pltpu.SemaphoreType.DMA((2,)),
         ],
-    )(keep(block_list), keep(block_values), scaled, half)
-    part, piece = call(
-        functools.partial(dom_sum_kernel, nd, side), [rows_f32, shape((piece_rows, width), BF16)],
-        0, 4 * nbytes, [SMEM] + [VMEM] * (nd + 1), [VMEM] * 2,
-    )(outer_targets, part, outs[0], *outer_back)
-    pieces = [send(piece, "shard", k, ns) for k in inner_order]
-    part, weight_sum = call(
-        functools.partial(shard_sum_kernel, ns, side), [rows_f32, shape((piece_rows, width), F32)],
-        0, 4 * nbytes, [SMEM] + [VMEM] * (2 * ns - 1), [VMEM] * 2,
-    )(inner_targets, part, piece, *inner_back[:-1], *pieces)
-    gathered = [weight_sum] + [send(weight_sum, "dom", k, nd) for k in outer_order]
-    grad_weight = call(
-        functools.partial(place_kernel, nd), shape((width, width), F32), 0, nbytes, [VMEM] * nd, VMEM
-    )(*gathered)
+    )(block_list, values, mixed, scaled, half)
+
+    back = {("shard", k): x for k, x in zip(inner_order, inner_back)}
+    back.update({("dom", k): x for k, x in zip(outer_order, outer_back)})
+    sizes = {"shard": ns, "dom": nd}
+
+    def stage(kernel, name, inputs, rows, dtype=F32):
+        gated = [back[item] for item in GATES[name] if item in back] + [part] * (name == "shard")
+        return call(
+            kernel, shape((rows, width), dtype), 0, nbytes // 4,
+            [VMEM] * len(inputs) + [ANY] * len(gated), VMEM,
+        )(*inputs, *gated)
+
+    bits = nd.bit_length() - 1
+    load = near_back
+    for bit in range(bits):
+        if bit == bits - 1:
+            piece = stage(last_sum_kernel, "last", [own, load], count, BF16)
+            break
+        kernel = functools.partial(near_sum_kernel, outer_cap * side) if bit == 0 else functools.partial(far_sum_kernel, bit + 1)
+        count //= 2
+        own, give = call(
+            kernel, [shape((count, width), F32)] * 2, 0, nbytes // 4,
+            [VMEM] * 2, [VMEM] * 2, [pltpu.VMEM((2 * count, width), F32)],
+        )(own, load)
+        load = send(give, "dom", 2 << bit, nd)
+    pieces = [piece] + [send(piece, "shard", k, ns) for k in inner_order]
+    weight_sum = stage(functools.partial(shard_sum_kernel, ns), "shard", pieces, count)
+    for bit in reversed(range(bits)):
+        count *= 2
+        load = send(weight_sum, "dom", 1 << bit, nd)
+        weight_sum = stage(
+            functools.partial(join_kernel, bit), "join" if bit == 1 else "place", [weight_sum, load], count
+        )
     grad_features = call(
-        functools.partial(finish_kernel, ns, side), rows_f32, 6 * node_count * width * width, 4 * nbytes,
-        [SMEM] + [VMEM] * 3, VMEM, [pltpu.VMEM((node_count, width), F32)],
-    )(inner_targets, part, weight, inner_back[-1])
+        functools.partial(finish_kernel, list(back), sizes, side), rows_f32,
+        6 * node_count * width * width, 4 * nbytes, [ANY] * 2 + [VMEM] * (2 + len(back)), HBM,
+        [
+            pltpu.VMEM((node_count, width), F32), pltpu.VMEM((node_count, width), F32), inner_table, outer_table,
+            pltpu.SemaphoreType.DMA((2 + row_blocks,)),
+        ],
+    )(inner_targets, outer_targets, part, weight, *back.values())
+    grad_weight = weight_sum
     return (activations, grad_features, grad_weight)
 
 

time: 49.7 us -> 48 us (0.966)
  starting transfers between devices: 18.5 us -> 21.4 us
  waiting for transfers between devices: 14.3 us -> 12 us
  Pallas kernels: 15.8 us -> 13.7 us
    ppermute x6, waiting for transfers between devices: 4.05 us -> 1 us  [send_back(): return lax.ppermute(x, axis, [(i, back_partner(i, k, n)) for i in range(n)])]
    ppermute x6, starting transfers between devices: 4.41 us -> 6.24 us  [send_back(): return lax.ppermute(x, axis, [(i, back_partner(i, k, n)) for i in range(n)])]
    pallas_call x5 -> x7, Pallas kernels: 6.87 us -> 5.33 us  [the longest x1 2.43 us: on_device(): call(functools.partial(spread_kernel, dims[:4]), [rows_f32, rows_f32], 2...]
    ppermute x12, starting transfers between devices: 14.1 us -> 15.1 us  [send(): return lax.ppermute(x, axis, [(i, partner(i, k, n)) for i in range(n)])]
    pallas_call x1, Pallas kernels: 2.19 us -> 1.46 us  [on_device(): call(functools.partial(middle_kernel, dims), [rows_f32, rows_f32, rows_f1...]
    ppermute x12, waiting for transfers between devices: 10.3 us -> 10.9 us  [send(): return lax.ppermute(x, axis, [(i, partner(i, k, n)) for i in range(n)])]
  transfers between devices with their start and end apart: 18 -> 18, of which waited for: 8 -> 9; matrix products, arithmetic and copies ran while one was open for 0% -> 0% of each run, Pallas kernels for 21% -> 19%
where the time goes in v3:
time: 48 us; the launch traced here: 47.8 us
  starting transfers between devices  21.4 us (45%)
  Pallas kernels  13.7 us (29%)
  waiting for transfers between devices  12 us (25%)
  between operations  0.77 us (2%)
    ppermute x12, starting transfers between devices, send(): return lax.ppermute(x, axis, [(i, partner(i, k, n)) for i in range(n)])  15.1 us
    ppermute x12, waiting for transfers between devices, send(): return lax.ppermute(x, axis, [(i, partner(i, k, n)) for i in range(n)])  10.9 us
    ppermute x6, starting transfers between devices, send_back(): return lax.ppermute(x, axis, [(i, back_partner(i, k, n)) for i in range(n)])  6.24 us
    pallas_call x1, Pallas kernels, on_device(): call(functools.partial(local_kernel, dims), [packed_outer[-1], rows_f32,...  4.52 us
    pallas_call x1, Pallas kernels, on_device(): call(functools.partial(spread_kernel, dims[:4]), [rows_f32, rows_f32], 2...  2.43 us
    pallas_call x1, Pallas kernels, on_device(): call(functools.partial(finish_kernel, list(back), sizes, side), rows_f32,...  2.08 us
    pallas_call x1, Pallas kernels, on_device(): call(functools.partial(middle_kernel, dims), [rows_f32, rows_f32, rows_f1...  1.46 us
    pallas_call x1, Pallas kernels, on_device(): call(functools.partial(pack_kernel, ns, nd, side), packed_inner + packed_...  1.2 us
  transfers between devices with their start and end apart: 18, of which 9 were waited for; matrix products, arithmetic and copies ran while one was open for 0% of the time, Pallas kernels for 19%

profile of v3, /device:TPU:0, one launch (start us, length us, event | category | flops | bytes accessed | tf_op | source)
XLA Modules:
  0.0 47.8 jit_solution(15769276179113416379)
XLA Ops:
  0.6 1.2 %shard_map.95 = (bf16[256,256]{1,0:T(8,128)(2,1)S(1)}, bf16[256,256]{1,0:T(8,128)(2,1)S(1)}, bf16[256,256]{1,0:T(8,128)(2,1)S(1)}, bf16[256,256]{1,0:T(8,128)(2,1)S(1)}, bf16[256,256]{1,0:T(8,128)(2,1)S(1)}) custom-call(s32[1,2,4]{2,1,0:T(2,128)} %bitcast.5, s32[1,2,4]{2,1,0:T(2,128)} %bitcast.2, f32[512,256]{1,0:T(8,128)} %features_ref.1), custom_call_target="tpu_custom_call" | custom-call | bytes 1572864 | tf_op jit(solution)/shard_map/pallas_call | solution.py:358
  1.8 4.1 %collective-permute-start = (bf16[256,256]{1,0:T(8,128)(2,1)S(1)}, bf16[256,256]{1,0:T(8,128)(2,1)S(1)}, u32[]{:S(2)}, u32[]{:S(2)}) collective-permute-start(bf16[256,256]{1,0:T(8,128)(2,1)S(1)} %get-tuple-element.33), channel_id=1, source_target_pairs={{0,8},{4,12},{8,0},{12,4},{1,9},{5,13},{9,1},{13,5},{2,10},{6,14},... | collective-permute-start | bytes 393224 | tf_op jit(solution)/shard_map/ppermute | solution.py:35
  5.9 1.3 %collective-permute-start.1 = (bf16[256,256]{1,0:T(8,128)(2,1)S(1)}, bf16[256,256]{1,0:T(8,128)(2,1)S(1)}, u32[]{:S(2)}, u32[]{:S(2)}) collective-permute-start(bf16[256,256]{1,0:T(8,128)(2,1)S(1)} %get-tuple-element.34), channel_id=1, source_target_pairs={{0,12},{4,8},{8,4},{12,0},{1,13},{5,9},{9,5},{13,1},{2,14},{6,10},... | collective-permute-start | bytes 393224 | tf_op jit(solution)/shard_map/ppermute | solution.py:35
  7.5 1.5 %collective-permute-start.3 = (bf16[256,256]{1,0:T(8,128)(2,1)S(1)}, bf16[256,256]{1,0:T(8,128)(2,1)S(1)}, u32[]{:S(2)}, u32[]{:S(2)}) collective-permute-start(bf16[256,256]{1,0:T(8,128)(2,1)S(1)} %get-tuple-element.36), channel_id=1, source_target_pairs={{0,2},{1,3},{2,0},{3,1},{4,6},{5,7},{6,4},{7,5},{8,10},{9,11},{10,... | collective-permute-start | bytes 393224 | tf_op jit(solution)/shard_map/ppermute | solution.py:35
  9.0 4.5 %shard_map.94 = (bf16[256,256]{1,0:T(8,128)(2,1)S(1)}, f32[512,256]{1,0:T(8,128)S(1)}, f32[512,256]{1,0:T(8,128)S(1)}, f32[512,256]{1,0:T(8,128)S(1)}, bf16[12,1...) custom-call(s32[4,16]{1,0:T(4,128)} %list_any.1, ...), custom_call_target="tpu_custom_call" | custom-call | flops 3221225472 | bytes 6291456 | tf_op jit(solution)/shard_map/pallas_call | solution.py:366
  13.6 2.4 %collective-permute-done.refs_0_ = bf16[256,256]{1,0:T(8,128)(2,1)S(1)} collective-permute-done((bf16[256,256]{1,0:T(8,128)(2,1)S(1)}, bf16[256,256]{1,0:T(8,128)(2,1)S(1)}, u32[]{:S(2)}, u32[]{:S(2)}) %collective-permute-start) | collective-permute-done | bytes 131104 | tf_op jit(solution)/shard_map/ppermute | solution.py:35
  16.4 0.8 %collective-permute-done.5.refs_5_ = bf16[256,256]{1,0:T(8,128)(2,1)S(1)} collective-permute-done((bf16[256,256]{1,0:T(8,128)(2,1)S(1)}, bf16[256,256]{1,0:T(8,128)(2,1)S(1)}, u32[]{:S(2)}, u32[]{:S(2)}) %collective-permute-start.5) | collective-permute-done | bytes 131104 | tf_op jit(solution)/shard_map/ppermute | solution.py:35
  17.3 1.5 %shard_map.96 = (f32[512,256]{1,0:T(8,128)S(1)}, f32[512,256]{1,0:T(8,128)S(1)}, bf16[512,256]{1,0:T(8,128)(2,1)S(1)}, f32[512,256]{1,0:T(8,128)S(1)}, bf16[256,...) custom-call(s32[12]{0:T(128)S(1)} %get-tuple-element.32.place_any, ...), custom_call_target="tpu_custom_call" | custom-call | flops 201326592 | bytes 4194304 | tf_op jit(solution)/shard_map/pallas_call | solution.py:385
  18.8 1.2 %shard_map.98 = (f32[128,256]{1,0:T(8,128)S(1)}, bf16[256,256]{1,0:T(8,128)(2,1)S(1)}, bf16[256,256]{1,0:T(8,128)(2,1)S(1)}, bf16[512,256]{1,0:T(8,128)(2,1)S(1)}) custom-call(s32[12]{0:T(128)S(1)} %get-tuple-element.32.place_any, f32[512,256]{1,0:T(8,128)S(1)} %copy-done, f32[512,256]{1,0:T(8,128)S(1)} %get-tuple-element.51.local_ref, ...), custom_call_target="tpu_custom_call" | custom-call | flops 335544320 | bytes 2621440 | tf_op jit(solution)/shard_map/pallas_call | solution.py:396
  20.2 1.9 %collective-permute-start.9 = (bf16[256,256]{1,0:T(8,128)(2,1)S(1)}, bf16[256,256]{1,0:T(8,128)(2,1)S(1)}, u32[]{:S(2)}, u32[]{:S(2)}) collective-permute-start(bf16[256,256]{1,0:T(8,128)(2,1)S(1)} %get-tuple-element.53), channel_id=1, source_target_pairs={{0,2},{1,3},{2,0},{3,1},{4,6},{5,7},{6,4},{7,5},{8,10},{9,11},{10,... | collective-permute-start | bytes 393224 | tf_op jit(solution)/shard_map/ppermute | solution.py:39
  22.0 3.2 %collective-permute-start.6 = (bf16[256,256]{1,0:T(8,128)(2,1)S(1)}, bf16[256,256]{1,0:T(8,128)(2,1)S(1)}, u32[]{:S(2)}, u32[]{:S(2)}) collective-permute-start(bf16[256,256]{1,0:T(8,128)(2,1)S(1)} %get-tuple-element.48), channel_id=1, source_target_pairs={{0,8},{4,12},{8,0},{12,4},{1,9},{5,13},{9,1},{13,5},{2,10},{6,14},... | collective-permute-start | bytes 393224 | tf_op jit(solution)/shard_map/ppermute | solution.py:39
  25.2 1.6 %collective-permute-start.12 = (f32[64,256]{1,0:T(8,128)S(1)}, f32[64,256]{1,0:T(8,128)S(1)}, u32[]{:S(2)}, u32[]{:S(2)}) collective-permute-start(f32[64,256]{1,0:T(8,128)S(1)} %get-tuple-element.58), channel_id=1, source_target_pairs={{0,2},{1,3},{2,0},{3,1},{4,6},{5,7},{6,4},{7,5},{8,10},{9,11},{10,... | collective-permute-start | bytes 196616 | tf_op jit(solution)/shard_map/ppermute | solution.py:35
  27.2 0.5 %collective-permute-start.8 = (bf16[256,256]{1,0:T(8,128)(2,1)S(1)}, bf16[256,256]{1,0:T(8,128)(2,1)S(1)}, u32[]{:S(2)}, u32[]{:S(2)}) collective-permute-start(bf16[256,256]{1,0:T(8,128)(2,1)S(1)} %get-tuple-element.50), channel_id=1, source_target_pairs={{0,4},{4,0},{8,12},{12,8},{1,5},{5,1},{9,13},{13,9},{2,6},{6,2},{1... | collective-permute-start | bytes 393224 | tf_op jit(solution)/shard_map/ppermute | solution.py:39
  27.8 0.9 %collective-permute-done.10.refs_4_.refs_1_ = bf16[256,256]{1,0:T(8,128)(2,1)S(1)} collective-permute-done((bf16[256,256]{1,0:T(8,128)(2,1)S(1)}, bf16[256,256]{1,0:T(8,128)(2,1)S(1)}, u32[]{:S(2)}, u32[]{:S(2)}) %collective-permute-start.10) | collective-permute-done | bytes 131104 | tf_op jit(solution)/shard_map/ppermute | solution.py:39
  28.7 1.6 %collective-permute-done.12.load_ref = f32[64,256]{1,0:T(8,128)S(1)} collective-permute-done((f32[64,256]{1,0:T(8,128)S(1)}, f32[64,256]{1,0:T(8,128)S(1)}, u32[]{:S(2)}, u32[]{:S(2)}) %collective-permute-start.12) | collective-permute-done | bytes 65568 | tf_op jit(solution)/shard_map/ppermute | solution.py:35
  30.2 1.4 %collective-permute-start.15 = (bf16[64,256]{1,0:T(8,128)(2,1)S(1)}, bf16[64,256]{1,0:T(8,128)(2,1)S(1)}, u32[]{:S(2)}, u32[]{:S(2)}) collective-permute-start(bf16[64,256]{1,0:T(8,128)(2,1)S(1)} %shard_map.101.own_ref), channel_id=1, source_target_pairs={{0,4},{4,0},{8,12},{12,8},{1,5},{5,1},{9,13},{13,9},{2,6},{6,2},{1... | collective-permute-start | bytes 98312 | tf_op jit(solution)/shard_map/ppermute | solution.py:35
  31.6 3.4 %collective-permute-start.14 = (bf16[64,256]{1,0:T(8,128)(2,1)S(1)}, bf16[64,256]{1,0:T(8,128)(2,1)S(1)}, u32[]{:S(2)}, u32[]{:S(2)}) collective-permute-start(bf16[64,256]{1,0:T(8,128)(2,1)S(1)} %shard_map.101.own_ref), channel_id=1, source_target_pairs={{0,12},{4,8},{8,4},{12,0},{1,13},{5,9},{9,5},{13,1},{2,14},{6,10},... | collective-permute-start | bytes 98312 | tf_op jit(solution)/shard_map/ppermute | solution.py:35
  35.2 2.4 %shard_map.97 = (f32[512,256]{1,0:T(8,128)}, f32[512,256]{1,0:T(8,128)S(1)}) custom-call(s32[4,16]{1,0:T(4,128)S(1)} %copy-done.5, bf16[4,16,128,128]{3,2,1,0:T(8,128)(2,1)S(1)} %get-tuple-element.31.values_ref, f32[512,256]{1,0:T(8,128)S(1)} %get-tuple-element.43.mixed_ref, f32[512,256]{1,0:T(8,128)S(1)} %get-tuple-element.44.scaled_ref, ...), custom_call_target="tpu_custom_call" | custom-call | flops 536870912 | bytes 4194304 | tf_op jit(solution)/shard_map/pallas_call | solution.py:407
  37.6 1.3 %collective-permute-done.15.refs_2_ = bf16[64,256]{1,0:T(8,128)(2,1)S(1)} collective-permute-done((bf16[64,256]{1,0:T(8,128)(2,1)S(1)}, bf16[64,256]{1,0:T(8,128)(2,1)S(1)}, u32[]{:S(2)}, u32[]{:S(2)}) %collective-permute-start.15) | collective-permute-done | bytes 32800 | tf_op jit(solution)/shard_map/ppermute | solution.py:35
  38.9 1.6 %collective-permute-done.13.refs_0_ = bf16[64,256]{1,0:T(8,128)(2,1)S(1)} collective-permute-done((bf16[64,256]{1,0:T(8,128)(2,1)S(1)}, bf16[64,256]{1,0:T(8,128)(2,1)S(1)}, u32[]{:S(2)}, u32[]{:S(2)}) %collective-permute-start.13) | collective-permute-done | bytes 32800 | tf_op jit(solution)/shard_map/ppermute | solution.py:35
  40.5 1.6 %collective-permute-start.16 = (f32[64,256]{1,0:T(8,128)S(1)}, f32[64,256]{1,0:T(8,128)S(1)}, u32[]{:S(2)}, u32[]{:S(2)}) collective-permute-start(f32[64,256]{1,0:T(8,128)S(1)} %shard_map.102.own_ref), channel_id=1, source_target_pairs={{0,2},{1,3},{2,0},{3,1},{4,6},{5,7},{6,4},{7,5},{8,10},{9,11},{10,... | collective-permute-start | bytes 196616 | tf_op jit(solution)/shard_map/ppermute | solution.py:35
  42.1 2.8 %collective-permute-done.16.load_ref = f32[64,256]{1,0:T(8,128)S(1)} collective-permute-done((f32[64,256]{1,0:T(8,128)S(1)}, f32[64,256]{1,0:T(8,128)S(1)}, u32[]{:S(2)}, u32[]{:S(2)}) %collective-permute-start.16) | collective-permute-done | bytes 65568 | tf_op jit(solution)/shard_map/ppermute | solution.py:35
  45.0 2.1 %shard_map.99 = f32[512,256]{1,0:T(8,128)} custom-call(s32[1,2,4]{2,1,0:T(2,128)S(1)} %bitcast.6, s32[1,2,4]{2,1,0:T(2,128)S(1)} %bitcast.4, f32[512,256]{1,0:T(8,128)S(1)} %get-tuple-element.47.part_ref.refs_4_, f32[256,256]{1,0:T(8,128)S(1)} %copy-done.1, bf16[256,256]{1,0:T(8,128)(2,1)S(1)} %collective-permute-done.6.refs_0_.refs_3_, ...), custom_call_target="tpu_custom_call" | custom-call | flops 201326592 | bytes 2097152 | tf_op jit(solution)/shard_map/pallas_call | solution.py:449
  47.1 0.7 %shard_map.104 = f32[256,256]{1,0:T(8,128)} custom-call(f32[128,256]{1,0:T(8,128)S(1)} %shard_map.103.own_ref, f32[128,256]{1,0:T(8,128)S(1)} %collective-permute-done.17.load_ref), custom_call_target="tpu_custom_call" | custom-call | bytes 131072 | tf_op jit(solution)/shard_map/pallas_call | solution.py:423
  (35 shorter events, 1.7 us)
Async XLA Ops:
  1.8 14.1 %collective-permute-start = (bf16[256,256]{1,0:T(8,128)(2,1)S(1)}, bf16[256,256]{1,0:T(8,128)(2,1)S(1)}, u32[]{:S(2)}, u32[]{:S(2)}) collective-permute-start(bf16[256,256]{1,0:T(8,128)(2,1)S(1)} %get-tuple-element.33), channel_id=1, source_target_pairs={{0,8},{4,12},{8,0},{12,4},{1,9},{5,13},{9,1},{13,5},{2,10},{6,14},... | collective-permute-start | bytes 393224 | tf_op jit(solution)/shard_map/ppermute | solution.py:35
  5.9 10.0 %collective-permute-start.1 = (bf16[256,256]{1,0:T(8,128)(2,1)S(1)}, bf16[256,256]{1,0:T(8,128)(2,1)S(1)}, u32[]{:S(2)}, u32[]{:S(2)}) collective-permute-start(bf16[256,256]{1,0:T(8,128)(2,1)S(1)} %get-tuple-element.34), channel_id=1, source_target_pairs={{0,12},{4,8},{8,4},{12,0},{1,13},{5,9},{9,5},{13,1},{2,14},{6,10},... | collective-permute-start | bytes 393224 | tf_op jit(solution)/shard_map/ppermute | solution.py:35
  7.3 9.2 %collective-permute-start.2 = (bf16[256,256]{1,0:T(8,128)(2,1)S(1)}, bf16[256,256]{1,0:T(8,128)(2,1)S(1)}, u32[]{:S(2)}, u32[]{:S(2)}) collective-permute-start(bf16[256,256]{1,0:T(8,128)(2,1)S(1)} %get-tuple-element.35), channel_id=1, source_target_pairs={{0,4},{4,0},{8,12},{12,8},{1,5},{5,1},{9,13},{13,9},{2,6},{6,2},{1... | collective-permute-start | bytes 393224 | tf_op jit(solution)/shard_map/ppermute | solution.py:35
  7.5 8.9 %collective-permute-start.3 = (bf16[256,256]{1,0:T(8,128)(2,1)S(1)}, bf16[256,256]{1,0:T(8,128)(2,1)S(1)}, u32[]{:S(2)}, u32[]{:S(2)}) collective-permute-start(bf16[256,256]{1,0:T(8,128)(2,1)S(1)} %get-tuple-element.36), channel_id=1, source_target_pairs={{0,2},{1,3},{2,0},{3,1},{4,6},{5,7},{6,4},{7,5},{8,10},{9,11},{10,... | collective-permute-start | bytes 393224 | tf_op jit(solution)/shard_map/ppermute | solution.py:35
  9.0 8.3 %copy-start.1 = (f32[256,256]{1,0:T(8,128)S(1)}, f32[256,256]{1,0:T(8,128)}, u32[]{:S(2)}) copy-start(f32[256,256]{1,0:T(8,128)} %weight_ref.1) | copy-start | bytes 786436
  9.0 8.3 %copy-start.2 = (f32[512,256]{1,0:T(8,128)S(1)}, f32[512,256]{1,0:T(8,128)}, u32[]{:S(2)}) copy-start(f32[512,256]{1,0:T(8,128)} %refs_11_.1) | copy-start | bytes 1572868
  9.0 7.4 %collective-permute-start.4 = (bf16[256,256]{1,0:T(8,128)(2,1)S(1)}, bf16[256,256]{1,0:T(8,128)(2,1)S(1)}, u32[]{:S(2)}, u32[]{:S(2)}) collective-permute-start(bf16[256,256]{1,0:T(8,128)(2,1)S(1)} %get-tuple-element.37), channel_id=1, source_target_pairs={{0,3},{1,2},{2,1},{3,0},{4,7},{5,6},{6,5},{7,4},{8,11},{9,10},{10,... | collective-permute-start | bytes 393224 | tf_op jit(solution)/shard_map/ppermute | solution.py:35
  13.5 5.2 %copy-start = (f32[512,256]{1,0:T(8,128)S(1)}, f32[512,256]{1,0:T(8,128)}, u32[]{:S(2)}) copy-start(f32[512,256]{1,0:T(8,128)} %features_ref.1) | copy-start | bytes 1572868
  15.9 1.3 %collective-permute-start.5 = (bf16[256,256]{1,0:T(8,128)(2,1)S(1)}, bf16[256,256]{1,0:T(8,128)(2,1)S(1)}, u32[]{:S(2)}, u32[]{:S(2)}) collective-permute-start(bf16[256,256]{1,0:T(8,128)(2,1)S(1)} %get-tuple-element.38), channel_id=1, source_target_pairs={{0,1},{1,0},{2,3},{3,2},{4,5},{5,4},{6,7},{7,6},{8,9},{9,8},{10,11... | collective-permute-start | bytes 393224 | tf_op jit(solution)/shard_map/ppermute | solution.py:35
  18.7 16.4 %copy-start.5 = (s32[4,16]{1,0:T(4,128)S(1)}, s32[4,16]{1,0:T(4,128)}, u32[]{:S(2)}) copy-start(s32[4,16]{1,0:T(4,128)} %list_any.1) | copy-start | bytes 772
  19.9 5.3 %collective-permute-start.11 = (bf16[512,256]{1,0:T(8,128)(2,1)S(1)}, bf16[512,256]{1,0:T(8,128)(2,1)S(1)}, u32[]{:S(2)}, u32[]{:S(2)}) collective-permute-start(bf16[512,256]{1,0:T(8,128)(2,1)S(1)} %get-tuple-element.55), channel_id=1, source_target_pairs={{0,1},{1,0},{2,3},{3,2},{4,5},{5,4},{6,7},{7,6},{8,9},{9,8},{10,11... | collective-permute-start | bytes 786440 | tf_op jit(solution)/shard_map/ppermute | solution.py:39
  20.2 7.1 %collective-permute-start.9 = (bf16[256,256]{1,0:T(8,128)(2,1)S(1)}, bf16[256,256]{1,0:T(8,128)(2,1)S(1)}, u32[]{:S(2)}, u32[]{:S(2)}) collective-permute-start(bf16[256,256]{1,0:T(8,128)(2,1)S(1)} %get-tuple-element.53), channel_id=1, source_target_pairs={{0,2},{1,3},{2,0},{3,1},{4,6},{5,7},{6,4},{7,5},{8,10},{9,11},{10,... | collective-permute-start | bytes 393224 | tf_op jit(solution)/shard_map/ppermute | solution.py:39
  22.0 6.6 %collective-permute-start.10 = (bf16[256,256]{1,0:T(8,128)(2,1)S(1)}, bf16[256,256]{1,0:T(8,128)(2,1)S(1)}, u32[]{:S(2)}, u32[]{:S(2)}) collective-permute-start(bf16[256,256]{1,0:T(8,128)(2,1)S(1)} %get-tuple-element.54), channel_id=1, source_target_pairs={{0,3},{1,2},{2,1},{3,0},{4,7},{5,6},{6,5},{7,4},{8,11},{9,10},{10,... | collective-permute-start | bytes 393224 | tf_op jit(solution)/shard_map/ppermute | solution.py:39
  22.0 13.1 %collective-permute-start.6 = (bf16[256,256]{1,0:T(8,128)(2,1)S(1)}, bf16[256,256]{1,0:T(8,128)(2,1)S(1)}, u32[]{:S(2)}, u32[]{:S(2)}) collective-permute-start(bf16[256,256]{1,0:T(8,128)(2,1)S(1)} %get-tuple-element.48), channel_id=1, source_target_pairs={{0,8},{4,12},{8,0},{12,4},{1,9},{5,13},{9,1},{13,5},{2,10},{6,14},... | collective-permute-start | bytes 393224 | tf_op jit(solution)/shard_map/ppermute | solution.py:39
  25.2 5.0 %collective-permute-start.12 = (f32[64,256]{1,0:T(8,128)S(1)}, f32[64,256]{1,0:T(8,128)S(1)}, u32[]{:S(2)}, u32[]{:S(2)}) collective-permute-start(f32[64,256]{1,0:T(8,128)S(1)} %get-tuple-element.58), channel_id=1, source_target_pairs={{0,2},{1,3},{2,0},{3,1},{4,6},{5,7},{6,4},{7,5},{8,10},{9,11},{10,... | collective-permute-start | bytes 196616 | tf_op jit(solution)/shard_map/ppermute | solution.py:35
  26.8 15.3 %collective-permute-start.7 = (bf16[256,256]{1,0:T(8,128)(2,1)S(1)}, bf16[256,256]{1,0:T(8,128)(2,1)S(1)}, u32[]{:S(2)}, u32[]{:S(2)}) collective-permute-start(bf16[256,256]{1,0:T(8,128)(2,1)S(1)} %get-tuple-element.49), channel_id=1, source_target_pairs={{0,12},{4,8},{8,4},{12,0},{1,13},{5,9},{9,5},{13,1},{2,14},{6,10},... | collective-permute-start | bytes 393224 | tf_op jit(solution)/shard_map/ppermute | solution.py:39
  27.2 14.8 %collective-permute-start.8 = (bf16[256,256]{1,0:T(8,128)(2,1)S(1)}, bf16[256,256]{1,0:T(8,128)(2,1)S(1)}, u32[]{:S(2)}, u32[]{:S(2)}) collective-permute-start(bf16[256,256]{1,0:T(8,128)(2,1)S(1)} %get-tuple-element.50), channel_id=1, source_target_pairs={{0,4},{4,0},{8,12},{12,8},{1,5},{5,1},{9,13},{13,9},{2,6},{6,2},{1... | collective-permute-start | bytes 393224 | tf_op jit(solution)/shard_map/ppermute | solution.py:39
  30.2 8.7 %collective-permute-start.15 = (bf16[64,256]{1,0:T(8,128)(2,1)S(1)}, bf16[64,256]{1,0:T(8,128)(2,1)S(1)}, u32[]{:S(2)}, u32[]{:S(2)}) collective-permute-start(bf16[64,256]{1,0:T(8,128)(2,1)S(1)} %shard_map.101.own_ref), channel_id=1, source_target_pairs={{0,4},{4,0},{8,12},{12,8},{1,5},{5,1},{9,13},{13,9},{2,6},{6,2},{1... | collective-permute-start | bytes 98312 | tf_op jit(solution)/shard_map/ppermute | solution.py:35
  31.6 7.3 %collective-permute-start.14 = (bf16[64,256]{1,0:T(8,128)(2,1)S(1)}, bf16[64,256]{1,0:T(8,128)(2,1)S(1)}, u32[]{:S(2)}, u32[]{:S(2)}) collective-permute-start(bf16[64,256]{1,0:T(8,128)(2,1)S(1)} %shard_map.101.own_ref), channel_id=1, source_target_pairs={{0,12},{4,8},{8,4},{12,0},{1,13},{5,9},{9,5},{13,1},{2,14},{6,10},... | collective-permute-start | bytes 98312 | tf_op jit(solution)/shard_map/ppermute | solution.py:35
  35.1 5.4 %collective-permute-start.13 = (bf16[64,256]{1,0:T(8,128)(2,1)S(1)}, bf16[64,256]{1,0:T(8,128)(2,1)S(1)}, u32[]{:S(2)}, u32[]{:S(2)}) collective-permute-start(bf16[64,256]{1,0:T(8,128)(2,1)S(1)} %shard_map.101.own_ref), channel_id=1, source_target_pairs={{0,8},{4,12},{8,0},{12,4},{1,9},{5,13},{9,1},{13,5},{2,10},{6,14},... | collective-permute-start | bytes 98312 | tf_op jit(solution)/shard_map/ppermute | solution.py:35
  35.1 9.8 %copy-start.3 = (s32[1,4,2]{1,2,0:T(2,128)S(1)}, s32[1,4,2]{1,2,0:T(2,128)}, u32[]{:S(2)}) copy-start(s32[1,4,2]{1,2,0:T(2,128)} %param.13) | copy-start | bytes 100
  35.1 9.8 %copy-start.4 = (s32[1,4,2]{1,2,0:T(2,128)S(1)}, s32[1,4,2]{1,2,0:T(2,128)}, u32[]{:S(2)}) copy-start(s32[1,4,2]{1,2,0:T(2,128)} %param.12) | copy-start | bytes 100
  40.5 4.3 %collective-permute-start.16 = (f32[64,256]{1,0:T(8,128)S(1)}, f32[64,256]{1,0:T(8,128)S(1)}, u32[]{:S(2)}, u32[]{:S(2)}) collective-permute-start(f32[64,256]{1,0:T(8,128)S(1)} %shard_map.102.own_ref), channel_id=1, source_target_pairs={{0,2},{1,3},{2,0},{3,1},{4,6},{5,7},{6,4},{7,5},{8,10},{9,11},{10,... | collective-permute-start | bytes 196616 | tf_op jit(solution)/shard_map/ppermute | solution.py:35
  44.9 2.2 %collective-permute-start.17 = (f32[128,256]{1,0:T(8,128)S(1)}, f32[128,256]{1,0:T(8,128)S(1)}, u32[]{:S(2)}, u32[]{:S(2)}) collective-permute-start(f32[128,256]{1,0:T(8,128)S(1)} %shard_map.103.own_ref), channel_id=1, source_target_pairs={{0,1},{1,0},{2,3},{3,2},{4,5},{5,4},{6,7},{7,6},{8,9},{9,8},{10,11... | collective-permute-start | bytes 393224 | tf_op jit(solution)/shard_map/ppermute | solution.py:35

commit v4 on v3

--- a/solution.py
+++ b/solution.py
@@ -263,11 +263,17 @@
     refs[-1][...] = tree_sum([terms[k][...].astype(F32) for k in range(ns)])
 
 
-def join_kernel(bit, own_ref, load_ref, *refs):
-    rows = own_ref.shape[0]
-    mine = (lax.axis_index("dom") >> bit) & 1
-    refs[-1][pl.ds(pl.multiple_of(mine * rows, 8), rows), :] = own_ref[...]
-    refs[-1][pl.ds(pl.multiple_of((1 - mine) * rows, 8), rows), :] = load_ref[...]
+def owned_piece(index, nd):
+    bits = nd.bit_length() - 1
+    return sum(((index >> bit) & 1) << (bits - 1 - bit) for bit in range(bits))
+
+
+def place_kernel(nd, *refs):
+    p = lax.axis_index("dom")
+    rows = refs[0].shape[0]
+    for ref, k in zip(refs, [0] + exchange_order(nd)):
+        at = pl.multiple_of(owned_piece(partner(p, k, nd), nd) * rows, 8)
+        refs[-1][pl.ds(at, rows), :] = ref[...]
 
 
 def spread_kernel(
@@ -328,7 +334,7 @@
         store.wait()
 
 
-GATES = {"last": [("dom", 2), ("dom", 3), ("dom", 1)], "shard": [("shard", 2)], "join": [("shard", 3), ("shard", 1)], "place": []}
+GATES = {"last": [("dom", 1), ("dom", 2), ("dom", 3)], "shard": ["part", ("shard", 2), ("shard", 3), ("shard", 1)], "place": ["finish"]}
 
 
 def on_device(features, weight, cotangent, block_values, block_list, send_inner, send_outer):
@@ -418,8 +424,19 @@
     back.update({("dom", k): x for k, x in zip(outer_order, outer_back)})
     sizes = {"shard": ns, "dom": nd}
 
+    grad_features = call(
+        functools.partial(finish_kernel, list(back), sizes, side), rows_f32,
+        6 * node_count * width * width, 4 * nbytes, [ANY] * 2 + [VMEM] * (2 + len(back)), HBM,
+        [
+            pltpu.VMEM((node_count, width), F32), pltpu.VMEM((node_count, width), F32), inner_table, outer_table,
+            pltpu.SemaphoreType.DMA((2 + row_blocks,)),
+        ],
+    )(inner_targets, outer_targets, part, weight, *back.values())
+    back["part"] = part
+    back["finish"] = keep(grad_features)
+
     def stage(kernel, name, inputs, rows, dtype=F32):
-        gated = [back[item] for item in GATES[name] if item in back] + [part] * (name == "shard")
+        gated = [back[item] for item in GATES.get(name, ()) if item in back]
         return call(
             kernel, shape((rows, width), dtype), 0, nbytes // 4,
             [VMEM] * len(inputs) + [ANY] * len(gated), VMEM,
@@ -440,20 +457,8 @@
         load = send(give, "dom", 2 << bit, nd)
     pieces = [piece] + [send(piece, "shard", k, ns) for k in inner_order]
     weight_sum = stage(functools.partial(shard_sum_kernel, ns), "shard", pieces, count)
-    for bit in reversed(range(bits)):
-        count *= 2
-        load = send(weight_sum, "dom", 1 << bit, nd)
-        weight_sum = stage(
-            functools.partial(join_kernel, bit), "join" if bit == 1 else "place", [weight_sum, load], count
-        )
-    grad_features = call(
-        functools.partial(finish_kernel, list(back), sizes, side), rows_f32,
-        6 * node_count * width * width, 4 * nbytes, [ANY] * 2 + [VMEM] * (2 + len(back)), HBM,
-        [
-            pltpu.VMEM((node_count, width), F32), pltpu.VMEM((node_count, width), F32), inner_table, outer_table,
-            pltpu.SemaphoreType.DMA((2 + row_blocks,)),
-        ],
-    )(inner_targets, outer_targets, part, weight, *back.values())
+    pieces = [weight_sum] + [send(weight_sum, "dom", k, nd) for k in outer_order]
+    weight_sum = stage(functools.partial(place_kernel, nd), "place", pieces, width)
     grad_weight = weight_sum
     return (activations, grad_features, grad_weight)
 

time: 48 us -> 47.3 us (0.985)
  waiting for transfers between devices: 12 us -> 10.9 us
    ppermute x12 -> x13, waiting for transfers between devices: 10.9 us -> 9.88 us  [send(): return lax.ppermute(x, axis, [(i, partner(i, k, n)) for i in range(n)])]
    ppermute x12 -> x13, starting transfers between devices: 15.1 us -> 16 us  [send(): return lax.ppermute(x, axis, [(i, partner(i, k, n)) for i in range(n)])]
  transfers between devices with their start and end apart: 18 -> 19, of which waited for: 9 -> 9; matrix products, arithmetic and copies ran while one was open for 0% -> 0% of each run, Pallas kernels for 19% -> 19%
where the time goes in v4:
time: 47.3 us; the launch traced here: 47.2 us
  starting transfers between devices  21.8 us (46%)
  Pallas kernels  13.7 us (29%)
  waiting for transfers between devices  10.9 us (23%)
  between operations  0.79 us (2%)
    ppermute x13, starting transfers between devices, send(): return lax.ppermute(x, axis, [(i, partner(i, k, n)) for i in range(n)])  16 us
    ppermute x13, waiting for transfers between devices, send(): return lax.ppermute(x, axis, [(i, partner(i, k, n)) for i in range(n)])  9.88 us
    ppermute x6, starting transfers between devices, send_back(): return lax.ppermute(x, axis, [(i, back_partner(i, k, n)) for i in range(n)])  5.82 us
    pallas_call x1, Pallas kernels, on_device(): call(functools.partial(local_kernel, dims), [packed_outer[-1], rows_f32,...  4.52 us
    pallas_call x1, Pallas kernels, on_device(): call(functools.partial(spread_kernel, dims[:4]), [rows_f32, rows_f32], 2...  2.43 us
    pallas_call x1, Pallas kernels, on_device(): call(functools.partial(finish_kernel, list(back), sizes, side), rows_f32,...  2.09 us
    pallas_call x1, Pallas kernels, on_device(): call(functools.partial(middle_kernel, dims), [rows_f32, rows_f32, rows_f1...  1.46 us
    pallas_call x1, Pallas kernels, on_device(): call(functools.partial(pack_kernel, ns, nd, side), packed_inner + packed_...  1.2 us
  transfers between devices with their start and end apart: 19, of which 9 were waited for; matrix products, arithmetic and copies ran while one was open for 0% of the time, Pallas kernels for 19%

profile of v4, /device:TPU:0, one launch (start us, length us, event | category | flops | bytes accessed | tf_op | source)
XLA Modules:
  0.0 47.2 jit_solution(16652413087090115243)
XLA Ops:
  0.6 1.2 %shard_map.95 = (bf16[256,256]{1,0:T(8,128)(2,1)S(1)}, bf16[256,256]{1,0:T(8,128)(2,1)S(1)}, bf16[256,256]{1,0:T(8,128)(2,1)S(1)}, bf16[256,256]{1,0:T(8,128)(2,1)S(1)}, bf16[256,256]{1,0:T(8,128)(2,1)S(1)}) custom-call(s32[1,2,4]{2,1,0:T(2,128)} %bitcast.5, s32[1,2,4]{2,1,0:T(2,128)} %bitcast.2, f32[512,256]{1,0:T(8,128)} %features_ref.1), custom_call_target="tpu_custom_call" | custom-call | bytes 1572864 | tf_op jit(solution)/shard_map/pallas_call | solution.py:364
  1.8 4.1 %collective-permute-start = (bf16[256,256]{1,0:T(8,128)(2,1)S(1)}, bf16[256,256]{1,0:T(8,128)(2,1)S(1)}, u32[]{:S(2)}, u32[]{:S(2)}) collective-permute-start(bf16[256,256]{1,0:T(8,128)(2,1)S(1)} %get-tuple-element.33), channel_id=1, source_target_pairs={{0,8},{4,12},{8,0},{12,4},{1,9},{5,13},{9,1},{13,5},{2,10},{6,14},... | collective-permute-start | bytes 393224 | tf_op jit(solution)/shard_map/ppermute | solution.py:35
  5.9 1.3 %collective-permute-start.1 = (bf16[256,256]{1,0:T(8,128)(2,1)S(1)}, bf16[256,256]{1,0:T(8,128)(2,1)S(1)}, u32[]{:S(2)}, u32[]{:S(2)}) collective-permute-start(bf16[256,256]{1,0:T(8,128)(2,1)S(1)} %get-tuple-element.34), channel_id=1, source_target_pairs={{0,12},{4,8},{8,4},{12,0},{1,13},{5,9},{9,5},{13,1},{2,14},{6,10},... | collective-permute-start | bytes 393224 | tf_op jit(solution)/shard_map/ppermute | solution.py:35
  7.5 1.5 %collective-permute-start.3 = (bf16[256,256]{1,0:T(8,128)(2,1)S(1)}, bf16[256,256]{1,0:T(8,128)(2,1)S(1)}, u32[]{:S(2)}, u32[]{:S(2)}) collective-permute-start(bf16[256,256]{1,0:T(8,128)(2,1)S(1)} %get-tuple-element.36), channel_id=1, source_target_pairs={{0,2},{1,3},{2,0},{3,1},{4,6},{5,7},{6,4},{7,5},{8,10},{9,11},{10,... | collective-permute-start | bytes 393224 | tf_op jit(solution)/shard_map/ppermute | solution.py:35
  9.0 4.5 %shard_map.94 = (bf16[256,256]{1,0:T(8,128)(2,1)S(1)}, f32[512,256]{1,0:T(8,128)S(1)}, f32[512,256]{1,0:T(8,128)S(1)}, f32[512,256]{1,0:T(8,128)S(1)}, bf16[12,1...) custom-call(s32[4,16]{1,0:T(4,128)} %list_any.1, ...), custom_call_target="tpu_custom_call" | custom-call | flops 3221225472 | bytes 6291456 | tf_op jit(solution)/shard_map/pallas_call | solution.py:372
  13.6 2.4 %collective-permute-done.refs_0_ = bf16[256,256]{1,0:T(8,128)(2,1)S(1)} collective-permute-done((bf16[256,256]{1,0:T(8,128)(2,1)S(1)}, bf16[256,256]{1,0:T(8,128)(2,1)S(1)}, u32[]{:S(2)}, u32[]{:S(2)}) %collective-permute-start) | collective-permute-done | bytes 131104 | tf_op jit(solution)/shard_map/ppermute | solution.py:35
  15.9 0.5 %collective-permute-done.2.refs_2_ = bf16[256,256]{1,0:T(8,128)(2,1)S(1)} collective-permute-done((bf16[256,256]{1,0:T(8,128)(2,1)S(1)}, bf16[256,256]{1,0:T(8,128)(2,1)S(1)}, u32[]{:S(2)}, u32[]{:S(2)}) %collective-permute-start.2) | collective-permute-done | bytes 131104 | tf_op jit(solution)/shard_map/ppermute | solution.py:35
  16.4 0.8 %collective-permute-done.5.refs_5_ = bf16[256,256]{1,0:T(8,128)(2,1)S(1)} collective-permute-done((bf16[256,256]{1,0:T(8,128)(2,1)S(1)}, bf16[256,256]{1,0:T(8,128)(2,1)S(1)}, u32[]{:S(2)}, u32[]{:S(2)}) %collective-permute-start.5) | collective-permute-done | bytes 131104 | tf_op jit(solution)/shard_map/ppermute | solution.py:35
  17.3 1.5 %shard_map.96 = (f32[512,256]{1,0:T(8,128)S(1)}, f32[512,256]{1,0:T(8,128)S(1)}, bf16[512,256]{1,0:T(8,128)(2,1)S(1)}, f32[512,256]{1,0:T(8,128)S(1)}, bf16[256,...) custom-call(s32[12]{0:T(128)S(1)} %get-tuple-element.32.place_any, ...), custom_call_target="tpu_custom_call" | custom-call | flops 201326592 | bytes 4194304 | tf_op jit(solution)/shard_map/pallas_call | solution.py:391
  18.8 1.2 %shard_map.98 = (f32[128,256]{1,0:T(8,128)S(1)}, bf16[256,256]{1,0:T(8,128)(2,1)S(1)}, bf16[256,256]{1,0:T(8,128)(2,1)S(1)}, bf16[512,256]{1,0:T(8,128)(2,1)S(1)}) custom-call(s32[12]{0:T(128)S(1)} %get-tuple-element.32.place_any, f32[512,256]{1,0:T(8,128)S(1)} %copy-done, f32[512,256]{1,0:T(8,128)S(1)} %get-tuple-element.51.local_ref, ...), custom_call_target="tpu_custom_call" | custom-call | flops 335544320 | bytes 2621440 | tf_op jit(solution)/shard_map/pallas_call | solution.py:402
  20.2 1.9 %collective-permute-start.9 = (bf16[256,256]{1,0:T(8,128)(2,1)S(1)}, bf16[256,256]{1,0:T(8,128)(2,1)S(1)}, u32[]{:S(2)}, u32[]{:S(2)}) collective-permute-start(bf16[256,256]{1,0:T(8,128)(2,1)S(1)} %get-tuple-element.53), channel_id=1, source_target_pairs={{0,2},{1,3},{2,0},{3,1},{4,6},{5,7},{6,4},{7,5},{8,10},{9,11},{10,... | collective-permute-start | bytes 393224 | tf_op jit(solution)/shard_map/ppermute | solution.py:39
  22.0 3.2 %collective-permute-start.6 = (bf16[256,256]{1,0:T(8,128)(2,1)S(1)}, bf16[256,256]{1,0:T(8,128)(2,1)S(1)}, u32[]{:S(2)}, u32[]{:S(2)}) collective-permute-start(bf16[256,256]{1,0:T(8,128)(2,1)S(1)} %get-tuple-element.48), channel_id=1, source_target_pairs={{0,8},{4,12},{8,0},{12,4},{1,9},{5,13},{9,1},{13,5},{2,10},{6,14},... | collective-permute-start | bytes 393224 | tf_op jit(solution)/shard_map/ppermute | solution.py:39
  25.8 0.7 %collective-permute-done.9.refs_3_.refs_1_ = bf16[256,256]{1,0:T(8,128)(2,1)S(1)} collective-permute-done((bf16[256,256]{1,0:T(8,128)(2,1)S(1)}, bf16[256,256]{1,0:T(8,128)(2,1)S(1)}, u32[]{:S(2)}, u32[]{:S(2)}) %collective-permute-start.9) | collective-permute-done | bytes 131104 | tf_op jit(solution)/shard_map/ppermute | solution.py:39
  26.5 1.8 %collective-permute-start.12 = (f32[64,256]{1,0:T(8,128)S(1)}, f32[64,256]{1,0:T(8,128)S(1)}, u32[]{:S(2)}, u32[]{:S(2)}) collective-permute-start(f32[64,256]{1,0:T(8,128)S(1)} %get-tuple-element.58), channel_id=1, source_target_pairs={{0,2},{1,3},{2,0},{3,1},{4,6},{5,7},{6,4},{7,5},{8,10},{9,11},{10,... | collective-permute-start | bytes 196616 | tf_op jit(solution)/shard_map/ppermute | solution.py:35
  28.7 2.1 %collective-permute-done.12.load_ref = f32[64,256]{1,0:T(8,128)S(1)} collective-permute-done((f32[64,256]{1,0:T(8,128)S(1)}, f32[64,256]{1,0:T(8,128)S(1)}, u32[]{:S(2)}, u32[]{:S(2)}) %collective-permute-start.12) | collective-permute-done | bytes 65568 | tf_op jit(solution)/shard_map/ppermute | solution.py:35
  30.8 1.4 %collective-permute-start.15 = (bf16[64,256]{1,0:T(8,128)(2,1)S(1)}, bf16[64,256]{1,0:T(8,128)(2,1)S(1)}, u32[]{:S(2)}, u32[]{:S(2)}) collective-permute-start(bf16[64,256]{1,0:T(8,128)(2,1)S(1)} %shard_map.101.own_ref), channel_id=1, source_target_pairs={{0,4},{4,0},{8,12},{12,8},{1,5},{5,1},{9,13},{13,9},{2,6},{6,2},{1... | collective-permute-start | bytes 98312 | tf_op jit(solution)/shard_map/ppermute | solution.py:35
  32.1 3.4 %collective-permute-start.14 = (bf16[64,256]{1,0:T(8,128)(2,1)S(1)}, bf16[64,256]{1,0:T(8,128)(2,1)S(1)}, u32[]{:S(2)}, u32[]{:S(2)}) collective-permute-start(bf16[64,256]{1,0:T(8,128)(2,1)S(1)} %shard_map.101.own_ref), channel_id=1, source_target_pairs={{0,12},{4,8},{8,4},{12,0},{1,13},{5,9},{9,5},{13,1},{2,14},{6,10},... | collective-permute-start | bytes 98312 | tf_op jit(solution)/shard_map/ppermute | solution.py:35
  35.5 2.4 %shard_map.97 = (f32[512,256]{1,0:T(8,128)}, f32[512,256]{1,0:T(8,128)S(1)}) custom-call(s32[4,16]{1,0:T(4,128)S(1)} %copy-done.5, bf16[4,16,128,128]{3,2,1,0:T(8,128)(2,1)S(1)} %get-tuple-element.31.values_ref, f32[512,256]{1,0:T(8,128)S(1)} %get-tuple-element.43.mixed_ref, f32[512,256]{1,0:T(8,128)S(1)} %get-tuple-element.44.scaled_ref, ...), custom_call_target="tpu_custom_call" | custom-call | flops 536870912 | bytes 4194304 | tf_op jit(solution)/shard_map/pallas_call | solution.py:413
  38.2 2.3 %collective-permute-done.13.refs_0_ = bf16[64,256]{1,0:T(8,128)(2,1)S(1)} collective-permute-done((bf16[64,256]{1,0:T(8,128)(2,1)S(1)}, bf16[64,256]{1,0:T(8,128)(2,1)S(1)}, u32[]{:S(2)}, u32[]{:S(2)}) %collective-permute-start.13) | collective-permute-done | bytes 32800 | tf_op jit(solution)/shard_map/ppermute | solution.py:35
  40.6 1.6 %collective-permute-start.17 = (f32[64,256]{1,0:T(8,128)S(1)}, f32[64,256]{1,0:T(8,128)S(1)}, u32[]{:S(2)}, u32[]{:S(2)}) collective-permute-start(f32[64,256]{1,0:T(8,128)S(1)} %shard_map.102.refs_0_), channel_id=1, source_target_pairs={{0,3},{1,2},{2,1},{3,0},{4,7},{5,6},{6,5},{7,4},{8,11},{9,10},{10,... | collective-permute-start | bytes 196616 | tf_op jit(solution)/shard_map/ppermute | solution.py:35
  42.2 0.5 %collective-permute-start.16 = (f32[64,256]{1,0:T(8,128)S(1)}, f32[64,256]{1,0:T(8,128)S(1)}, u32[]{:S(2)}, u32[]{:S(2)}) collective-permute-start(f32[64,256]{1,0:T(8,128)S(1)} %shard_map.102.refs_0_), channel_id=1, source_target_pairs={{0,2},{1,3},{2,0},{3,1},{4,6},{5,7},{6,4},{7,5},{8,10},{9,11},{10,... | collective-permute-start | bytes 196616 | tf_op jit(solution)/shard_map/ppermute | solution.py:35
  42.7 2.1 %shard_map.99.refs_4_ = f32[512,256]{1,0:T(8,128)} custom-call(s32[1,2,4]{2,1,0:T(2,128)S(1)} %bitcast.6, s32[1,2,4]{2,1,0:T(2,128)S(1)} %bitcast.4, f32[512,256]{1,0:T(8,128)S(1)} %get-tuple-element.47.part_ref.refs_3_, f32[256,256]{1,0:T(8,128)S(1)} %copy-done.1, bf16[256,256]{1,0:T(8,128)(2,1)S(1)} %collective-permute-done.6.refs_0_.refs_4_, ...), custom_call_target="tpu_custom_call" | custom-call | flops 201326592 | bytes 2097152 | tf_op jit(solution)/shard_map/pallas_call | solution.py:427
  44.9 1.6 %collective-permute-done.16.refs_1_ = f32[64,256]{1,0:T(8,128)S(1)} collective-permute-done((f32[64,256]{1,0:T(8,128)S(1)}, f32[64,256]{1,0:T(8,128)S(1)}, u32[]{:S(2)}, u32[]{:S(2)}) %collective-permute-start.16) | collective-permute-done | bytes 65568 | tf_op jit(solution)/shard_map/ppermute | solution.py:35
  46.5 0.7 %shard_map.103 = f32[256,256]{1,0:T(8,128)} custom-call(f32[64,256]{1,0:T(8,128)S(1)} %shard_map.102.refs_0_, f32[64,256]{1,0:T(8,128)S(1)} %collective-permute-done.16.refs_1_, f32[64,256]{1,0:T(8,128)S(1)} %collective-permute-done.17.refs_2_, f32[64,256]{1,0:T(8,128)S(1)} %collective-permute-done.18.refs_3_, f32[512,256]{1,0:T(8,128)} %shard_map.99.refs_4_), custom_call_target="tpu_custom_call" | custom-call | bytes 131072 | tf_op jit(solution)/shard_map/pallas_call | solution.py:440
  (36 shorter events, 1.7 us)
Async XLA Ops:
  1.8 14.1 %collective-permute-start = (bf16[256,256]{1,0:T(8,128)(2,1)S(1)}, bf16[256,256]{1,0:T(8,128)(2,1)S(1)}, u32[]{:S(2)}, u32[]{:S(2)}) collective-permute-start(bf16[256,256]{1,0:T(8,128)(2,1)S(1)} %get-tuple-element.33), channel_id=1, source_target_pairs={{0,8},{4,12},{8,0},{12,4},{1,9},{5,13},{9,1},{13,5},{2,10},{6,14},... | collective-permute-start | bytes 393224 | tf_op jit(solution)/shard_map/ppermute | solution.py:35
  5.9 10.0 %collective-permute-start.1 = (bf16[256,256]{1,0:T(8,128)(2,1)S(1)}, bf16[256,256]{1,0:T(8,128)(2,1)S(1)}, u32[]{:S(2)}, u32[]{:S(2)}) collective-permute-start(bf16[256,256]{1,0:T(8,128)(2,1)S(1)} %get-tuple-element.34), channel_id=1, source_target_pairs={{0,12},{4,8},{8,4},{12,0},{1,13},{5,9},{9,5},{13,1},{2,14},{6,10},... | collective-permute-start | bytes 393224 | tf_op jit(solution)/shard_map/ppermute | solution.py:35
  7.3 9.2 %collective-permute-start.2 = (bf16[256,256]{1,0:T(8,128)(2,1)S(1)}, bf16[256,256]{1,0:T(8,128)(2,1)S(1)}, u32[]{:S(2)}, u32[]{:S(2)}) collective-permute-start(bf16[256,256]{1,0:T(8,128)(2,1)S(1)} %get-tuple-element.35), channel_id=1, source_target_pairs={{0,4},{4,0},{8,12},{12,8},{1,5},{5,1},{9,13},{13,9},{2,6},{6,2},{1... | collective-permute-start | bytes 393224 | tf_op jit(solution)/shard_map/ppermute | solution.py:35
  7.5 8.9 %collective-permute-start.3 = (bf16[256,256]{1,0:T(8,128)(2,1)S(1)}, bf16[256,256]{1,0:T(8,128)(2,1)S(1)}, u32[]{:S(2)}, u32[]{:S(2)}) collective-permute-start(bf16[256,256]{1,0:T(8,128)(2,1)S(1)} %get-tuple-element.36), channel_id=1, source_target_pairs={{0,2},{1,3},{2,0},{3,1},{4,6},{5,7},{6,4},{7,5},{8,10},{9,11},{10,... | collective-permute-start | bytes 393224 | tf_op jit(solution)/shard_map/ppermute | solution.py:35
  9.0 8.3 %copy-start.1 = (f32[256,256]{1,0:T(8,128)S(1)}, f32[256,256]{1,0:T(8,128)}, u32[]{:S(2)}) copy-start(f32[256,256]{1,0:T(8,128)} %weight_ref.1) | copy-start | bytes 786436
  9.0 8.3 %copy-start.2 = (f32[512,256]{1,0:T(8,128)S(1)}, f32[512,256]{1,0:T(8,128)}, u32[]{:S(2)}) copy-start(f32[512,256]{1,0:T(8,128)} %refs_11_.1) | copy-start | bytes 1572868
  9.0 7.4 %collective-permute-start.4 = (bf16[256,256]{1,0:T(8,128)(2,1)S(1)}, bf16[256,256]{1,0:T(8,128)(2,1)S(1)}, u32[]{:S(2)}, u32[]{:S(2)}) collective-permute-start(bf16[256,256]{1,0:T(8,128)(2,1)S(1)} %get-tuple-element.37), channel_id=1, source_target_pairs={{0,3},{1,2},{2,1},{3,0},{4,7},{5,6},{6,5},{7,4},{8,11},{9,10},{10,... | collective-permute-start | bytes 393224 | tf_op jit(solution)/shard_map/ppermute | solution.py:35
  15.9 1.3 %collective-permute-start.5 = (bf16[256,256]{1,0:T(8,128)(2,1)S(1)}, bf16[256,256]{1,0:T(8,128)(2,1)S(1)}, u32[]{:S(2)}, u32[]{:S(2)}) collective-permute-start(bf16[256,256]{1,0:T(8,128)(2,1)S(1)} %get-tuple-element.38), channel_id=1, source_target_pairs={{0,1},{1,0},{2,3},{3,2},{4,5},{5,4},{6,7},{7,6},{8,9},{9,8},{10,11... | collective-permute-start | bytes 393224 | tf_op jit(solution)/shard_map/ppermute | solution.py:35
  18.7 16.8 %copy-start.5 = (s32[4,16]{1,0:T(4,128)S(1)}, s32[4,16]{1,0:T(4,128)}, u32[]{:S(2)}) copy-start(s32[4,16]{1,0:T(4,128)} %list_any.1) | copy-start | bytes 772
  19.9 5.7 %collective-permute-start.11 = (bf16[512,256]{1,0:T(8,128)(2,1)S(1)}, bf16[512,256]{1,0:T(8,128)(2,1)S(1)}, u32[]{:S(2)}, u32[]{:S(2)}) collective-permute-start(bf16[512,256]{1,0:T(8,128)(2,1)S(1)} %get-tuple-element.55), channel_id=1, source_target_pairs={{0,1},{1,0},{2,3},{3,2},{4,5},{5,4},{6,7},{7,6},{8,9},{9,8},{10,11... | collective-permute-start | bytes 786440 | tf_op jit(solution)/shard_map/ppermute | solution.py:39
  20.2 6.3 %collective-permute-start.9 = (bf16[256,256]{1,0:T(8,128)(2,1)S(1)}, bf16[256,256]{1,0:T(8,128)(2,1)S(1)}, u32[]{:S(2)}, u32[]{:S(2)}) collective-permute-start(bf16[256,256]{1,0:T(8,128)(2,1)S(1)} %get-tuple-element.53), channel_id=1, source_target_pairs={{0,2},{1,3},{2,0},{3,1},{4,6},{5,7},{6,4},{7,5},{8,10},{9,11},{10,... | collective-permute-start | bytes 393224 | tf_op jit(solution)/shard_map/ppermute | solution.py:39
  22.0 6.6 %collective-permute-start.10 = (bf16[256,256]{1,0:T(8,128)(2,1)S(1)}, bf16[256,256]{1,0:T(8,128)(2,1)S(1)}, u32[]{:S(2)}, u32[]{:S(2)}) collective-permute-start(bf16[256,256]{1,0:T(8,128)(2,1)S(1)} %get-tuple-element.54), channel_id=1, source_target_pairs={{0,3},{1,2},{2,1},{3,0},{4,7},{5,6},{6,5},{7,4},{8,11},{9,10},{10,... | collective-permute-start | bytes 393224 | tf_op jit(solution)/shard_map/ppermute | solution.py:39
  22.0 13.5 %collective-permute-start.6 = (bf16[256,256]{1,0:T(8,128)(2,1)S(1)}, bf16[256,256]{1,0:T(8,128)(2,1)S(1)}, u32[]{:S(2)}, u32[]{:S(2)}) collective-permute-start(bf16[256,256]{1,0:T(8,128)(2,1)S(1)} %get-tuple-element.48), channel_id=1, source_target_pairs={{0,8},{4,12},{8,0},{12,4},{1,9},{5,13},{9,1},{13,5},{2,10},{6,14},... | collective-permute-start | bytes 393224 | tf_op jit(solution)/shard_map/ppermute | solution.py:39
  25.2 12.8 %collective-permute-start.7 = (bf16[256,256]{1,0:T(8,128)(2,1)S(1)}, bf16[256,256]{1,0:T(8,128)(2,1)S(1)}, u32[]{:S(2)}, u32[]{:S(2)}) collective-permute-start(bf16[256,256]{1,0:T(8,128)(2,1)S(1)} %get-tuple-element.49), channel_id=1, source_target_pairs={{0,12},{4,8},{8,4},{12,0},{1,13},{5,9},{9,5},{13,1},{2,14},{6,10},... | collective-permute-start | bytes 393224 | tf_op jit(solution)/shard_map/ppermute | solution.py:39
  25.7 12.3 %collective-permute-start.8 = (bf16[256,256]{1,0:T(8,128)(2,1)S(1)}, bf16[256,256]{1,0:T(8,128)(2,1)S(1)}, u32[]{:S(2)}, u32[]{:S(2)}) collective-permute-start(bf16[256,256]{1,0:T(8,128)(2,1)S(1)} %get-tuple-element.50), channel_id=1, source_target_pairs={{0,4},{4,0},{8,12},{12,8},{1,5},{5,1},{9,13},{13,9},{2,6},{6,2},{1... | collective-permute-start | bytes 393224 | tf_op jit(solution)/shard_map/ppermute | solution.py:39
  26.5 4.3 %collective-permute-start.12 = (f32[64,256]{1,0:T(8,128)S(1)}, f32[64,256]{1,0:T(8,128)S(1)}, u32[]{:S(2)}, u32[]{:S(2)}) collective-permute-start(f32[64,256]{1,0:T(8,128)S(1)} %get-tuple-element.58), channel_id=1, source_target_pairs={{0,2},{1,3},{2,0},{3,1},{4,6},{5,7},{6,4},{7,5},{8,10},{9,11},{10,... | collective-permute-start | bytes 196616 | tf_op jit(solution)/shard_map/ppermute | solution.py:35
  30.8 7.3 %collective-permute-start.15 = (bf16[64,256]{1,0:T(8,128)(2,1)S(1)}, bf16[64,256]{1,0:T(8,128)(2,1)S(1)}, u32[]{:S(2)}, u32[]{:S(2)}) collective-permute-start(bf16[64,256]{1,0:T(8,128)(2,1)S(1)} %shard_map.101.own_ref), channel_id=1, source_target_pairs={{0,4},{4,0},{8,12},{12,8},{1,5},{5,1},{9,13},{13,9},{2,6},{6,2},{1... | collective-permute-start | bytes 98312 | tf_op jit(solution)/shard_map/ppermute | solution.py:35
  32.1 6.1 %collective-permute-start.14 = (bf16[64,256]{1,0:T(8,128)(2,1)S(1)}, bf16[64,256]{1,0:T(8,128)(2,1)S(1)}, u32[]{:S(2)}, u32[]{:S(2)}) collective-permute-start(bf16[64,256]{1,0:T(8,128)(2,1)S(1)} %shard_map.101.own_ref), channel_id=1, source_target_pairs={{0,12},{4,8},{8,4},{12,0},{1,13},{5,9},{9,5},{13,1},{2,14},{6,10},... | collective-permute-start | bytes 98312 | tf_op jit(solution)/shard_map/ppermute | solution.py:35
  35.5 5.0 %collective-permute-start.13 = (bf16[64,256]{1,0:T(8,128)(2,1)S(1)}, bf16[64,256]{1,0:T(8,128)(2,1)S(1)}, u32[]{:S(2)}, u32[]{:S(2)}) collective-permute-start(bf16[64,256]{1,0:T(8,128)(2,1)S(1)} %shard_map.101.own_ref), channel_id=1, source_target_pairs={{0,8},{4,12},{8,0},{12,4},{1,9},{5,13},{9,1},{13,5},{2,10},{6,14},... | collective-permute-start | bytes 98312 | tf_op jit(solution)/shard_map/ppermute | solution.py:35
  35.5 7.2 %copy-start.3 = (s32[1,4,2]{1,2,0:T(2,128)S(1)}, s32[1,4,2]{1,2,0:T(2,128)}, u32[]{:S(2)}) copy-start(s32[1,4,2]{1,2,0:T(2,128)} %param.13) | copy-start | bytes 100
  35.5 7.2 %copy-start.4 = (s32[1,4,2]{1,2,0:T(2,128)S(1)}, s32[1,4,2]{1,2,0:T(2,128)}, u32[]{:S(2)}) copy-start(s32[1,4,2]{1,2,0:T(2,128)} %param.12) | copy-start | bytes 100
  40.5 4.3 %collective-permute-start.18 = (f32[64,256]{1,0:T(8,128)S(1)}, f32[64,256]{1,0:T(8,128)S(1)}, u32[]{:S(2)}, u32[]{:S(2)}) collective-permute-start(f32[64,256]{1,0:T(8,128)S(1)} %shard_map.102.refs_0_), channel_id=1, source_target_pairs={{0,1},{1,0},{2,3},{3,2},{4,5},{5,4},{6,7},{7,6},{8,9},{9,8},{10,11... | collective-permute-start | bytes 196616 | tf_op jit(solution)/shard_map/ppermute | solution.py:35
  40.6 4.3 %collective-permute-start.17 = (f32[64,256]{1,0:T(8,128)S(1)}, f32[64,256]{1,0:T(8,128)S(1)}, u32[]{:S(2)}, u32[]{:S(2)}) collective-permute-start(f32[64,256]{1,0:T(8,128)S(1)} %shard_map.102.refs_0_), channel_id=1, source_target_pairs={{0,3},{1,2},{2,1},{3,0},{4,7},{5,6},{6,5},{7,4},{8,11},{9,10},{10,... | collective-permute-start | bytes 196616 | tf_op jit(solution)/shard_map/ppermute | solution.py:35
  42.2 4.3 %collective-permute-start.16 = (f32[64,256]{1,0:T(8,128)S(1)}, f32[64,256]{1,0:T(8,128)S(1)}, u32[]{:S(2)}, u32[]{:S(2)}) collective-permute-start(f32[64,256]{1,0:T(8,128)S(1)} %shard_map.102.refs_0_), channel_id=1, source_target_pairs={{0,2},{1,3},{2,0},{3,1},{4,6},{5,7},{6,4},{7,5},{8,10},{9,11},{10,... | collective-permute-start | bytes 196616 | tf_op jit(solution)/shard_map/ppermute | solution.py:35
  (1 other events, 5.2 us)

commit v5 on v4

--- a/solution.py
+++ b/solution.py
@@ -28,7 +28,7 @@
 
 
 def exchange_order(n):
-    return sorted(range(1, n), key=lambda k: (k == 1, k))
+    return sorted(range(1, n), key=lambda k: -k)
 
 
 def send(x, axis, k, n):
@@ -334,7 +334,7 @@
         store.wait()
 
 
-GATES = {"last": [("dom", 1), ("dom", 2), ("dom", 3)], "shard": ["part", ("shard", 2), ("shard", 3), ("shard", 1)], "place": ["finish"]}
+GATES = {'last': [('dom', 1), ('dom', 2), ('dom', 3), 'part'], 'shard': [('shard', 2), ('shard', 3), ('shard', 1)], 'place': ['finish']}
 
 
 def on_device(features, weight, cotangent, block_values, block_list, send_inner, send_outer):

time: 47.3 us -> 47.2 us (level)
  waiting for transfers between devices: 10.9 us -> 10.3 us
  starting transfers between devices: 21.8 us -> 22.3 us
    ppermute x6, starting transfers between devices: 5.82 us -> 6.6 us  [send_back(): return lax.ppermute(x, axis, [(i, back_partner(i, k, n)) for i in range(n)])]
  transfers between devices with their start and end apart: 19 -> 19, of which waited for: 9 -> 7; matrix products, arithmetic and copies ran while one was open for 0% -> 0% of each run, Pallas kernels for 19% -> 19%
where the time goes in v5:
time: 47.2 us; the launch traced here: 47 us
  starting transfers between devices  22.3 us (47%)
  Pallas kernels  13.6 us (29%)
  waiting for transfers between devices  10.3 us (22%)
  between operations  0.8 us (2%)
    ppermute x13, starting transfers between devices, send(): return lax.ppermute(x, axis, [(i, partner(i, k, n)) for i in range(n)])  15.7 us
    ppermute x13, waiting for transfers between devices, send(): return lax.ppermute(x, axis, [(i, partner(i, k, n)) for i in range(n)])  9.58 us
    ppermute x6, starting transfers between devices, send_back(): return lax.ppermute(x, axis, [(i, back_partner(i, k, n)) for i in range(n)])  6.6 us
    pallas_call x1, Pallas kernels, on_device(): call(functools.partial(local_kernel, dims), [packed_outer[-1], rows_f32,...  4.45 us
    pallas_call x1, Pallas kernels, on_device(): call(functools.partial(spread_kernel, dims[:4]), [rows_f32, rows_f32], 2...  2.42 us
    pallas_call x1, Pallas kernels, on_device(): call(functools.partial(finish_kernel, list(back), sizes, side), rows_f32,...  2.08 us
    pallas_call x1, Pallas kernels, on_device(): call(functools.partial(middle_kernel, dims), [rows_f32, rows_f32, rows_f1...  1.48 us
    pallas_call x1, Pallas kernels, on_device(): call(functools.partial(pack_kernel, ns, nd, side), packed_inner + packed_...  1.2 us
  transfers between devices with their start and end apart: 19, of which 7 were waited for; matrix products, arithmetic and copies ran while one was open for 0% of the time, Pallas kernels for 19%

profile of v5, /device:TPU:0, one launch (start us, length us, event | category | flops | bytes accessed | tf_op | source)
XLA Modules:
  0.0 47.0 jit_solution(12841340500944203459)
XLA Ops:
  0.6 1.2 %shard_map.95 = (bf16[256,256]{1,0:T(8,128)(2,1)S(1)}, bf16[256,256]{1,0:T(8,128)(2,1)S(1)}, bf16[256,256]{1,0:T(8,128)(2,1)S(1)}, bf16[256,256]{1,0:T(8,128)(2,1)S(1)}, bf16[256,256]{1,0:T(8,128)(2,1)S(1)}) custom-call(s32[1,2,4]{2,1,0:T(2,128)} %bitcast.5, s32[1,2,4]{2,1,0:T(2,128)} %bitcast.2, f32[512,256]{1,0:T(8,128)} %features_ref.1), custom_call_target="tpu_custom_call" | custom-call | bytes 1572864 | tf_op jit(solution)/shard_map/pallas_call | solution.py:364
  1.8 5.1 %collective-permute-start = (bf16[256,256]{1,0:T(8,128)(2,1)S(1)}, bf16[256,256]{1,0:T(8,128)(2,1)S(1)}, u32[]{:S(2)}, u32[]{:S(2)}) collective-permute-start(bf16[256,256]{1,0:T(8,128)(2,1)S(1)} %get-tuple-element.33), channel_id=1, source_target_pairs={{0,12},{4,8},{8,4},{12,0},{1,13},{5,9},{9,5},{13,1},{2,14},{6,10},... | collective-permute-start | bytes 393224 | tf_op jit(solution)/shard_map/ppermute | solution.py:35
  7.0 0.6 %collective-permute-start.2 = (bf16[256,256]{1,0:T(8,128)(2,1)S(1)}, bf16[256,256]{1,0:T(8,128)(2,1)S(1)}, u32[]{:S(2)}, u32[]{:S(2)}) collective-permute-start(bf16[256,256]{1,0:T(8,128)(2,1)S(1)} %get-tuple-element.35), channel_id=1, source_target_pairs={{0,4},{4,0},{8,12},{12,8},{1,5},{5,1},{9,13},{13,9},{2,6},{6,2},{1... | collective-permute-start | bytes 393224 | tf_op jit(solution)/shard_map/ppermute | solution.py:35
  8.0 1.3 %collective-permute-start.4 = (bf16[256,256]{1,0:T(8,128)(2,1)S(1)}, bf16[256,256]{1,0:T(8,128)(2,1)S(1)}, u32[]{:S(2)}, u32[]{:S(2)}) collective-permute-start(bf16[256,256]{1,0:T(8,128)(2,1)S(1)} %get-tuple-element.37), channel_id=1, source_target_pairs={{0,2},{1,3},{2,0},{3,1},{4,6},{5,7},{6,4},{7,5},{8,10},{9,11},{10,... | collective-permute-start | bytes 393224 | tf_op jit(solution)/shard_map/ppermute | solution.py:35
  9.3 4.4 %shard_map.94 = (bf16[256,256]{1,0:T(8,128)(2,1)S(1)}, f32[512,256]{1,0:T(8,128)S(1)}, f32[512,256]{1,0:T(8,128)S(1)}, f32[512,256]{1,0:T(8,128)S(1)}, bf16[12,1...) custom-call(s32[4,16]{1,0:T(4,128)} %list_any.1, ...), custom_call_target="tpu_custom_call" | custom-call | flops 3221225472 | bytes 6291456 | tf_op jit(solution)/shard_map/pallas_call | solution.py:372
  14.1 4.0 %collective-permute-done.1.refs_1_ = bf16[256,256]{1,0:T(8,128)(2,1)S(1)} collective-permute-done((bf16[256,256]{1,0:T(8,128)(2,1)S(1)}, bf16[256,256]{1,0:T(8,128)(2,1)S(1)}, u32[]{:S(2)}, u32[]{:S(2)}) %collective-permute-start.1) | collective-permute-done | bytes 131104 | tf_op jit(solution)/shard_map/ppermute | solution.py:35
  18.1 1.5 %shard_map.96 = (f32[512,256]{1,0:T(8,128)S(1)}, f32[512,256]{1,0:T(8,128)S(1)}, bf16[512,256]{1,0:T(8,128)(2,1)S(1)}, f32[512,256]{1,0:T(8,128)S(1)}, bf16[256,...) custom-call(s32[12]{0:T(128)S(1)} %get-tuple-element.32.place_any, ...), custom_call_target="tpu_custom_call" | custom-call | flops 201326592 | bytes 4194304 | tf_op jit(solution)/shard_map/pallas_call | solution.py:391
  19.6 1.2 %shard_map.98 = (f32[128,256]{1,0:T(8,128)S(1)}, bf16[256,256]{1,0:T(8,128)(2,1)S(1)}, bf16[256,256]{1,0:T(8,128)(2,1)S(1)}, bf16[512,256]{1,0:T(8,128)(2,1)S(1)}) custom-call(s32[12]{0:T(128)S(1)} %get-tuple-element.32.place_any, f32[512,256]{1,0:T(8,128)S(1)} %copy-done, f32[512,256]{1,0:T(8,128)S(1)} %get-tuple-element.51.local_ref, ...), custom_call_target="tpu_custom_call" | custom-call | flops 335544320 | bytes 2621440 | tf_op jit(solution)/shard_map/pallas_call | solution.py:402
  20.8 1.6 %collective-permute-start.9 = (bf16[256,256]{1,0:T(8,128)(2,1)S(1)}, bf16[256,256]{1,0:T(8,128)(2,1)S(1)}, u32[]{:S(2)}, u32[]{:S(2)}) collective-permute-start(bf16[256,256]{1,0:T(8,128)(2,1)S(1)} %get-tuple-element.53), channel_id=1, source_target_pairs={{0,3},{1,2},{2,1},{3,0},{4,7},{5,6},{6,5},{7,4},{8,11},{9,10},{10,... | collective-permute-start | bytes 393224 | tf_op jit(solution)/shard_map/ppermute | solution.py:39
  22.4 0.5 %collective-permute-start.10 = (bf16[256,256]{1,0:T(8,128)(2,1)S(1)}, bf16[256,256]{1,0:T(8,128)(2,1)S(1)}, u32[]{:S(2)}, u32[]{:S(2)}) collective-permute-start(bf16[256,256]{1,0:T(8,128)(2,1)S(1)} %get-tuple-element.54), channel_id=1, source_target_pairs={{0,2},{1,3},{2,0},{3,1},{4,6},{5,7},{6,4},{7,5},{8,10},{9,11},{10,... | collective-permute-start | bytes 393224 | tf_op jit(solution)/shard_map/ppermute | solution.py:39
  23.0 2.5 %collective-permute-start.6 = (bf16[256,256]{1,0:T(8,128)(2,1)S(1)}, bf16[256,256]{1,0:T(8,128)(2,1)S(1)}, u32[]{:S(2)}, u32[]{:S(2)}) collective-permute-start(bf16[256,256]{1,0:T(8,128)(2,1)S(1)} %get-tuple-element.48), channel_id=1, source_target_pairs={{0,12},{4,8},{8,4},{12,0},{1,13},{5,9},{9,5},{13,1},{2,14},{6,10},... | collective-permute-start | bytes 393224 | tf_op jit(solution)/shard_map/ppermute | solution.py:39
  25.5 1.9 %collective-permute-start.8 = (bf16[256,256]{1,0:T(8,128)(2,1)S(1)}, bf16[256,256]{1,0:T(8,128)(2,1)S(1)}, u32[]{:S(2)}, u32[]{:S(2)}) collective-permute-start(bf16[256,256]{1,0:T(8,128)(2,1)S(1)} %get-tuple-element.50), channel_id=1, source_target_pairs={{0,4},{4,0},{8,12},{12,8},{1,5},{5,1},{9,13},{13,9},{2,6},{6,2},{1... | collective-permute-start | bytes 393224 | tf_op jit(solution)/shard_map/ppermute | solution.py:39
  27.4 1.6 %collective-permute-start.12 = (f32[64,256]{1,0:T(8,128)S(1)}, f32[64,256]{1,0:T(8,128)S(1)}, u32[]{:S(2)}, u32[]{:S(2)}) collective-permute-start(f32[64,256]{1,0:T(8,128)S(1)} %get-tuple-element.58), channel_id=1, source_target_pairs={{0,2},{1,3},{2,0},{3,1},{4,6},{5,7},{6,4},{7,5},{8,10},{9,11},{10,... | collective-permute-start | bytes 196616 | tf_op jit(solution)/shard_map/ppermute | solution.py:35
  29.0 2.4 %shard_map.97 = (f32[512,256]{1,0:T(8,128)}, f32[512,256]{1,0:T(8,128)S(1)}) custom-call(s32[4,16]{1,0:T(4,128)S(1)} %copy-done.5, bf16[4,16,128,128]{3,2,1,0:T(8,128)(2,1)S(1)} %get-tuple-element.31.values_ref, f32[512,256]{1,0:T(8,128)S(1)} %get-tuple-element.43.mixed_ref, f32[512,256]{1,0:T(8,128)S(1)} %get-tuple-element.44.scaled_ref, ...), custom_call_target="tpu_custom_call" | custom-call | flops 536870912 | bytes 4194304 | tf_op jit(solution)/shard_map/pallas_call | solution.py:413
  31.9 2.9 %collective-permute-start.14 = (bf16[64,256]{1,0:T(8,128)(2,1)S(1)}, bf16[64,256]{1,0:T(8,128)(2,1)S(1)}, u32[]{:S(2)}, u32[]{:S(2)}) collective-permute-start(bf16[64,256]{1,0:T(8,128)(2,1)S(1)} %shard_map.101.own_ref), channel_id=1, source_target_pairs={{0,8},{4,12},{8,0},{12,4},{1,9},{5,13},{9,1},{13,5},{2,10},{6,14},... | collective-permute-start | bytes 98312 | tf_op jit(solution)/shard_map/ppermute | solution.py:35
  34.9 1.3 %collective-permute-start.13 = (bf16[64,256]{1,0:T(8,128)(2,1)S(1)}, bf16[64,256]{1,0:T(8,128)(2,1)S(1)}, u32[]{:S(2)}, u32[]{:S(2)}) collective-permute-start(bf16[64,256]{1,0:T(8,128)(2,1)S(1)} %shard_map.101.own_ref), channel_id=1, source_target_pairs={{0,12},{4,8},{8,4},{12,0},{1,13},{5,9},{9,5},{13,1},{2,14},{6,10},... | collective-permute-start | bytes 98312 | tf_op jit(solution)/shard_map/ppermute | solution.py:35
  36.2 0.7 %collective-permute-done.7.refs_1_.refs_3_ = bf16[256,256]{1,0:T(8,128)(2,1)S(1)} collective-permute-done((bf16[256,256]{1,0:T(8,128)(2,1)S(1)}, bf16[256,256]{1,0:T(8,128)(2,1)S(1)}, u32[]{:S(2)}, u32[]{:S(2)}) %collective-permute-start.7) | collective-permute-done | bytes 131104 | tf_op jit(solution)/shard_map/ppermute | solution.py:39
  36.9 0.6 %collective-permute-done.14.refs_1_ = bf16[64,256]{1,0:T(8,128)(2,1)S(1)} collective-permute-done((bf16[64,256]{1,0:T(8,128)(2,1)S(1)}, bf16[64,256]{1,0:T(8,128)(2,1)S(1)}, u32[]{:S(2)}, u32[]{:S(2)}) %collective-permute-start.14) | collective-permute-done | bytes 32800 | tf_op jit(solution)/shard_map/ppermute | solution.py:35
  37.6 3.0 %collective-permute-done.13.refs_0_ = bf16[64,256]{1,0:T(8,128)(2,1)S(1)} collective-permute-done((bf16[64,256]{1,0:T(8,128)(2,1)S(1)}, bf16[64,256]{1,0:T(8,128)(2,1)S(1)}, u32[]{:S(2)}, u32[]{:S(2)}) %collective-permute-start.13) | collective-permute-done | bytes 32800 | tf_op jit(solution)/shard_map/ppermute | solution.py:35
  40.7 1.5 %collective-permute-start.17 = (f32[64,256]{1,0:T(8,128)S(1)}, f32[64,256]{1,0:T(8,128)S(1)}, u32[]{:S(2)}, u32[]{:S(2)}) collective-permute-start(f32[64,256]{1,0:T(8,128)S(1)} %shard_map.102.refs_0_), channel_id=1, source_target_pairs={{0,2},{1,3},{2,0},{3,1},{4,6},{5,7},{6,4},{7,5},{8,10},{9,11},{10,... | collective-permute-start | bytes 196616 | tf_op jit(solution)/shard_map/ppermute | solution.py:35
  42.5 2.1 %shard_map.99.refs_4_ = f32[512,256]{1,0:T(8,128)} custom-call(s32[1,2,4]{2,1,0:T(2,128)S(1)} %bitcast.6, s32[1,2,4]{2,1,0:T(2,128)S(1)} %bitcast.4, f32[512,256]{1,0:T(8,128)S(1)} %get-tuple-element.47.part_ref.refs_3_, f32[256,256]{1,0:T(8,128)S(1)} %copy-done.1, bf16[256,256]{1,0:T(8,128)(2,1)S(1)} %collective-permute-done.6.refs_0_.refs_4_, ...), custom_call_target="tpu_custom_call" | custom-call | flops 201326592 | bytes 2097152 | tf_op jit(solution)/shard_map/pallas_call | solution.py:427
  44.6 0.5 %collective-permute-done.17.refs_2_ = f32[64,256]{1,0:T(8,128)S(1)} collective-permute-done((f32[64,256]{1,0:T(8,128)S(1)}, f32[64,256]{1,0:T(8,128)S(1)}, u32[]{:S(2)}, u32[]{:S(2)}) %collective-permute-start.17) | collective-permute-done | bytes 65568 | tf_op jit(solution)/shard_map/ppermute | solution.py:35
  45.2 1.1 %collective-permute-done.16.refs_1_ = f32[64,256]{1,0:T(8,128)S(1)} collective-permute-done((f32[64,256]{1,0:T(8,128)S(1)}, f32[64,256]{1,0:T(8,128)S(1)}, u32[]{:S(2)}, u32[]{:S(2)}) %collective-permute-start.16) | collective-permute-done | bytes 65568 | tf_op jit(solution)/shard_map/ppermute | solution.py:35
  46.3 0.7 %shard_map.103 = f32[256,256]{1,0:T(8,128)} custom-call(f32[64,256]{1,0:T(8,128)S(1)} %shard_map.102.refs_0_, f32[64,256]{1,0:T(8,128)S(1)} %collective-permute-done.16.refs_1_, f32[64,256]{1,0:T(8,128)S(1)} %collective-permute-done.17.refs_2_, f32[64,256]{1,0:T(8,128)S(1)} %collective-permute-done.18.refs_3_, f32[512,256]{1,0:T(8,128)} %shard_map.99.refs_4_), custom_call_target="tpu_custom_call" | custom-call | bytes 131072 | tf_op jit(solution)/shard_map/pallas_call | solution.py:440
  (36 shorter events, 1.8 us)
Async XLA Ops:
  1.8 11.9 %collective-permute-start = (bf16[256,256]{1,0:T(8,128)(2,1)S(1)}, bf16[256,256]{1,0:T(8,128)(2,1)S(1)}, u32[]{:S(2)}, u32[]{:S(2)}) collective-permute-start(bf16[256,256]{1,0:T(8,128)(2,1)S(1)} %get-tuple-element.33), channel_id=1, source_target_pairs={{0,12},{4,8},{8,4},{12,0},{1,13},{5,9},{9,5},{13,1},{2,14},{6,10},... | collective-permute-start | bytes 393224 | tf_op jit(solution)/shard_map/ppermute | solution.py:35
  7.0 11.1 %collective-permute-start.1 = (bf16[256,256]{1,0:T(8,128)(2,1)S(1)}, bf16[256,256]{1,0:T(8,128)(2,1)S(1)}, u32[]{:S(2)}, u32[]{:S(2)}) collective-permute-start(bf16[256,256]{1,0:T(8,128)(2,1)S(1)} %get-tuple-element.34), channel_id=1, source_target_pairs={{0,8},{4,12},{8,0},{12,4},{1,9},{5,13},{9,1},{13,5},{2,10},{6,14},... | collective-permute-start | bytes 393224 | tf_op jit(solution)/shard_map/ppermute | solution.py:35
  7.0 11.1 %collective-permute-start.2 = (bf16[256,256]{1,0:T(8,128)(2,1)S(1)}, bf16[256,256]{1,0:T(8,128)(2,1)S(1)}, u32[]{:S(2)}, u32[]{:S(2)}) collective-permute-start(bf16[256,256]{1,0:T(8,128)(2,1)S(1)} %get-tuple-element.35), channel_id=1, source_target_pairs={{0,4},{4,0},{8,12},{12,8},{1,5},{5,1},{9,13},{13,9},{2,6},{6,2},{1... | collective-permute-start | bytes 393224 | tf_op jit(solution)/shard_map/ppermute | solution.py:35
  7.6 10.4 %collective-permute-start.3 = (bf16[256,256]{1,0:T(8,128)(2,1)S(1)}, bf16[256,256]{1,0:T(8,128)(2,1)S(1)}, u32[]{:S(2)}, u32[]{:S(2)}) collective-permute-start(bf16[256,256]{1,0:T(8,128)(2,1)S(1)} %get-tuple-element.36), channel_id=1, source_target_pairs={{0,3},{1,2},{2,1},{3,0},{4,7},{5,6},{6,5},{7,4},{8,11},{9,10},{10,... | collective-permute-start | bytes 393224 | tf_op jit(solution)/shard_map/ppermute | solution.py:35
  8.0 10.1 %copy-start.1 = (f32[256,256]{1,0:T(8,128)S(1)}, f32[256,256]{1,0:T(8,128)}, u32[]{:S(2)}) copy-start(f32[256,256]{1,0:T(8,128)} %weight_ref.1) | copy-start | bytes 786436
  8.0 10.1 %copy-start.2 = (f32[512,256]{1,0:T(8,128)S(1)}, f32[512,256]{1,0:T(8,128)}, u32[]{:S(2)}) copy-start(f32[512,256]{1,0:T(8,128)} %refs_11_.1) | copy-start | bytes 1572868
  8.0 10.1 %collective-permute-start.4 = (bf16[256,256]{1,0:T(8,128)(2,1)S(1)}, bf16[256,256]{1,0:T(8,128)(2,1)S(1)}, u32[]{:S(2)}, u32[]{:S(2)}) collective-permute-start(bf16[256,256]{1,0:T(8,128)(2,1)S(1)} %get-tuple-element.37), channel_id=1, source_target_pairs={{0,2},{1,3},{2,0},{3,1},{4,6},{5,7},{6,4},{7,5},{8,10},{9,11},{10,... | collective-permute-start | bytes 393224 | tf_op jit(solution)/shard_map/ppermute | solution.py:35
  13.7 4.3 %collective-permute-start.5 = (bf16[256,256]{1,0:T(8,128)(2,1)S(1)}, bf16[256,256]{1,0:T(8,128)(2,1)S(1)}, u32[]{:S(2)}, u32[]{:S(2)}) collective-permute-start(bf16[256,256]{1,0:T(8,128)(2,1)S(1)} %get-tuple-element.38), channel_id=1, source_target_pairs={{0,1},{1,0},{2,3},{3,2},{4,5},{5,4},{6,7},{7,6},{8,9},{9,8},{10,11... | collective-permute-start | bytes 393224 | tf_op jit(solution)/shard_map/ppermute | solution.py:35
  19.6 9.4 %copy-start.5 = (s32[4,16]{1,0:T(4,128)S(1)}, s32[4,16]{1,0:T(4,128)}, u32[]{:S(2)}) copy-start(s32[4,16]{1,0:T(4,128)} %list_any.1) | copy-start | bytes 772
  20.7 4.7 %collective-permute-start.11 = (bf16[512,256]{1,0:T(8,128)(2,1)S(1)}, bf16[512,256]{1,0:T(8,128)(2,1)S(1)}, u32[]{:S(2)}, u32[]{:S(2)}) collective-permute-start(bf16[512,256]{1,0:T(8,128)(2,1)S(1)} %get-tuple-element.55), channel_id=1, source_target_pairs={{0,1},{1,0},{2,3},{3,2},{4,5},{5,4},{6,7},{7,6},{8,9},{9,8},{10,11... | collective-permute-start | bytes 786440 | tf_op jit(solution)/shard_map/ppermute | solution.py:39
  20.8 6.6 %collective-permute-start.9 = (bf16[256,256]{1,0:T(8,128)(2,1)S(1)}, bf16[256,256]{1,0:T(8,128)(2,1)S(1)}, u32[]{:S(2)}, u32[]{:S(2)}) collective-permute-start(bf16[256,256]{1,0:T(8,128)(2,1)S(1)} %get-tuple-element.53), channel_id=1, source_target_pairs={{0,3},{1,2},{2,1},{3,0},{4,7},{5,6},{6,5},{7,4},{8,11},{9,10},{10,... | collective-permute-start | bytes 393224 | tf_op jit(solution)/shard_map/ppermute | solution.py:39
  22.4 9.0 %collective-permute-start.10 = (bf16[256,256]{1,0:T(8,128)(2,1)S(1)}, bf16[256,256]{1,0:T(8,128)(2,1)S(1)}, u32[]{:S(2)}, u32[]{:S(2)}) collective-permute-start(bf16[256,256]{1,0:T(8,128)(2,1)S(1)} %get-tuple-element.54), channel_id=1, source_target_pairs={{0,2},{1,3},{2,0},{3,1},{4,6},{5,7},{6,4},{7,5},{8,10},{9,11},{10,... | collective-permute-start | bytes 393224 | tf_op jit(solution)/shard_map/ppermute | solution.py:39
  23.0 11.9 %collective-permute-start.6 = (bf16[256,256]{1,0:T(8,128)(2,1)S(1)}, bf16[256,256]{1,0:T(8,128)(2,1)S(1)}, u32[]{:S(2)}, u32[]{:S(2)}) collective-permute-start(bf16[256,256]{1,0:T(8,128)(2,1)S(1)} %get-tuple-element.48), channel_id=1, source_target_pairs={{0,12},{4,8},{8,4},{12,0},{1,13},{5,9},{9,5},{13,1},{2,14},{6,10},... | collective-permute-start | bytes 393224 | tf_op jit(solution)/shard_map/ppermute | solution.py:39
  25.4 11.5 %collective-permute-start.7 = (bf16[256,256]{1,0:T(8,128)(2,1)S(1)}, bf16[256,256]{1,0:T(8,128)(2,1)S(1)}, u32[]{:S(2)}, u32[]{:S(2)}) collective-permute-start(bf16[256,256]{1,0:T(8,128)(2,1)S(1)} %get-tuple-element.49), channel_id=1, source_target_pairs={{0,8},{4,12},{8,0},{12,4},{1,9},{5,13},{9,1},{13,5},{2,10},{6,14},... | collective-permute-start | bytes 393224 | tf_op jit(solution)/shard_map/ppermute | solution.py:39
  25.5 11.5 %collective-permute-start.8 = (bf16[256,256]{1,0:T(8,128)(2,1)S(1)}, bf16[256,256]{1,0:T(8,128)(2,1)S(1)}, u32[]{:S(2)}, u32[]{:S(2)}) collective-permute-start(bf16[256,256]{1,0:T(8,128)(2,1)S(1)} %get-tuple-element.50), channel_id=1, source_target_pairs={{0,4},{4,0},{8,12},{12,8},{1,5},{5,1},{9,13},{13,9},{2,6},{6,2},{1... | collective-permute-start | bytes 393224 | tf_op jit(solution)/shard_map/ppermute | solution.py:39
  27.4 4.3 %collective-permute-start.12 = (f32[64,256]{1,0:T(8,128)S(1)}, f32[64,256]{1,0:T(8,128)S(1)}, u32[]{:S(2)}, u32[]{:S(2)}) collective-permute-start(f32[64,256]{1,0:T(8,128)S(1)} %get-tuple-element.58), channel_id=1, source_target_pairs={{0,2},{1,3},{2,0},{3,1},{4,6},{5,7},{6,4},{7,5},{8,10},{9,11},{10,... | collective-permute-start | bytes 196616 | tf_op jit(solution)/shard_map/ppermute | solution.py:35
  29.0 13.6 %copy-start.3 = (s32[1,4,2]{1,2,0:T(2,128)S(1)}, s32[1,4,2]{1,2,0:T(2,128)}, u32[]{:S(2)}) copy-start(s32[1,4,2]{1,2,0:T(2,128)} %param.13) | copy-start | bytes 100
  29.0 13.6 %copy-start.4 = (s32[1,4,2]{1,2,0:T(2,128)S(1)}, s32[1,4,2]{1,2,0:T(2,128)}, u32[]{:S(2)}) copy-start(s32[1,4,2]{1,2,0:T(2,128)} %param.12) | copy-start | bytes 100
  31.8 5.2 %collective-permute-start.15 = (bf16[64,256]{1,0:T(8,128)(2,1)S(1)}, bf16[64,256]{1,0:T(8,128)(2,1)S(1)}, u32[]{:S(2)}, u32[]{:S(2)}) collective-permute-start(bf16[64,256]{1,0:T(8,128)(2,1)S(1)} %shard_map.101.own_ref), channel_id=1, source_target_pairs={{0,4},{4,0},{8,12},{12,8},{1,5},{5,1},{9,13},{13,9},{2,6},{6,2},{1... | collective-permute-start | bytes 98312 | tf_op jit(solution)/shard_map/ppermute | solution.py:35
  31.9 5.6 %collective-permute-start.14 = (bf16[64,256]{1,0:T(8,128)(2,1)S(1)}, bf16[64,256]{1,0:T(8,128)(2,1)S(1)}, u32[]{:S(2)}, u32[]{:S(2)}) collective-permute-start(bf16[64,256]{1,0:T(8,128)(2,1)S(1)} %shard_map.101.own_ref), channel_id=1, source_target_pairs={{0,8},{4,12},{8,0},{12,4},{1,9},{5,13},{9,1},{13,5},{2,10},{6,14},... | collective-permute-start | bytes 98312 | tf_op jit(solution)/shard_map/ppermute | solution.py:35
  34.9 5.7 %collective-permute-start.13 = (bf16[64,256]{1,0:T(8,128)(2,1)S(1)}, bf16[64,256]{1,0:T(8,128)(2,1)S(1)}, u32[]{:S(2)}, u32[]{:S(2)}) collective-permute-start(bf16[64,256]{1,0:T(8,128)(2,1)S(1)} %shard_map.101.own_ref), channel_id=1, source_target_pairs={{0,12},{4,8},{8,4},{12,0},{1,13},{5,9},{9,5},{13,1},{2,14},{6,10},... | collective-permute-start | bytes 98312 | tf_op jit(solution)/shard_map/ppermute | solution.py:35
  40.6 4.0 %collective-permute-start.18 = (f32[64,256]{1,0:T(8,128)S(1)}, f32[64,256]{1,0:T(8,128)S(1)}, u32[]{:S(2)}, u32[]{:S(2)}) collective-permute-start(f32[64,256]{1,0:T(8,128)S(1)} %shard_map.102.refs_0_), channel_id=1, source_target_pairs={{0,1},{1,0},{2,3},{3,2},{4,5},{5,4},{6,7},{7,6},{8,9},{9,8},{10,11... | collective-permute-start | bytes 196616 | tf_op jit(solution)/shard_map/ppermute | solution.py:35
  40.7 4.5 %collective-permute-start.17 = (f32[64,256]{1,0:T(8,128)S(1)}, f32[64,256]{1,0:T(8,128)S(1)}, u32[]{:S(2)}, u32[]{:S(2)}) collective-permute-start(f32[64,256]{1,0:T(8,128)S(1)} %shard_map.102.refs_0_), channel_id=1, source_target_pairs={{0,2},{1,3},{2,0},{3,1},{4,6},{5,7},{6,4},{7,5},{8,10},{9,11},{10,... | collective-permute-start | bytes 196616 | tf_op jit(solution)/shard_map/ppermute | solution.py:35
  42.2 4.0 %collective-permute-start.16 = (f32[64,256]{1,0:T(8,128)S(1)}, f32[64,256]{1,0:T(8,128)S(1)}, u32[]{:S(2)}, u32[]{:S(2)}) collective-permute-start(f32[64,256]{1,0:T(8,128)S(1)} %shard_map.102.refs_0_), channel_id=1, source_target_pairs={{0,3},{1,2},{2,1},{3,0},{4,7},{5,6},{6,5},{7,4},{8,11},{9,10},{10,... | collective-permute-start | bytes 196616 | tf_op jit(solution)/shard_map/ppermute | solution.py:35
  (1 other events, 5.9 us)
